TPU v7x, 32 devices: a whole 2x2x4 slice. The times are simulated.
32 devices in a mesh: fsdp: 8 (over z, x), tp: 4 (over y, core).
Axes of the slice: x: 2, y: 2, z: 4, core: 2. Of those that a mesh axis runs over, the one named last changes fastest.
Arguments:
- tokens: bfloat16 [16384, 768], P(('fsdp', 'tp')), may hold values from -6 to 6
- seq_lengths: int32 [8, 8], P('fsdp'), may hold values from 1 to 1024, 2048 in all within a row
- w_qkv: bfloat16 [3, 768, 768], P(None, 'fsdp', 'tp'), may hold values from -0.21875 to 0.21875
- w_out: bfloat16 [768, 768], P('tp', 'fsdp'), may hold values from -1.25 to 1.25
- w_in: bfloat16 [2, 768, 1152], P(None, 'fsdp', 'tp'), may hold values from -0.21875 to 0.21875
- w_down: bfloat16 [1152, 768], P('tp', 'fsdp'), may hold values from -0.1875 to 0.1875
- gains: bfloat16 [2, 768], P(None, 'fsdp'), may hold values from 0.5 to 1.5
- cotangent: bfloat16 [16384, 768], P(('fsdp', 'tp')), may hold values from -6 to 6
Outputs:
- output: bfloat16 [16384, 768], P(('fsdp', 'tp'))
- grad_tokens: bfloat16 [16384, 768], P(('fsdp', 'tp'))
- grad_qkv: float32 [3, 768, 768], P(None, 'fsdp', 'tp')
- grad_out: float32 [768, 768], P('tp', 'fsdp')
- grad_in: float32 [2, 768, 1152], P(None, 'fsdp', 'tp')
- grad_down: float32 [1152, 768], P('tp', 'fsdp')
- grad_gains: float32 [2, 768], P(None, 'fsdp')
Inputs may be any that keep to these rules, and one draw needn't show every extreme that they name: `seq_lengths`: each row of a group holds 8 lengths that add up to 2048; the longest of each group is exactly 1024.
All inputs are finite; a program needn't handle non-finite values.
Results may differ from a plain program's by a relative error of at most 0.018.
Values may be sent and summed in bfloat16 or wider, within the bound.
No kernel may reach another device: no remote copies, remote signals or barrier semaphores. Data moves between devices by JAX's collectives and lax.ppermute only.
A program may use at most 128 MiB of HBM per device.

v0:
```python
import jax
import jax.numpy as jnp
from jax import lax
from jax.sharding import PartitionSpec as P

HEAD_DIM = 64


def norm_rows(values, gain):
    center = values - jnp.mean(values, axis=-1, keepdims=True)
    spread = jnp.mean(center * center, axis=-1, keepdims=True)
    return center * lax.rsqrt(spread + 1e-05) * gain


def positions(lengths, total):
    ends = jnp.cumsum(lengths)
    starts = ends - lengths
    index = jnp.arange(total, dtype=jnp.int32)
    segment = jnp.sum((index[:, None] >= ends[None, :]).astype(jnp.int32), axis=1)
    onehot = segment[:, None] == jnp.arange(lengths.shape[0], dtype=jnp.int32)[None, :]
    first = jnp.sum(jnp.where(onehot, starts[None, :], 0), axis=1)
    return (segment, index - first)


def rope_tables(place, size):
    half = size // 2
    freq = jnp.exp(
        -jnp.log(jnp.float32(160000.0)) * jnp.arange(half, dtype=jnp.float32) * (2.0 / size)
    )
    angle = place.astype(jnp.float32)[:, None] * freq[None, :]
    return (jnp.cos(angle), jnp.sin(angle))


def rotate(values, cosine, sine):
    half = values.shape[-1] // 2
    first = values[..., :half]
    second = values[..., half:]
    cos_b = cosine[:, None, :]
    sin_b = sine[:, None, :]
    return jnp.concatenate(
        [first * cos_b - second * sin_b, second * cos_b + first * sin_b], axis=-1
    )


def dot_nt(left, right):
    return lax.dot_general(
        left, right, (((1,), (1,)), ((), ())), preferred_element_type=jnp.float32
    )


def dot_tn(left, right):
    return lax.dot_general(
        left, right, (((0,), (0,)), ((), ())), preferred_element_type=jnp.float32
    )


def geglu(up_in, gate_in):
    return jax.nn.gelu(up_in, approximate=False) * gate_in


def shards(tokens, seq_lengths, w_qkv, w_out, w_in, w_down, gains, cotangent):
    w_proj, w_back, w_pair, w_last, gain_pair = (
        lax.all_gather(w_qkv, "fsdp", axis=1, tiled=True),
        lax.all_gather(w_out, "fsdp", axis=1, tiled=True),
        lax.all_gather(w_in, "fsdp", axis=1, tiled=True),
        lax.all_gather(w_down, "fsdp", axis=1, tiled=True),
        lax.all_gather(gains, "fsdp", axis=1, tiled=True),
    )
    rows = tokens.shape[0]
    model = tokens.shape[1]
    lanes = w_proj.shape[2]
    units = w_pair.shape[2]
    group = rows * lax.axis_size("tp")
    heads_here = lanes // HEAD_DIM
    block = min(512, group)
    count = group // block
    scale = HEAD_DIM ** (-0.5)
    proj_cat = jnp.transpose(w_proj, (1, 0, 2)).reshape(model, 3 * lanes)
    pair_cat = jnp.transpose(w_pair, (1, 0, 2)).reshape(model, 2 * units)
    gain_one = gain_pair[0].astype(jnp.float32)
    gain_two = gain_pair[1].astype(jnp.float32)
    inputs = tokens.astype(jnp.float32)
    normed1 = norm_rows(inputs, gain_one).astype(jnp.bfloat16)
    full1 = lax.all_gather(normed1, "tp", axis=0, tiled=True)
    mixed = jnp.dot(full1, proj_cat, preferred_element_type=jnp.float32)
    segment, place = positions(seq_lengths[0], group)
    cosine, sine = rope_tables(place, HEAD_DIM)
    q_raw = mixed[:, :lanes].reshape(group, heads_here, HEAD_DIM)
    k_raw = mixed[:, lanes : 2 * lanes].reshape(group, heads_here, HEAD_DIM)
    query = rotate(q_raw, cosine, sine).astype(jnp.bfloat16)
    keys = rotate(k_raw, cosine, sine).astype(jnp.bfloat16)
    values = mixed[:, 2 * lanes :].reshape(group, heads_here, HEAD_DIM).astype(jnp.bfloat16)
    q_blocks = query.reshape(count, block, heads_here, HEAD_DIM)
    seg_blocks = segment.reshape(count, block)

    def scores_of(q_block, seg_block):
        raw = jnp.einsum("qhd,khd->hqk", q_block, keys, preferred_element_type=jnp.float32)
        same = (seg_block[:, None] == segment[None, :])[None]
        return jnp.where(same, raw * scale, -1e30)

    def attend(pair):
        q_block, seg_block = pair
        scores = scores_of(q_block, seg_block)
        top = jnp.max(scores, axis=-1, keepdims=True)
        expo = jnp.exp(scores - top)
        total = jnp.sum(expo, axis=-1, keepdims=True)
        probs = (expo / total).astype(jnp.bfloat16)
        ctx = jnp.einsum("hqk,khd->qhd", probs, values, preferred_element_type=jnp.float32)
        return (ctx, (top + jnp.log(total))[..., 0])

    ctx_blocks, log_totals = lax.map(attend, (q_blocks, seg_blocks))
    context = ctx_blocks.reshape(group, lanes).astype(jnp.bfloat16)
    attn = lax.psum_scatter(
        jnp.dot(context, w_back, preferred_element_type=jnp.float32),
        "tp",
        scatter_dimension=0,
        tiled=True,
    )
    h_mid = inputs + attn
    normed2 = norm_rows(h_mid, gain_two).astype(jnp.bfloat16)
    full2 = lax.all_gather(normed2, "tp", axis=0, tiled=True)
    both = jnp.dot(full2, pair_cat, preferred_element_type=jnp.float32)
    up_in = both[:, :units]
    gate_in = both[:, units:]
    hidden = geglu(up_in, gate_in).astype(jnp.bfloat16)
    mlp = lax.psum_scatter(
        jnp.dot(hidden, w_last, preferred_element_type=jnp.float32).astype(jnp.bfloat16),
        "tp",
        scatter_dimension=0,
        tiled=True,
    ).astype(jnp.float32)
    output = (h_mid + mlp).astype(jnp.bfloat16)
    piece = lax.all_gather(cotangent, "tp", axis=0, tiled=True)
    d_hid = dot_nt(piece, w_last)
    d_last = dot_tn(hidden, piece)
    _, geglu_pull = jax.vjp(geglu, up_in, gate_in)
    d_up, d_gate = geglu_pull(d_hid)
    d_both = jnp.concatenate([d_up, d_gate], axis=1).astype(jnp.bfloat16)
    d_normed2 = lax.psum_scatter(dot_nt(d_both, pair_cat), "tp", scatter_dimension=0, tiled=True)
    grad_pair_cat = dot_tn(full2, d_both)
    _, norm_two_pull = jax.vjp(norm_rows, h_mid, gain_two)
    d_mid_part, d_gain_two = norm_two_pull(d_normed2)
    d_mid = cotangent.astype(jnp.float32) + d_mid_part
    d_attn = d_mid.astype(jnp.bfloat16)
    piece = lax.all_gather(d_attn, "tp", axis=0, tiled=True)
    d_ctx = dot_nt(piece, w_back)
    d_back = dot_tn(context, piece)
    d_ctx_blocks = d_ctx.astype(jnp.bfloat16).reshape(count, block, heads_here, HEAD_DIM)

    def back_step(carry, items):
        d_keys, d_values = carry
        q_block, seg_block, log_block, d_block = items
        scores = scores_of(q_block, seg_block)
        probs = jnp.exp(scores - log_block[..., None])
        d_values = d_values + jnp.einsum(
            "hqk,qhd->khd", probs.astype(jnp.bfloat16), d_block, preferred_element_type=jnp.float32
        )
        d_probs = jnp.einsum("qhd,khd->hqk", d_block, values, preferred_element_type=jnp.float32)
        delta = jnp.sum(probs * d_probs, axis=-1, keepdims=True)
        d_scores = (probs * (d_probs - delta) * scale).astype(jnp.bfloat16)
        d_query = jnp.einsum("hqk,khd->qhd", d_scores, keys, preferred_element_type=jnp.float32)
        d_keys = d_keys + jnp.einsum(
            "hqk,qhd->khd", d_scores, q_block, preferred_element_type=jnp.float32
        )
        return ((d_keys, d_values), d_query)

    start_kv = (
        jnp.zeros((group, heads_here, HEAD_DIM), jnp.float32),
        jnp.zeros((group, heads_here, HEAD_DIM), jnp.float32),
    )
    (d_keys, d_values), d_q_blocks = lax.scan(
        back_step, start_kv, (q_blocks, seg_blocks, log_totals, d_ctx_blocks)
    )
    _, rope_pull = jax.vjp(lambda vec: rotate(vec, cosine, sine), q_raw)
    d_q_raw = rope_pull(d_q_blocks.reshape(group, heads_here, HEAD_DIM))[0]
    d_k_raw = rope_pull(d_keys)[0]
    d_mixed = jnp.concatenate(
        [
            d_q_raw.reshape(group, lanes),
            d_k_raw.reshape(group, lanes),
            d_values.reshape(group, lanes),
        ],
        axis=1,
    ).astype(jnp.bfloat16)
    d_normed1 = lax.psum_scatter(
        dot_nt(d_mixed, proj_cat).astype(jnp.bfloat16), "tp", scatter_dimension=0, tiled=True
    ).astype(jnp.float32)
    grad_proj_cat = dot_tn(full1, d_mixed)
    _, norm_one_pull = jax.vjp(norm_rows, inputs, gain_one)
    d_input_part, d_gain_one = norm_one_pull(d_normed1)
    grad_tokens = (d_mid + d_input_part).astype(jnp.bfloat16)
    gain_terms = lax.psum(jnp.stack([d_gain_one, d_gain_two]), "tp")
    grad_proj = jnp.transpose(grad_proj_cat.reshape(model, 3, lanes), (1, 0, 2))
    grad_pair = jnp.transpose(grad_pair_cat.reshape(model, 2, units), (1, 0, 2))
    grad_qkv, grad_out, grad_in, grad_down, grad_gains = (
        lax.psum_scatter(grad_proj, "fsdp", scatter_dimension=1, tiled=True),
        lax.psum_scatter(d_back, "fsdp", scatter_dimension=1, tiled=True),
        lax.psum_scatter(grad_pair, "fsdp", scatter_dimension=1, tiled=True),
        lax.psum_scatter(d_last, "fsdp", scatter_dimension=1, tiled=True),
        lax.psum_scatter(gain_terms, "fsdp", scatter_dimension=1, tiled=True),
    )
    return (output, grad_tokens, grad_qkv, grad_out, grad_in, grad_down, grad_gains)


def solution(mesh):
    placed = (
        P(("fsdp", "tp"), None),
        P("fsdp", None),
        P(None, "fsdp", "tp"),
        P("tp", "fsdp"),
        P(None, "fsdp", "tp"),
        P("tp", "fsdp"),
        P(None, "fsdp"),
        P(("fsdp", "tp"), None),
    )
    return jax.shard_map(
        shards,
        mesh=mesh,
        in_specs=placed,
        out_specs=(
            P(("fsdp", "tp"), None),
            P(("fsdp", "tp"), None),
            P(None, "fsdp", "tp"),
            P("tp", "fsdp"),
            P(None, "fsdp", "tp"),
            P("tp", "fsdp"),
            P(None, "fsdp"),
        ),
        check_vma=False,
    )
```

profile of v0, /device:TPU:0, one launch (start us, length us, event | category | flops | bytes accessed | tf_op | source)
XLA Modules:
  0.0 1189.1 jit_solution(271472552211506861)
XLA Ops:
  10.1 22.3 %all-gather = bf16[8,96,2]{1,2,0:T(2,128)(2,1)S(1)} all-gather(bf16[1,96,2]{1,2,0:T(2,128)(2,1)} %bitcast.182), channel_id=1, replica_groups=mesh['fsdp'=8,'tp'=4] {'fsdp'}, dimensions={0}, use_global_device_ids=true | all-gather | bytes 3456 | tf_op jit(solution)/shard_map/all_gather | solution.py:67
  36.1 35.3 %all_gather.29 = bf16[3,768,192]{2,0,1:T(4,128)(2,1)S(1)} all-gather(bf16[3,96,192]{2,0,1:T(4,128)(2,1)S(1)} %copy.45), channel_id=1, replica_groups=mesh['fsdp'=8,'tp'=4] {'fsdp'}, dimensions={1}, use_global_device_ids=true | all-gather | bytes 995328 | tf_op jit(solution)/shard_map/all_gather | solution.py:63
  73.6 31.2 %all_gather.30 = bf16[192,768]{0,1:T(8,128)(2,1)S(1)} all-gather(bf16[192,96]{0,1:T(8,128)(2,1)S(1)} %copy.50), channel_id=1, replica_groups=mesh['fsdp'=8,'tp'=4] {'fsdp'}, dimensions={1}, use_global_device_ids=true | all-gather | bytes 331776 | tf_op jit(solution)/shard_map/all_gather | solution.py:64
  111.3 84.4 %while.27 = (s32[]{:T(128)}, bf16[4,512,3,64]{1,3,2,0:T(8,128)(2,1)}, f32[4,3,512]{2,1,0:T(4,128)}, s32[4,512]{1,0:T(4,128)S(1)}, s32[2048]{0:T(1024)S(1)}, /*in...) while((s32[]{:T(128)}, ...), condition=%wide.region_8.9_spmd, body=%wide.region_5.8_spmd.sunk | while | flops 844102144 | bytes 50466988 | solution.py:111
  111.9 6.0 fusion.167
  118.0 6.8 fusion.168
  124.8 6.7 fusion.169
  133.1 6.0 fusion.167
  139.1 6.8 fusion.168
  145.9 6.7 fusion.169
  154.2 6.0 fusion.167
  160.2 6.8 fusion.168
  167.0 6.7 fusion.169
  175.3 6.0 fusion.167
  181.3 6.8 fusion.168
  188.1 6.7 fusion.169
  203.2 58.2 %reduce-scatter.16.cloned.1.call-done = f32[512,768]{1,0:T(8,128)} async-done(((f32[2048,768]{1,0:T(8,128)}), f32[512,768]{1,0:T(8,128)}) %reduce-scatter.16.cloned.1.call-update) | async-done | bytes 1572880 | tf_op jit(solution)/shard_map/reduce_scatter | solution.py:113
  269.8 35.3 %all_gather.32 = bf16[2,768,288]{2,0,1:T(2,128)(2,1)} all-gather(bf16[2,96,288]{2,0,1:T(2,128)(2,1)S(1)} %copy.51), channel_id=1, replica_groups=mesh['fsdp'=8,'tp'=4] {'fsdp'}, dimensions={1}, use_global_device_ids=true | all-gather | bytes 995328 | tf_op jit(solution)/shard_map/all_gather | solution.py:65
  309.9 33.9 %all_gather.33 = bf16[288,768]{0,1:T(8,128)(2,1)} all-gather(bf16[288,96]{0,1:T(8,128)(2,1)} %copy.53), channel_id=1, replica_groups=mesh['fsdp'=8,'tp'=4] {'fsdp'}, dimensions={1}, use_global_device_ids=true | all-gather | bytes 497664 | tf_op jit(solution)/shard_map/all_gather | solution.py:66
  343.7 6.3 fusion.119
  350.0 9.2 add_convert_fusion
  372.2 53.7 %reduce-scatter.20.cloned.1.call-done = f32[512,768]{1,0:T(8,128)} async-done(((f32[2048,768]{1,0:T(8,128)}), f32[512,768]{1,0:T(8,128)}) %reduce-scatter.20.cloned.1.call-update) | async-done | bytes 1572880 | tf_op jit(solution)/shard_map/reduce_scatter | solution.py:139
  429.1 37.2 %reduce-scatter.18.cloned.1.call-done = bf16[512,768]{1,0:T(8,128)(2,1)} async-done(((bf16[2048,768]{1,0:T(8,128)(2,1)}), bf16[512,768]{1,0:T(8,128)(2,1)}) %reduce-scatter.18.cloned.1.call-update) | async-done | bytes 786448 | tf_op jit(solution)/shard_map/reduce_scatter | solution.py:126
  471.9 28.6 %all-gather.12.cloned.1.call-done = bf16[2048,768]{1,0:T(8,128)(2,1)} async-done(((bf16[512,768]{1,0:T(8,128)(2,1)}), bf16[2048,768]{1,0:T(8,128)(2,1)}) %all-gather.12.cloned.1.call-update) | async-done | bytes 3145744 | tf_op jit(solution)/shard_map/all_gather | solution.py:145
  505.2 287.7 %while.28 = (s32[]{:T(128)}, f32[2048,3,64]{0,2,1:T(8,128)}, f32[2048,3,64]{0,2,1:T(8,128)}, f32[4,512,3,64]{1,0,3,2:T(4,128)}, bf16[4,512,3,64]{1,3,2,0:T(8,128...) while((s32[]{:T(128)}, f32[2048,3,64]{0,2,1:T(8,128)}, ...), condition=%wide.region_18.19_spmd.clone, body=%wide.region_16.18_spmd.clone.sunk | while | flops 2097683456 | bytes 192862448 | solution.py:171
  527.3 7.2 fusion.180
  534.5 20.0 %fusion.184 = f32[1,512,3,64]{1,3,2,0:T(8,128)S(1)} fusion(bf16[2048,3,64]{0,2,1:T(8,128)(2,1)S(1)} %get-tuple-element.448, f32[3,512,2048]{2,1,0:T(8,128)} %fusion.180, f32[3,512,2048]{2,1,0:T(8,128)} %copy-done, f32[3,512]{1,0:T(4,128)S(1)} %dynamic-slice_bitcast_fusion.2, pred[512,2048]{1,0:T(8,128)(4,1)S(1)} %broadcast_compare_fusion.5), kind=kOutput, calls=%fused_computation.40.clone.1 | convolution fusion | flops 437259776 | bytes 27400192 | tf_op jit(solution)/shard_map/while/body/eval_jaxpr/hqk,khd->qhd/dot_general | solution.py:161
  554.5 22.0 %fusion.182 = f32[2048,3,64]{0,2,1:T(8,128)} fusion(f32[3,512,2048]{2,1,0:T(8,128)} %fusion.180, f32[3,512,2048]{2,1,0:T(8,128)} %copy-done, f32[3,512]{1,0:T(4,128)S(1)} %dynamic-slice_bitcast_fusion.2, pred[512,2048]{1,0:T(8,128)(4,1)S(1)} %broadcast_compare_fusion.5, f32[2048,3,64]{0,2,1:T(8,128)} %get-tuple-element.429, pred[]{:T(512)S(6)} %compare.7, ...), kind=kOutput, calls=%fused_computation.37.clone.1 | convolution fusion | flops 438046208 | bytes 55787524 | tf_op jit(solution)/shard_map/while/body/eval_jaxpr/hqk,qhd->khd/dot_general | solution.py:162
  576.9 8.6 dynamic_update_slice.19
  595.8 7.2 fusion.180
  603.1 20.0 %fusion.184 = f32[1,512,3,64]{1,3,2,0:T(8,128)S(1)} fusion(bf16[2048,3,64]{0,2,1:T(8,128)(2,1)S(1)} %get-tuple-element.448, f32[3,512,2048]{2,1,0:T(8,128)} %fusion.180, f32[3,512,2048]{2,1,0:T(8,128)} %copy-done, f32[3,512]{1,0:T(4,128)S(1)} %dynamic-slice_bitcast_fusion.2, pred[512,2048]{1,0:T(8,128)(4,1)S(1)} %broadcast_compare_fusion.5), kind=kOutput, calls=%fused_computation.40.clone.1 | convolution fusion | flops 437259776 | bytes 27400192 | tf_op jit(solution)/shard_map/while/body/eval_jaxpr/hqk,khd->qhd/dot_general | solution.py:161
  623.1 22.5 %fusion.182 = f32[2048,3,64]{0,2,1:T(8,128)} fusion(f32[3,512,2048]{2,1,0:T(8,128)} %fusion.180, f32[3,512,2048]{2,1,0:T(8,128)} %copy-done, f32[3,512]{1,0:T(4,128)S(1)} %dynamic-slice_bitcast_fusion.2, pred[512,2048]{1,0:T(8,128)(4,1)S(1)} %broadcast_compare_fusion.5, f32[2048,3,64]{0,2,1:T(8,128)} %get-tuple-element.429, pred[]{:T(512)S(6)} %compare.7, ...), kind=kOutput, calls=%fused_computation.37.clone.1 | convolution fusion | flops 438046208 | bytes 55787524 | tf_op jit(solution)/shard_map/while/body/eval_jaxpr/hqk,qhd->khd/dot_general | solution.py:162
  646.0 8.6 dynamic_update_slice.19
  664.9 7.2 fusion.180
  672.2 20.0 %fusion.184 = f32[1,512,3,64]{1,3,2,0:T(8,128)S(1)} fusion(bf16[2048,3,64]{0,2,1:T(8,128)(2,1)S(1)} %get-tuple-element.448, f32[3,512,2048]{2,1,0:T(8,128)} %fusion.180, f32[3,512,2048]{2,1,0:T(8,128)} %copy-done, f32[3,512]{1,0:T(4,128)S(1)} %dynamic-slice_bitcast_fusion.2, pred[512,2048]{1,0:T(8,128)(4,1)S(1)} %broadcast_compare_fusion.5), kind=kOutput, calls=%fused_computation.40.clone.1 | convolution fusion | flops 437259776 | bytes 27400192 | tf_op jit(solution)/shard_map/while/body/eval_jaxpr/hqk,khd->qhd/dot_general | solution.py:161
  692.2 22.5 %fusion.182 = f32[2048,3,64]{0,2,1:T(8,128)} fusion(f32[3,512,2048]{2,1,0:T(8,128)} %fusion.180, f32[3,512,2048]{2,1,0:T(8,128)} %copy-done, f32[3,512]{1,0:T(4,128)S(1)} %dynamic-slice_bitcast_fusion.2, pred[512,2048]{1,0:T(8,128)(4,1)S(1)} %broadcast_compare_fusion.5, f32[2048,3,64]{0,2,1:T(8,128)} %get-tuple-element.429, pred[]{:T(512)S(6)} %compare.7, ...), kind=kOutput, calls=%fused_computation.37.clone.1 | convolution fusion | flops 438046208 | bytes 55787524 | tf_op jit(solution)/shard_map/while/body/eval_jaxpr/hqk,qhd->khd/dot_general | solution.py:162
  715.1 8.6 dynamic_update_slice.19
  734.1 7.2 fusion.180
  741.3 20.0 %fusion.184 = f32[1,512,3,64]{1,3,2,0:T(8,128)S(1)} fusion(bf16[2048,3,64]{0,2,1:T(8,128)(2,1)S(1)} %get-tuple-element.448, f32[3,512,2048]{2,1,0:T(8,128)} %fusion.180, f32[3,512,2048]{2,1,0:T(8,128)} %copy-done, f32[3,512]{1,0:T(4,128)S(1)} %dynamic-slice_bitcast_fusion.2, pred[512,2048]{1,0:T(8,128)(4,1)S(1)} %broadcast_compare_fusion.5), kind=kOutput, calls=%fused_computation.40.clone.1 | convolution fusion | flops 437259776 | bytes 27400192 | tf_op jit(solution)/shard_map/while/body/eval_jaxpr/hqk,khd->qhd/dot_general | solution.py:161
  761.3 22.4 %fusion.182 = f32[2048,3,64]{0,2,1:T(8,128)} fusion(f32[3,512,2048]{2,1,0:T(8,128)} %fusion.180, f32[3,512,2048]{2,1,0:T(8,128)} %copy-done, f32[3,512]{1,0:T(4,128)S(1)} %dynamic-slice_bitcast_fusion.2, pred[512,2048]{1,0:T(8,128)(4,1)S(1)} %broadcast_compare_fusion.5, f32[2048,3,64]{0,2,1:T(8,128)} %get-tuple-element.429, pred[]{:T(512)S(6)} %compare.7, ...), kind=kOutput, calls=%fused_computation.37.clone.1 | convolution fusion | flops 438046208 | bytes 55787524 | tf_op jit(solution)/shard_map/while/body/eval_jaxpr/hqk,qhd->khd/dot_general | solution.py:162
  784.2 8.6 dynamic_update_slice.19
  813.8 27.4 %reduce-scatter.22.cloned.1.call-done = bf16[512,768]{1,0:T(8,128)(2,1)} async-done(((bf16[2048,768]{1,0:T(8,128)(2,1)}), bf16[512,768]{1,0:T(8,128)(2,1)}) %reduce-scatter.22.cloned.1.call-update) | async-done | bytes 786448 | tf_op jit(solution)/shard_map/reduce_scatter | solution.py:185
  859.5 49.2 %reduce-scatter.30.cloned.1.call-done = f32[96,288]{1,0:T(8,128)} async-done(((f32[768,288]{1,0:T(8,128)}), f32[96,288]{1,0:T(8,128)}) %reduce-scatter.30.cloned.1.call-update) | async-done | bytes 110608
  910.4 62.9 %reduce-scatter.28.cloned.1.call-done = f32[96,192]{1,0:T(8,128)} async-done(((f32[768,192]{1,0:T(8,128)}), f32[96,192]{1,0:T(8,128)}) %reduce-scatter.28.cloned.1.call-update) | async-done | bytes 73744
  977.7 59.5 %reduce-scatter.32.cloned.1.call-done = f32[96,2]{1,0:T(8,128)} async-done(((f32[768,2]{1,0:T(8,128)}), f32[96,2]{1,0:T(8,128)}) %reduce-scatter.32.cloned.1.call-update) | async-done | bytes 784
  1038.1 6.2 psum.8
  1044.3 65.4 %reduce-scatter.26.cloned.1.call-done = f32[2,96,288]{2,1,0:T(8,128)} async-done(((f32[2,768,288]{2,1,0:T(8,128)}), f32[2,96,288]{2,1,0:T(8,128)}) %reduce-scatter.26.cloned.1.call-update) | async-done | bytes 221200 | tf_op jit(solution)/shard_map/reduce_scatter | solution.py:198
  1109.7 72.5 %reduce-scatter.24.cloned.1.call-done = f32[3,96,192]{2,1,0:T(8,128)} async-done(((f32[3,768,192]{2,1,0:T(8,128)}), f32[3,96,192]{2,1,0:T(8,128)}) %reduce-scatter.24.cloned.1.call-update) | async-done | bytes 221200 | tf_op jit(solution)/shard_map/reduce_scatter | solution.py:196
  (261 shorter events, 156.5 us)
Async XLA Ops:
  7.2 28.4 %copy-start.43 = (s32[1,8]{1,0:T(1,128)S(1)}, s32[1,8]{1,0:T(1,128)}, u32[]{:S(2)}) copy-start(s32[1,8]{1,0:T(1,128)} %param.13) | copy-start | bytes 100
  7.2 28.7 %copy-start.31 = (bf16[192,96]{1,0:T(8,128)(2,1)S(1)}, bf16[192,96]{1,0:T(8,128)(2,1)}, u32[]{:S(2)}) copy-start(bf16[192,96]{1,0:T(8,128)(2,1)} %param.15) | copy-start | bytes 110596
  7.2 28.8 %copy-start.25 = (bf16[3,96,192]{2,1,0:T(8,128)(2,1)S(1)}, bf16[3,96,192]{2,1,0:T(8,128)(2,1)}, u32[]{:S(2)}) copy-start(bf16[3,96,192]{2,1,0:T(8,128)(2,1)} %param.14) | copy-start | bytes 331780
  7.2 98.7 %all-gather.6.cloned.1.call-start = ((), (), s32[]{:S(2)}) async-start(), calls=%async_computation.9 | async-start | bytes 3932160 | tf_op jit(solution)/shard_map/all_gather | solution.py:84
  8.6 27.2 %copy-start.28 = (f32[512]{0:T(512)}, f32[512]{0:T(512)S(1)}, u32[]{:S(2)}) copy-start(f32[512]{0:T(512)S(1)} %broadcast_multiply_fusion.1) | copy-start | bytes 6148
  10.1 22.4 %copy-start.37 = (f32[512]{0:T(512)}, f32[512]{0:T(512)S(1)}, u32[]{:S(2)}) copy-start(f32[512]{0:T(512)S(1)} %fusion.97) | copy-start | bytes 6148
  10.1 25.7 %copy-start.32 = (f32[512]{0:T(512)}, f32[512]{0:T(512)S(1)}, u32[]{:S(2)}) copy-start(f32[512]{0:T(512)S(1)} %fusion.106) | copy-start | bytes 6148
  35.5 225.9 %reduce-scatter.16.cloned.1.call-start = ((), (), s32[]{:S(2)}) async-start(), calls=%async_computation.10 | async-start | bytes 7864320 | tf_op jit(solution)/shard_map/reduce_scatter | solution.py:113
  105.8 4.8 copy-start.10
  105.8 4.8 copy-start.12
  118.0 6.8 copy-start.22
  139.1 6.8 copy-start.22
  160.2 6.8 copy-start.22
  181.3 6.8 copy-start.22
  203.2 140.6 %all-gather.8.cloned.1.call-start = ((), (), s32[]{:S(2)}) async-start(), calls=%async_computation.11 | async-start | bytes 3932160 | tf_op jit(solution)/shard_map/all_gather | solution.py:121
  266.5 83.5 %all-gather.10.cloned.1.call-start = ((), (), s32[]{:S(2)}) async-start(), calls=%async_computation.13 | async-start | bytes 3932160 | tf_op jit(solution)/shard_map/all_gather | solution.py:133
  267.1 158.8 %reduce-scatter.20.cloned.1.call-start = ((), (), s32[]{:S(2)}) async-start(), calls=%async_computation.14 | async-start | bytes 7864320 | tf_op jit(solution)/shard_map/reduce_scatter | solution.py:139
  350.0 9.2 copy-start.8
  359.3 3.2 copy-start.20
  367.1 99.2 %reduce-scatter.18.cloned.1.call-start = ((), (), s32[]{:S(2)}) async-start(), calls=%async_computation.12 | async-start | bytes 3932160 | tf_op jit(solution)/shard_map/reduce_scatter | solution.py:126
  372.1 128.4 %all-gather.12.cloned.1.call-start = ((), (), s32[]{:S(2)}) async-start(), calls=%async_computation.15 | async-start | bytes 3932160 | tf_op jit(solution)/shard_map/all_gather | solution.py:145
  466.3 4.4 copy-start.4
  469.5 31.0 %copy-start.35 = (f32[512]{0:T(512)}, f32[512]{0:T(512)S(1)}, u32[]{:S(2)}) copy-start(f32[512]{0:T(512)S(1)} %negate_multiply_fusion.2) | copy-start | bytes 6148
  471.9 369.3 %reduce-scatter.22.cloned.1.call-start = ((), (), s32[]{:S(2)}) async-start(), calls=%async_computation.16 | async-start | bytes 3932160 | tf_op jit(solution)/shard_map/reduce_scatter | solution.py:185
  521.2 4.8 copy-start
  586.9 2.9 copy-start.14
  589.8 4.8 copy-start
  658.9 4.8 copy-start
  725.1 2.9 copy-start.14
  728.0 4.8 copy-start
  793.0 4.1 copy-start.11
  793.0 4.1 copy-start.13
  803.1 6.2 copy-start.7
  803.1 105.6 %reduce-scatter.30.cloned.1.call-start = ((), (), s32[]{:S(2)}) async-start(), calls=%async_computation.20 | async-start | bytes 1327104
  809.2 4.6 copy-start.41
  809.2 32.0 %copy-start.1 = (bf16[512,768]{1,0:T(8,128)(2,1)S(1)}, bf16[512,768]{1,0:T(8,128)(2,1)}, u32[]{:S(2)}) copy-start(bf16[512,768]{1,0:T(8,128)(2,1)} %param.12) | copy-start | bytes 2359300
  809.2 32.0 %copy-start.27 = (f32[768]{0:T(1024)S(1)}, f32[768]{0:T(1024)}, u32[]{:S(2)}) copy-start(f32[768]{0:T(1024)} %copy-done.26) | copy-start | bytes 9220
  809.2 32.0 %copy-start.29 = (f32[512]{0:T(512)S(1)}, f32[512]{0:T(512)}, u32[]{:S(2)}) copy-start(f32[512]{0:T(512)} %copy-done.28) | copy-start | bytes 6148
  809.2 164.1 %reduce-scatter.28.cloned.1.call-start = ((), (), s32[]{:S(2)}) async-start(), calls=%async_computation.19 | async-start | bytes 884736
  813.7 29.1 %copy-start.38 = (f32[512]{0:T(512)S(1)}, f32[512]{0:T(512)}, u32[]{:S(2)}) copy-start(f32[512]{0:T(512)} %copy-done.37) | copy-start | bytes 6148
  813.7 29.1 %copy-start.33 = (f32[512]{0:T(512)S(1)}, f32[512]{0:T(512)}, u32[]{:S(2)}) copy-start(f32[512]{0:T(512)} %copy-done.32) | copy-start | bytes 6148
  813.8 223.5 %reduce-scatter.32.cloned.1.call-start = ((), (), s32[]{:S(2)}) async-start(), calls=%async_computation.21 | async-start | bytes 442368
  846.5 263.2 %reduce-scatter.26.cloned.1.call-start = ((), (), s32[]{:S(2)}) async-start(), calls=%async_computation.18 | async-start | bytes 2654208 | tf_op jit(solution)/shard_map/reduce_scatter | solution.py:198
  853.1 329.0 %reduce-scatter.24.cloned.1.call-start = ((), (), s32[]{:S(2)}) async-start(), calls=%async_computation.17 | async-start | bytes 2654208 | tf_op jit(solution)/shard_map/reduce_scatter | solution.py:196
  859.5 115.4 %copy-start.42 = (f32[512]{0:T(512)S(1)}, f32[512]{0:T(512)}, u32[]{:S(2)}) copy-start(f32[512]{0:T(512)} %get-tuple-element.197) | copy-start | bytes 6148
  859.5 115.4 %copy-start.3 = (f32[512,768]{1,0:T(8,128)S(1)}, f32[512,768]{1,0:T(8,128)}, u32[]{:S(2)}) copy-start(f32[512,768]{1,0:T(8,128)} %copy-done.2) | copy-start | bytes 4718596
  859.5 115.4 %copy-start.5 = (bf16[512,768]{1,0:T(8,128)(2,1)S(1)}, bf16[512,768]{1,0:T(8,128)(2,1)}, u32[]{:S(2)}) copy-start(bf16[512,768]{1,0:T(8,128)(2,1)} %param.19) | copy-start | bytes 2359300
  859.5 115.4 %copy-start.36 = (f32[512]{0:T(512)S(1)}, f32[512]{0:T(512)}, u32[]{:S(2)}) copy-start(f32[512]{0:T(512)} %copy-done.35) | copy-start | bytes 6148
  (25 other events, 34.1 us)
Sparse Core Ops, SparseCore 0:
  35.6 25.8 all-gather.5
  203.3 58.0 reduce-scatter.15
  266.7 28.5 all-gather.7
  296.7 28.5 all-gather.9
  367.2 58.6 reduce-scatter.19
  428.3 37.9 reduce-scatter.17
  472.0 28.5 all-gather.11
  803.2 37.9 reduce-scatter.21
  844.6 64.0 reduce-scatter.29
  911.8 61.3 reduce-scatter.27
  976.9 60.3 reduce-scatter.31
  1041.6 68.0 reduce-scatter.25
  1114.2 67.9 reduce-scatter.23
where the time goes:
time: 1200 us; the launch traced here: 1190 us
  waiting for transfers between devices  515 us (43%)
  matrix products  338 us (28%)
  blocking collectives  164 us (14%)
  local copies, waits for them, and re-layouts  77.5 us (6%)
  other arithmetic  66 us (6%)
  between operations  14.9 us (1%)
  loops' own time  12.3 us (1%)
    unnamed x16, waiting for transfers between devices  172 us
    dot_general x4, matrix products, back_step(): jnp.einsum('hqk,qhd->khd', d_scores, q_block, preferred_element_type=jnp....  89.4 us
    dot_general x4, matrix products, back_step(): jnp.einsum('hqk,khd->qhd', d_scores, keys, preferred_element_type=jnp.flo...  80.2 us
    reduce_scatter x1, waiting for transfers between devices, shards(): lax.psum_scatter(grad_proj, 'fsdp', scatter_dimension=1, tiled=True)  72.5 us
    reduce_scatter x1, waiting for transfers between devices, shards(): lax.psum_scatter(grad_pair, 'fsdp', scatter_dimension=1, tiled=True)  65.4 us
    reduce_scatter x1, waiting for transfers between devices, shards(): lax.psum_scatter(jnp.dot(context, w_back, preferred_element_type=jnp.floa...  58.2 us
    reduce_scatter x1, waiting for transfers between devices, shards(): lax.psum_scatter(dot_nt(d_both, pair_cat), 'tp', scatter_dimension=0, til...  53.7 us
    reduce_scatter x1, waiting for transfers between devices, shards(): lax.psum_scatter(jnp.dot(hidden, w_last, preferred_element_type=jnp.float...  37.2 us
  transfers between devices with their start and end apart: 13, of which 10 were waited for; matrix products, arithmetic and copies ran while one was open for 5% of the time, Pallas kernels for 0%

commit v1 on v0

v1 whole, which is shorter than its diff:
```python
import functools

import jax
import jax.numpy as jnp
from jax import lax
from jax.experimental import pallas as pl
from jax.experimental.pallas import tpu as pltpu
from jax.sharding import PartitionSpec as P

HEAD_DIM = 64
HALF = HEAD_DIM // 2
WIDE = 128
TILE = 256
FAR = -1e30
VMEM_BYTES = 56 * 1024 * 1024
BF16 = jnp.bfloat16
F32 = jnp.float32

NN = (((1,), (0,)), ((), ()))
NT = (((1,), (1,)), ((), ()))
TN = (((0,), (0,)), ((), ()))


def mm(left, right, dims=NN):
    return lax.dot_general(left, right, dims, preferred_element_type=F32)


def positions(lengths, total):
    ends = jnp.cumsum(lengths)
    starts = ends - lengths
    index = jnp.arange(total, dtype=jnp.int32)
    segment = jnp.sum((index[:, None] >= ends[None, :]).astype(jnp.int32), axis=1)
    onehot = segment[:, None] == jnp.arange(lengths.shape[0], dtype=jnp.int32)[None, :]
    first = jnp.sum(jnp.where(onehot, starts[None, :], 0), axis=1)
    last = jnp.sum(jnp.where(onehot, ends[None, :], 0), axis=1)
    return (segment, index - first, first, last)


def rope_tables(place):
    freq = jnp.exp(
        -jnp.log(jnp.float32(160000.0)) * jnp.arange(HALF, dtype=F32) * (2.0 / HEAD_DIM)
    )
    angle = freq[:, None] * place.astype(F32)[None, :]
    return (jnp.cos(angle), jnp.sin(angle))


def pieces_of(row):
    high = row.astype(BF16).astype(F32)
    rest = row - high
    middle = rest.astype(BF16).astype(F32)
    return high, middle, rest - middle


def extend(body, rows):
    rest = WIDE - body.shape[0] - sum(row.shape[0] for row in rows)
    return jnp.concatenate([body, *rows, jnp.zeros((rest, body.shape[1]), F32)], axis=0)


def forward_kernel(
    low_ref, high_ref, tok_ref, gain_ref, seg_ref, cos_ref, sin_ref, wproj_ref, wback_ref,
    normed_ref, query_ref, keys_ref, values_ref, ctx_ref, log_ref, attn_ref,
    nat_ref,
):
    group = tok_ref.shape[0]
    lanes = wback_ref.shape[0]
    heads = lanes // HEAD_DIM
    parts = 8
    count = group // TILE

    @pl.loop(0, count)
    def project(step):
        here = pl.ds(pl.multiple_of(step * TILE, TILE), TILE)
        rows = tok_ref[here, :].astype(F32)
        center = rows - jnp.mean(rows, axis=-1, keepdims=True)
        spread = jnp.mean(center * center, axis=-1, keepdims=True)
        normed = (center * lax.rsqrt(spread + 1e-05) * gain_ref[...]).astype(BF16)
        normed_ref[here, :] = normed
        mixed = mm(wproj_ref[...], normed, NT)
        cosine = cos_ref[:, here]
        sine = sin_ref[:, here]
        segment = seg_ref[:, here]
        same = (segment == lax.broadcasted_iota(jnp.int32, (parts, TILE), 0)).astype(F32)
        ones = jnp.ones((parts, TILE), F32)

        def rotated(top):
            first = mixed[top : top + HALF]
            second = mixed[top + HALF : top + HEAD_DIM]
            return jnp.concatenate(
                [first * cosine - second * sine, second * cosine + first * sine], axis=0
            )

        for head in range(heads):
            top = head * HEAD_DIM
            query = rotated(top) * (HEAD_DIM ** (-0.5))
            query_ref[head, :, here] = extend(query, [(1.0 - same) * FAR]).astype(BF16)
            key = extend(rotated(lanes + top), [same, ones]).astype(BF16)
            keys_ref[head, :, here] = key[:HEAD_DIM]
            nat_ref[head, here, :] = key.T
            value = mixed[2 * lanes + top : 2 * lanes + top + HEAD_DIM]
            values_ref[head, :, here] = value.astype(BF16)

    @pl.loop(0, count)
    def attend(step):
        here = pl.ds(pl.multiple_of(step * TILE, TILE), TILE)

        def inner(at, carry):
            there = pl.ds(pl.multiple_of(at * TILE, TILE), TILE)
            out = []
            for head in range(heads):
                top, total, acc = carry[head]
                scores = mm(nat_ref[head, there, :], query_ref[head, :, here])
                new_top = jnp.maximum(top, jnp.max(scores, axis=0, keepdims=True))
                scale = jnp.exp(top - new_top)
                expo = jnp.exp(scores - new_top)
                total = total * scale + jnp.sum(expo, axis=0, keepdims=True)
                acc = acc * scale + mm(values_ref[head, :, there], expo.astype(BF16))
                out.append((new_top, total, acc))
            return tuple(out)

        start = (
            jnp.full((1, TILE), -jnp.inf, F32),
            jnp.zeros((1, TILE), F32),
            jnp.zeros((HEAD_DIM, TILE), F32),
        )
        done = lax.fori_loop(low_ref[step], high_ref[step], inner, (start,) * heads)
        ctx = jnp.concatenate([acc / total for _, total, acc in done], axis=0).astype(BF16)
        ctx_ref[:, here] = ctx
        logs = [top + jnp.log(total) for top, total, _ in done]
        log_ref[:, here] = jnp.concatenate(
            logs + [jnp.zeros((8 - heads, TILE), F32)], axis=0
        )
        attn_ref[here, :] = mm(ctx.T, wback_ref[...]).astype(BF16)


def backward_kernel(
    low_ref, high_ref, dattn_ref, normed_ref, query_ref, keys_ref, values_ref, ctx_ref, log_ref,
    seg_ref, cos_ref, sin_ref, wproj_ref, wback_ref,
    dnormed_ref, gproj_ref, gback_ref,
    qx_ref, kx_ref, vx_ref, dx_ref, dq_ref, dmix_ref,
):
    group = dattn_ref.shape[0]
    lanes = wback_ref.shape[0]
    heads = lanes // HEAD_DIM
    parts = 8
    count = group // TILE
    scale = HEAD_DIM ** (-0.5)

    @pl.loop(0, count)
    def prepare(step):
        here = pl.ds(pl.multiple_of(step * TILE, TILE), TILE)
        d_ctx = mm(wback_ref[...], dattn_ref[here, :], NT).astype(BF16).astype(F32)
        ctx = ctx_ref[:, here].astype(F32)
        segment = seg_ref[:, here]
        same = (segment == lax.broadcasted_iota(jnp.int32, (parts, TILE), 0)).astype(F32)
        ones = jnp.ones((parts, TILE), F32)
        blank = jnp.zeros((parts - 3, TILE), F32)
        logs = log_ref[:, here]
        for head in range(heads):
            rows = slice(head * HEAD_DIM, (head + 1) * HEAD_DIM)
            delta = -jnp.sum(d_ctx[rows] * ctx[rows], axis=0, keepdims=True)
            dx_ref[head, :, here] = extend(d_ctx[rows], [*pieces_of(delta), blank]).astype(BF16)
            log = -logs[head : head + 1]
            query = query_ref[head, : HEAD_DIM + parts, here].astype(F32)
            qx_ref[head, :, here] = extend(query, [*pieces_of(log), blank]).astype(BF16)
            key = keys_ref[head, :, here].astype(F32)
            kx_ref[head, here, :] = extend(key, [same, ones]).astype(BF16).T
            value = values_ref[head, :, here].astype(F32)
            vx_ref[head, here, :] = extend(value, [ones]).astype(BF16).T
            dq_ref[head, :, here] = jnp.zeros((HEAD_DIM, TILE), F32)

    def turned_back(grad, where):
        cosine = cos_ref[:, where]
        sine = sin_ref[:, where]
        first = grad[:HALF]
        second = grad[HALF:]
        return jnp.concatenate(
            [first * cosine + second * sine, second * cosine - first * sine], axis=0
        ).astype(BF16)

    @pl.loop(0, count)
    def attend(step):
        here = pl.ds(pl.multiple_of(step * TILE, TILE), TILE)

        def inner(at, carry):
            there = pl.ds(pl.multiple_of(at * TILE, TILE), TILE)
            out = []
            for head in range(heads):
                d_key, d_value = carry[head]
                query = qx_ref[head, :, there]
                d_out = dx_ref[head, :, there]
                probs = jnp.exp(mm(kx_ref[head, here, :], query))
                d_probs = mm(vx_ref[head, here, :], d_out)
                d_scores = (probs * d_probs).astype(BF16)
                d_value = d_value + mm(d_out[:HEAD_DIM], probs.astype(BF16), NT)
                d_key = d_key + mm(query[:HEAD_DIM], d_scores, NT)
                dq_ref[head, :, there] += mm(keys_ref[head, :, here], d_scores)
                out.append((d_key, d_value))
            return tuple(out)

        zero = jnp.zeros((HEAD_DIM, TILE), F32)
        done = lax.fori_loop(low_ref[step], high_ref[step], inner, ((zero, zero),) * heads)
        for head in range(heads):
            top = head * HEAD_DIM
            d_key, d_value = done[head]
            dmix_ref[lanes + top : lanes + top + HEAD_DIM, here] = turned_back(d_key, here)
            dmix_ref[2 * lanes + top : 2 * lanes + top + HEAD_DIM, here] = d_value.astype(BF16)

    @pl.loop(0, count)
    def finish(step):
        here = pl.ds(pl.multiple_of(step * TILE, TILE), TILE)
        for head in range(heads):
            top = head * HEAD_DIM
            dmix_ref[top : top + HEAD_DIM, here] = turned_back(dq_ref[head, :, here] * scale, here)
        dnormed_ref[here, :] = mm(dmix_ref[:, here].T, wproj_ref[...]).astype(BF16)

    width = normed_ref.shape[1]
    columns = WIDE
    gback = mm(ctx_ref[...], dattn_ref[...])
    gback_ref[...] = gback.astype(BF16)

    @pl.loop(0, 3)
    def weights(step):
        rows = pl.ds(pl.multiple_of(step * lanes, 64), lanes)
        gproj_ref[rows, :] = mm(dmix_ref[rows, :], normed_ref[...]).astype(BF16)


def vmem_spec():
    return pl.BlockSpec(memory_space=pltpu.VMEM)


def smem_spec():
    return pl.BlockSpec(memory_space=pltpu.SMEM)


def attention_forward(low, high, tok, gain, seg, cosine, sine, wproj, wback):
    group, model = tok.shape
    lanes = wback.shape[0]
    heads = lanes // HEAD_DIM
    shape = jax.ShapeDtypeStruct
    return pl.pallas_call(
        forward_kernel,
        out_shape=(
            shape((group, model), BF16),
            shape((heads, WIDE, group), BF16),
            shape((heads, HEAD_DIM, group), BF16),
            shape((heads, HEAD_DIM, group), BF16),
            shape((lanes, group), BF16),
            shape((8, group), F32),
            shape((group, model), BF16),
        ),
        in_specs=[smem_spec()] * 2 + [vmem_spec()] * 7,
        out_specs=[vmem_spec()] * 7,
        scratch_shapes=[pltpu.VMEM((heads, group, WIDE), BF16)],
        compiler_params=pltpu.CompilerParams(vmem_limit_bytes=VMEM_BYTES),
        cost_estimate=pl.CostEstimate(
            flops=2 * group * model * lanes * 4 + 2 * group * group * lanes,
            bytes_accessed=group * model * 8,
            transcendentals=group * group,
        ),
        name="attention_forward",
    )(low, high, tok, gain, seg, cosine, sine, wproj, wback)


def attention_backward(low, high, d_attn, kept, seg, cosine, sine, wproj, wback):
    group, model = d_attn.shape
    lanes = wback.shape[0]
    heads = lanes // HEAD_DIM
    shape = jax.ShapeDtypeStruct
    return pl.pallas_call(
        backward_kernel,
        out_shape=(
            shape((group, model), BF16),
            shape((3 * lanes, model), BF16),
            shape((lanes, model), BF16),
        ),
        in_specs=[smem_spec()] * 2 + [vmem_spec()] * 12,
        out_specs=[vmem_spec()] * 3,
        scratch_shapes=[
            pltpu.VMEM((heads, WIDE, group), BF16),
            pltpu.VMEM((heads, group, WIDE), BF16),
            pltpu.VMEM((heads, group, WIDE), BF16),
            pltpu.VMEM((heads, WIDE, group), BF16),
            pltpu.VMEM((heads, HEAD_DIM, group), F32),
            pltpu.VMEM((3 * lanes, group), BF16),
        ],
        compiler_params=pltpu.CompilerParams(vmem_limit_bytes=VMEM_BYTES),
        cost_estimate=pl.CostEstimate(
            flops=2 * group * model * lanes * 8 + 4 * group * group * lanes,
            bytes_accessed=group * model * 12,
            transcendentals=group * group,
        ),
        name="attention_backward",
    )(low, high, d_attn, *kept, seg, cosine, sine, wproj, wback)


def swap(value, axis, bit):
    size = lax.axis_size(axis)
    return lax.ppermute(value, axis, [(i, i ^ bit) for i in range(size)])


def gather_rows(rows):
    me = lax.axis_index("tp")
    far = swap(rows, "tp", 2)
    near = swap(rows, "tp", 1)
    corner = swap(far, "tp", 1)
    whole = jnp.zeros((4,) + rows.shape, rows.dtype)
    for bit, block in ((0, rows), (1, near), (2, far), (3, corner)):
        whole = lax.dynamic_update_index_in_dim(whole, block, me ^ bit, 0)
    return whole.reshape(4 * rows.shape[0], rows.shape[1])


def scatter_rows(partial):
    me = lax.axis_index("tp")
    chip, core = me // 2, me % 2
    grid = partial.reshape(2, 2, partial.shape[0] // 4, partial.shape[1])
    take = functools.partial(lax.dynamic_index_in_dim, keepdims=False)
    came = swap(take(grid, 1 - core, 1), "tp", 1)
    pair = came.astype(F32) + take(grid, core, 1).astype(F32)
    far = swap(take(pair, 1 - chip, 0).astype(BF16), "tp", 2)
    return far.astype(F32) + take(pair, chip, 0)


def center_rows(values):
    center = values - jnp.mean(values, axis=-1, keepdims=True)
    spread = jnp.mean(center * center, axis=-1, keepdims=True)
    inverse = lax.rsqrt(spread + 1e-05)
    return center * inverse, inverse


def norm_pull(normal, inverse, gain, grad):
    scaled = grad * gain
    mean = jnp.mean(scaled, axis=-1, keepdims=True)
    along = jnp.mean(scaled * normal, axis=-1, keepdims=True)
    return (scaled - mean - normal * along) * inverse


def geglu(up_in, gate_in):
    return jax.nn.gelu(up_in, approximate=False) * gate_in


def shards(tokens, seq_lengths, w_qkv, w_out, w_in, w_down, gains, cotangent):
    rows, model = tokens.shape
    slab = w_qkv.shape[1]
    lanes = w_qkv.shape[2]
    units = w_in.shape[2]
    group = rows * lax.axis_size("tp")
    count = group // TILE

    own_proj = jnp.transpose(w_qkv, (1, 0, 2)).reshape(slab, 3 * lanes)
    own_pair = jnp.transpose(w_in, (1, 0, 2)).reshape(slab, 2 * units)
    first = jnp.concatenate([own_proj, gains.T], axis=1)
    rest = jnp.concatenate([own_pair, w_out.T, w_down.T], axis=1)
    whole_first = lax.all_gather(first, "fsdp", axis=0, tiled=True)
    whole_rest = lax.all_gather(rest, "fsdp", axis=0, tiled=True)
    proj_t = whole_first[:, : 3 * lanes].T
    gain_one = whole_first[:, 3 * lanes].astype(F32)[None, :]
    gain_two = whole_first[:, 3 * lanes + 1].astype(F32)[None, :]
    pair_cat = whole_rest[:, : 2 * units]
    back = whole_rest[:, 2 * units : 2 * units + lanes].T
    last_t = whole_rest[:, 2 * units + lanes :]

    segment, place, seq_first, seq_last = positions(seq_lengths[0], group)
    cosine, sine = rope_tables(place)
    low = seq_first[::TILE] // TILE
    high = (seq_last[TILE - 1 :: TILE] + TILE - 1) // TILE
    seg = segment[None, :]

    full_tok = gather_rows(tokens)
    full_cot = gather_rows(cotangent)
    normed1, query, keys, values, ctx, logs, attn_part = attention_forward(
        low, high, full_tok, gain_one, seg, cosine, sine, proj_t, back
    )
    inputs = tokens.astype(F32)
    h_mid = inputs + scatter_rows(attn_part)
    normal2, inverse2 = center_rows(h_mid)
    full2 = gather_rows((normal2 * gain_two).astype(BF16))
    both = mm(full2, pair_cat)
    up_in = both[:, :units]
    gate_in = both[:, units:]
    hidden = geglu(up_in, gate_in).astype(BF16)
    mlp = scatter_rows(mm(hidden, last_t, NT).astype(BF16))
    output = (h_mid + mlp).astype(BF16)
    d_hid = mm(full_cot, last_t)
    grad_last_t = mm(full_cot, hidden, TN)
    _, geglu_pull = jax.vjp(geglu, up_in, gate_in)
    d_up, d_gate = geglu_pull(d_hid)
    d_both = jnp.concatenate([d_up, d_gate], axis=1).astype(BF16)
    d_normed2 = scatter_rows(mm(d_both, pair_cat, NT).astype(BF16))
    grad_pair_cat = mm(full2, d_both, TN)
    d_mid = cotangent.astype(F32) + norm_pull(normal2, inverse2, gain_two, d_normed2)
    full_d = gather_rows(d_mid.astype(BF16))
    d_part, grad_proj_t, grad_back = attention_backward(
        low, high, full_d, (normed1, query, keys, values, ctx, logs),
        seg, cosine, sine, proj_t, back,
    )
    d_normed1 = scatter_rows(d_part)
    normal1, inverse1 = center_rows(inputs)
    grad_tokens = (d_mid + norm_pull(normal1, inverse1, gain_one, d_normed1)).astype(BF16)

    late = jnp.concatenate([grad_proj_t, grad_back], axis=0).T
    early = jnp.concatenate([grad_pair_cat, grad_last_t], axis=1).astype(BF16)
    own_early = lax.psum_scatter(early, "fsdp", scatter_dimension=0, tiled=True).astype(F32)
    own_late = lax.psum_scatter(late, "fsdp", scatter_dimension=0, tiled=True).astype(F32)
    sum_proj = own_late[:, : 3 * lanes]
    sum_pair = own_early[:, : 2 * units]
    terms = jnp.stack(
        [
            jnp.sum(sum_proj * own_proj.astype(F32), axis=1),
            jnp.sum(sum_pair * own_pair.astype(F32), axis=1),
        ]
    ) / gains.astype(F32)
    terms = terms + swap(terms, "tp", 1)
    grad_gains = terms + swap(terms, "tp", 2)
    grad_qkv = jnp.transpose(sum_proj.reshape(slab, 3, lanes), (1, 0, 2))
    grad_in = jnp.transpose(sum_pair.reshape(slab, 2, units), (1, 0, 2))
    grad_out = own_late[:, 3 * lanes :].T
    grad_down = own_early[:, 2 * units :].T
    return (output, grad_tokens, grad_qkv, grad_out, grad_in, grad_down, grad_gains)


def solution(mesh):
    rows = P(("fsdp", "tp"), None)
    weights = (P(None, "fsdp", "tp"), P("tp", "fsdp"), P(None, "fsdp", "tp"), P("tp", "fsdp"))
    gains = P(None, "fsdp")
    return jax.shard_map(
        shards,
        mesh=mesh,
        in_specs=(rows, P("fsdp", None), *weights, gains, rows),
        out_specs=(rows, rows, *weights, gains),
        check_vma=False,
    )
```

time: 1200 us -> 394 us (0.33)
  waiting for transfers between devices: 515 us -> 146 us
  matrix products: 338 us -> 16.4 us
  blocking collectives: 164 us -> 34.8 us
  Pallas kernels: 0 us -> 97.2 us
  other arithmetic: 66 us -> 25.9 us
  local copies, waits for them, and re-layouts: 77.5 us -> 46.6 us
  loops' own time: 12.3 us -> 0 us
    reduce_scatter x6 -> x1, waiting for transfers between devices: 314 us -> 0.01 us  [shards(): lax.psum_scatter(early, 'fsdp', scatter_dimension=0, tiled=True).astype(F32)]
    dot_general x38 -> x6, matrix products: 329 us -> 16.4 us  [mm(): return lax.dot_general(left, right, dims, preferred_element_type=F32)]
    unnamed x16 -> x4, waiting for transfers between devices: 172 us -> 45.4 us
    all_gather x5 -> x1, blocking collectives: 158 us -> 34.8 us  [shards(): whole_first = lax.all_gather(first, 'fsdp', axis=0, tiled=True)]
    ppermute x0 -> x22, waiting for transfers between devices: none -> 97.6 us  [swap(): return lax.ppermute(value, axis, [(i, i ^ bit) for i in range(size)])]
    pallas_call x0 -> x2, Pallas kernels: none -> 97.2 us  [the longest x1 49.6 us: attention_backward(): pl.pallas_call(backward_kernel, out_shape=(shape((group, model), BF16), s...]
    reduce_sum x13 -> x8, other arithmetic: 42.5 us -> 8.66 us  [the longest x2 3.67 us: norm_pull(): mean = jnp.mean(scaled, axis=-1, keepdims=True)]
    dynamic_update_slice x8 -> x14, local copies, waits for them, and re-layouts: 36.1 us -> 9.28 us  [gather_rows(): whole = lax.dynamic_update_index_in_dim(whole, block, me ^ bit, 0)]
  transfers between devices with their start and end apart: 13 -> 25, of which waited for: 10 -> 13; matrix products, arithmetic and copies ran while one was open for 5% -> 16% of each run, Pallas kernels for 0% -> 13%
where the time goes in v1:
time: 394 us; the launch traced here: 392 us
  waiting for transfers between devices  146 us (37%)
  Pallas kernels  97.2 us (25%)
  local copies, waits for them, and re-layouts  46.6 us (12%)
  blocking collectives  34.8 us (9%)
  other arithmetic  25.9 us (7%)
  matrix products  16.4 us (4%)
  between operations  14.2 us (4%)
  starting transfers between devices  11.6 us (3%)
    ppermute x22, waiting for transfers between devices, swap(): return lax.ppermute(value, axis, [(i, i ^ bit) for i in range(size)])  97.6 us
    pallas_call x1, Pallas kernels, attention_backward(): pl.pallas_call(backward_kernel, out_shape=(shape((group, model), BF16), s...  49.6 us
    pallas_call x1, Pallas kernels, attention_forward(): pl.pallas_call(forward_kernel, out_shape=(shape((group, model), BF16), sh...  47.6 us
    unnamed x4, waiting for transfers between devices  45.4 us
    all_gather x1, blocking collectives, shards(): whole_first = lax.all_gather(first, 'fsdp', axis=0, tiled=True)  34.8 us
    unnamed x35, local copies, waits for them, and re-layouts  16.9 us
    dot_general x6, matrix products, mm(): return lax.dot_general(left, right, dims, preferred_element_type=F32)  16.4 us
    ppermute x22, starting transfers between devices, swap(): return lax.ppermute(value, axis, [(i, i ^ bit) for i in range(size)])  11.5 us
  transfers between devices with their start and end apart: 25, of which 13 were waited for; matrix products, arithmetic and copies ran while one was open for 16% of the time, Pallas kernels for 13%

profile of v1, /device:TPU:0, one launch (start us, length us, event | category | flops | bytes accessed | tf_op | source)
XLA Modules:
  0.0 392.4 jit_solution(15817899970752081435)
XLA Ops:
  7.7 2.6 collective-permute-start.1
  18.2 34.8 %all_gather.6 = bf16[768,578]{1,0:T(8,128)(2,1)S(1)} all-gather(bf16[96,578]{1,0:T(8,128)(2,1)S(1)} %copy.56), channel_id=1, replica_groups=mesh['fsdp'=8,'tp'=4] {'fsdp'}, dimensions={0}, use_global_device_ids=true | all-gather | bytes 998784 | tf_op jit(solution)/shard_map/all_gather | solution.py:353
  53.8 1.3 copy.74
  55.6 1.8 multiply_sine_fusion
  57.5 1.9 broadcast.191.clone.1
  63.1 2.8 all-gather.2.cloned.1.call-done
  65.9 1.2 slice.58
  68.0 47.6 %attention_forward.1 = (bf16[2048,768]{1,0:T(8,128)(2,1)}, bf16[3,128,2048]{2,1,0:T(8,128)(2,1)}, bf16[3,64,2048]{2,1,0:T(8,128)(2,1)}, bf16[3,64,2048]{2,1,0:T(...) custom-call(s32[8]{0:T(128)} %get-tuple-element.73.low_ref, ...), custom_call_target="tpu_custom_call" | custom-call | flops 4026531840 | bytes 12582912 | tf_op jit(solution)/shard_map/attention_forward/pallas_call | solution.py:240
  115.7 2.7 dynamic-slice_bitcast_fusion.3
  119.2 2.9 collective-permute-done.3
  122.0 1.7 convert_add_fusion.3
  123.8 1.7 copy-done.3
  127.4 11.5 %collective-permute-done.11 = bf16[512,768]{1,0:T(8,128)(2,1)} collective-permute-done((bf16[512,768]{1,0:T(8,128)(2,1)S(1)}, bf16[512,768]{1,0:T(8,128)(2,1)}, u32[]{:S(2)}, u32[]{:S(2)}) %collective-permute-start.11) | collective-permute-done | bytes 786464 | tf_op jit(solution)/shard_map/ppermute | solution.py:298
  138.9 16.5 %collective-permute-done.4 = bf16[512,768]{1,0:T(8,128)(2,1)} collective-permute-done((bf16[512,768]{1,0:T(8,128)(2,1)}, bf16[512,768]{1,0:T(8,128)(2,1)}, u32[]{:S(2)}, u32[]{:S(2)}) %collective-permute-start.4) | collective-permute-done | bytes 786464 | tf_op jit(solution)/shard_map/ppermute | solution.py:298
  155.3 2.2 fusion.39
  159.6 1.2 bitcast_dynamic-update-slice_fusion.5
  160.8 16.8 %collective-permute-done.6 = bf16[512,768]{1,0:T(8,128)(2,1)S(1)} collective-permute-done((bf16[512,768]{1,0:T(8,128)(2,1)S(1)}, bf16[512,768]{1,0:T(8,128)(2,1)S(1)}, u32[]{:S(2)}, u32[]{:S(2)}) %collective-permute-start.6) | collective-permute-done | bytes 786464 | tf_op jit(solution)/shard_map/ppermute | solution.py:298
  177.8 2.1 collective-permute-done.7
  180.0 2.1 fusion.24
  182.1 6.4 %add_convert_fusion = (bf16[2048,288]{0,1:T(8,128)(2,1)S(1)}, f32[2048,288]{0,1:T(8,128)S(1)}, f32[2048,288]{0,1:T(8,128)S(1)}) fusion(f32[2048,576]{0,1:T(8,128)S(1)} %fusion.24, bf16[2048,768]{1,0:T(8,128)(2,1)S(1)} %bitcast.153, bf16[768,1056]{1,0:T(8,128)(2,1)S(1)} %copy-done.10), kind=kOutput, calls=%fused_computation.13 | convolution fusion | flops 949026816 | bytes 14352384 | tf_op jit(solution)/shard_map/dot_general | solution.py:25
  188.5 1.4 multiply_convert_fusion
  189.9 1.8 convolution_convert_fusion.1
  192.0 2.9 convolution_convert_fusion
  196.8 1.8 collective-permute-done.13
  199.9 2.0 fusion.22
  201.9 14.5 %collective-permute-done.9 = bf16[512,768]{1,0:T(8,128)(2,1)S(1)} collective-permute-done((bf16[512,768]{1,0:T(8,128)(2,1)S(1)}, bf16[512,768]{1,0:T(8,128)(2,1)S(1)}, u32[]{:S(2)}, u32[]{:S(2)}) %collective-permute-start.9) | collective-permute-done | bytes 786464 | tf_op jit(solution)/shard_map/ppermute | solution.py:298
  216.5 16.1 %collective-permute-done.14 = bf16[512,768]{1,0:T(8,128)(2,1)S(1)} collective-permute-done((bf16[512,768]{1,0:T(8,128)(2,1)S(1)}, bf16[512,768]{1,0:T(8,128)(2,1)S(1)}, u32[]{:S(2)}, u32[]{:S(2)}) %collective-permute-start.14) | collective-permute-done | bytes 786464 | tf_op jit(solution)/shard_map/ppermute | solution.py:298
  232.5 1.6 fusion.33
  234.4 1.6 bitcast_dynamic-update-slice_fusion.3
  235.9 1.7 copy-done.5
  239.5 1.2 pad_maximum_fusion.5
  240.7 2.6 copy.72
  243.3 13.2 %collective-permute-done.16 = bf16[512,768]{1,0:T(8,128)(2,1)S(1)} collective-permute-done((bf16[512,768]{1,0:T(8,128)(2,1)}, bf16[512,768]{1,0:T(8,128)(2,1)S(1)}, u32[]{:S(2)}, u32[]{:S(2)}) %collective-permute-start.16) | collective-permute-done | bytes 786464 | tf_op jit(solution)/shard_map/ppermute | solution.py:298
  256.6 2.1 bitcast_dynamic-update-slice_fusion.2
  260.6 49.6 %attention_backward.1 = (bf16[2048,768]{1,0:T(8,128)(2,1)}, bf16[576,768]{1,0:T(8,128)(2,1)}, bf16[192,768]{1,0:T(8,128)(2,1)}) custom-call(s32[8]{0:T(128)} %get-tuple-element.73.low_ref, s32[8]{0:T(128)} %get-tuple-element.72.high_ref, bf16[2048,768]{1,0:T(8,128)(2,1)} %bitcast.150, bf16[2048,768]{1,0:T(8,128)(2,1)} %get-tuple-element.18.normed_ref, ...), custom_call_target="tpu_custom_call" | custom-call | flops 8053063680 | bytes 18874368 | tf_op jit(solution)/shard_map/attention_backward/pallas_call | solution.py:269
  310.1 2.8 dynamic-slice_bitcast_fusion
  313.5 1.5 copy.70
  315.0 1.8 collective-permute-done.18
  316.8 2.2 convert_add_fusion
  319.0 1.6 copy-done.1
  322.4 1.6 slice.66
  324.0 1.2 reshape.160
  327.6 1.7 copy.69
  330.3 45.3 %reduce-scatter.7.cloned.1.call-done = bf16[96,768]{1,0:T(8,128)(2,1)} async-done(((bf16[768,768]{1,0:T(8,128)(2,1)}), bf16[96,768]{1,0:T(8,128)(2,1)}) %reduce-scatter.7.cloned.1.call-update) | async-done | bytes 147472
  376.8 1.2 multiply_reduce_fusion.2
  378.1 2.0 fusion.34
  380.1 1.5 fusion.15
  381.7 1.5 collective-permute-start.21
  (130 shorter events, 36.4 us)
Async XLA Ops:
  7.2 58.8 %all-gather.2.cloned.1.call-start = ((), (), s32[]{:S(2)}) async-start(), calls=%async_computation.2 | async-start | bytes 1990656 | tf_op jit(solution)/shard_map/all_gather | solution.py:354
  7.2 53.1 %collective-permute-start = (bf16[512,768]{1,0:T(8,128)(2,1)}, bf16[512,768]{1,0:T(8,128)(2,1)S(1)}, u32[]{:S(2)}, u32[]{:S(2)}) collective-permute-start(bf16[512,768]{1,0:T(8,128)(2,1)} %param.8), channel_id=1, source_target_pairs={{0,1},{1,0},{2,3},{3,2},{4,5},{5,4},{6,7},{7,6},{8,9},{9,8},{10,11... | collective-permute-start | bytes 2359304 | tf_op jit(solution)/shard_map/ppermute | solution.py:298
  7.7 49.7 %collective-permute-start.1 = (bf16[512,768]{1,0:T(8,128)(2,1)}, bf16[512,768]{1,0:T(8,128)(2,1)S(1)}, u32[]{:S(2)}, u32[]{:S(2)}) collective-permute-start(bf16[512,768]{1,0:T(8,128)(2,1)} %param.8), channel_id=1, source_target_pairs={{0,2},{1,3},{2,0},{3,1},{4,6},{5,7},{6,4},{7,5},{8,10},{9,11},{10,... | collective-permute-start | bytes 2359304 | tf_op jit(solution)/shard_map/ppermute | solution.py:298
  11.5 4.7 %copy-start.7 = (bf16[96,576]{1,0:T(8,128)(2,1)}, bf16[96,576]{1,0:T(8,128)(2,1)S(1)}, u32[]{:S(2)}) copy-start(bf16[96,576]{1,0:T(8,128)(2,1)S(1)} %reshape.151) | copy-start | bytes 331780
  14.3 308.1 %reduce-scatter.9.cloned.1.call-start = ((), (), s32[]{:S(2)}) async-start(), calls=%async_computation.4 | async-start | bytes 1548288 | tf_op jit(solution)/shard_map/reduce_scatter | solution.py:402
  15.9 41.6 %copy-start.11 = (s32[2048]{0:T(1024)}, s32[2048]{0:T(1024)S(1)}, u32[]{:S(2)}) copy-start(s32[2048]{0:T(1024)S(1)} %convert_reduce_fusion.3) | copy-start | bytes 24580
  17.3 36.5 %copy-start.6 = (bf16[96,3,192]{0,2,1:T(8,128)(2,1)}, bf16[96,3,192]{0,2,1:T(8,128)(2,1)S(1)}, u32[]{:S(2)}) copy-start(bf16[96,3,192]{0,2,1:T(8,128)(2,1)S(1)} %copy.55) | copy-start | bytes 331780
  53.8 5.6 %copy-start = (bf16[512,768]{1,0:T(8,128)(2,1)S(1)}, bf16[512,768]{1,0:T(8,128)(2,1)}, u32[]{:S(2)}) copy-start(bf16[512,768]{1,0:T(8,128)(2,1)} %param.8) | copy-start | bytes 2359300
  57.5 4.7 %collective-permute-start.2 = (bf16[512,768]{1,0:T(8,128)(2,1)S(1)}, bf16[512,768]{1,0:T(8,128)(2,1)S(1)}, u32[]{:S(2)}, u32[]{:S(2)}) collective-permute-start(bf16[512,768]{1,0:T(8,128)(2,1)S(1)} %collective-permute-done.1), channel_id=1, source_target_pairs={{0,1},{1,0},{2,3},{3,2},{4,5},{5,4},{6,7},{7,6},{8,9},{9,8},{10,11... | collective-permute-start | bytes 2359304 | tf_op jit(solution)/shard_map/ppermute | solution.py:298
  115.7 2.7 copy-start.4
  118.4 3.6 collective-permute-start.3
  118.4 20.4 %collective-permute-start.11 = (bf16[512,768]{1,0:T(8,128)(2,1)S(1)}, bf16[512,768]{1,0:T(8,128)(2,1)}, u32[]{:S(2)}, u32[]{:S(2)}) collective-permute-start(bf16[512,768]{1,0:T(8,128)(2,1)S(1)} %copy-done.4), channel_id=1, source_target_pairs={{0,2},{1,3},{2,0},{3,1},{4,6},{5,7},{6,4},{7,5},{8,10},{9,11},{10,... | collective-permute-start | bytes 2359304 | tf_op jit(solution)/shard_map/ppermute | solution.py:298
  123.7 1.7 copy-start.3
  126.5 28.9 %collective-permute-start.4 = (bf16[512,768]{1,0:T(8,128)(2,1)}, bf16[512,768]{1,0:T(8,128)(2,1)}, u32[]{:S(2)}, u32[]{:S(2)}) collective-permute-start(bf16[512,768]{1,0:T(8,128)(2,1)} %fusion.26), channel_id=1, source_target_pairs={{0,2},{1,3},{2,0},{3,1},{4,6},{5,7},{6,4},{7,5},{8,10},{9,11},{10,... | collective-permute-start | bytes 2359304 | tf_op jit(solution)/shard_map/ppermute | solution.py:298
  127.2 32.4 %collective-permute-start.10 = (bf16[512,768]{1,0:T(8,128)(2,1)S(1)}, bf16[512,768]{1,0:T(8,128)(2,1)S(1)}, u32[]{:S(2)}, u32[]{:S(2)}) collective-permute-start(bf16[512,768]{1,0:T(8,128)(2,1)S(1)} %copy-done.4), channel_id=1, source_target_pairs={{0,1},{1,0},{2,3},{3,2},{4,5},{5,4},{6,7},{7,6},{8,9},{9,8},{10,11... | collective-permute-start | bytes 2359304 | tf_op jit(solution)/shard_map/ppermute | solution.py:298
  138.9 38.8 %collective-permute-start.12 = (bf16[512,768]{1,0:T(8,128)(2,1)}, bf16[512,768]{1,0:T(8,128)(2,1)S(1)}, u32[]{:S(2)}, u32[]{:S(2)}) collective-permute-start(bf16[512,768]{1,0:T(8,128)(2,1)} %collective-permute-done.11), channel_id=1, source_target_pairs={{0,1},{1,0},{2,3},{3,2},{4,5},{5,4},{6,7},{7,6},{8,9},{9,8},{10,11... | collective-permute-start | bytes 2359304 | tf_op jit(solution)/shard_map/ppermute | solution.py:298
  158.4 19.2 %collective-permute-start.6 = (bf16[512,768]{1,0:T(8,128)(2,1)S(1)}, bf16[512,768]{1,0:T(8,128)(2,1)S(1)}, u32[]{:S(2)}, u32[]{:S(2)}) collective-permute-start(bf16[512,768]{1,0:T(8,128)(2,1)S(1)} %get-tuple-element.62), channel_id=1, source_target_pairs={{0,2},{1,3},{2,0},{3,1},{4,6},{5,7},{6,4},{7,5},{8,10},{9,11},{10,... | collective-permute-start | bytes 2359304 | tf_op jit(solution)/shard_map/ppermute | solution.py:298
  159.5 18.2 %collective-permute-start.5 = (bf16[512,768]{1,0:T(8,128)(2,1)S(1)}, bf16[512,768]{1,0:T(8,128)(2,1)S(1)}, u32[]{:S(2)}, u32[]{:S(2)}) collective-permute-start(bf16[512,768]{1,0:T(8,128)(2,1)S(1)} %get-tuple-element.62), channel_id=1, source_target_pairs={{0,1},{1,0},{2,3},{3,2},{4,5},{5,4},{6,7},{7,6},{8,9},{9,8},{10,11... | collective-permute-start | bytes 2359304 | tf_op jit(solution)/shard_map/ppermute | solution.py:298
  177.6 2.3 collective-permute-start.7
  177.7 2.3 copy-start.10
  191.8 3.7 collective-permute-start.8
  195.1 3.5 collective-permute-start.13
  196.0 20.5 %collective-permute-start.9 = (bf16[512,768]{1,0:T(8,128)(2,1)S(1)}, bf16[512,768]{1,0:T(8,128)(2,1)S(1)}, u32[]{:S(2)}, u32[]{:S(2)}) collective-permute-start(bf16[512,768]{1,0:T(8,128)(2,1)S(1)} %fusion.27), channel_id=1, source_target_pairs={{0,2},{1,3},{2,0},{3,1},{4,6},{5,7},{6,4},{7,5},{8,10},{9,11},{10,... | collective-permute-start | bytes 2359304 | tf_op jit(solution)/shard_map/ppermute | solution.py:298
  199.1 33.4 %collective-permute-start.14 = (bf16[512,768]{1,0:T(8,128)(2,1)S(1)}, bf16[512,768]{1,0:T(8,128)(2,1)S(1)}, u32[]{:S(2)}, u32[]{:S(2)}) collective-permute-start(bf16[512,768]{1,0:T(8,128)(2,1)S(1)} %fusion.28), channel_id=1, source_target_pairs={{0,2},{1,3},{2,0},{3,1},{4,6},{5,7},{6,4},{7,5},{8,10},{9,11},{10,... | collective-permute-start | bytes 2359304 | tf_op jit(solution)/shard_map/ppermute | solution.py:298
  235.9 1.7 copy-start.5
  237.6 19.0 %collective-permute-start.16 = (bf16[512,768]{1,0:T(8,128)(2,1)}, bf16[512,768]{1,0:T(8,128)(2,1)S(1)}, u32[]{:S(2)}, u32[]{:S(2)}) collective-permute-start(bf16[512,768]{1,0:T(8,128)(2,1)} %get-tuple-element.57), channel_id=1, source_target_pairs={{0,2},{1,3},{2,0},{3,1},{4,6},{5,7},{6,4},{7,5},{8,10},{9,11},{10,... | collective-permute-start | bytes 2359304 | tf_op jit(solution)/shard_map/ppermute | solution.py:298
  239.5 17.1 %collective-permute-start.15 = (bf16[512,768]{1,0:T(8,128)(2,1)}, bf16[512,768]{1,0:T(8,128)(2,1)}, u32[]{:S(2)}, u32[]{:S(2)}) collective-permute-start(bf16[512,768]{1,0:T(8,128)(2,1)} %get-tuple-element.57), channel_id=1, source_target_pairs={{0,1},{1,0},{2,3},{3,2},{4,5},{5,4},{6,7},{7,6},{8,9},{9,8},{10,11... | collective-permute-start | bytes 2359304 | tf_op jit(solution)/shard_map/ppermute | solution.py:298
  243.3 132.4 %reduce-scatter.7.cloned.1.call-start = ((), (), s32[]{:S(2)}) async-start(), calls=%async_computation.3 | async-start | bytes 1327104
  256.6 3.0 collective-permute-start.17
  310.1 3.2 copy-start.8
  310.1 3.2 copy-start.9
  312.9 3.8 collective-permute-start.18
  319.0 1.7 copy-start.1
  321.6 56.4 %copy-start.12 = (bf16[2,96]{1,0:T(2,128)(2,1)S(1)}, bf16[2,96]{1,0:T(2,128)(2,1)}, u32[]{:S(2)}) copy-start(bf16[2,96]{1,0:T(2,128)(2,1)} %param.14) | copy-start | bytes 1156
  321.6 56.5 %collective-permute-start.19 = (bf16[512,768]{1,0:T(8,128)(2,1)}, bf16[512,768]{1,0:T(8,128)(2,1)S(1)}, u32[]{:S(2)}, u32[]{:S(2)}) collective-permute-start(bf16[512,768]{1,0:T(8,128)(2,1)} %fusion.29), channel_id=1, source_target_pairs={{0,2},{1,3},{2,0},{3,1},{4,6},{5,7},{6,4},{7,5},{8,10},{9,11},{10,... | collective-permute-start | bytes 2359304 | tf_op jit(solution)/shard_map/ppermute | solution.py:298
  376.8 3.4 copy-start.2
  378.0 3.7 collective-permute-start.20
  381.7 3.6 collective-permute-start.21
Sparse Core Ops, SparseCore 0:
  14.4 51.4 all-gather.1
  243.4 62.2 reduce-scatter.8
  315.1 60.5 reduce-scatter.6

commit v2 on v1

v2 whole, which is shorter than its diff:
```python
import functools

import jax
import jax.numpy as jnp
from jax import lax
from jax.experimental import pallas as pl
from jax.experimental.pallas import tpu as pltpu
from jax.sharding import PartitionSpec as P

HEAD_DIM = 64
HALF = HEAD_DIM // 2
WIDE = 128
TILE = 256
FAR = -1e30
VMEM_BYTES = 56 * 1024 * 1024
BF16 = jnp.bfloat16
F32 = jnp.float32

NN = (((1,), (0,)), ((), ()))
NT = (((1,), (1,)), ((), ()))
TN = (((0,), (0,)), ((), ()))


def mm(left, right, dims=NN):
    return lax.dot_general(left, right, dims, preferred_element_type=F32)


def positions(lengths, total):
    ends = jnp.cumsum(lengths)
    starts = ends - lengths
    index = jnp.arange(total, dtype=jnp.int32)
    segment = jnp.sum((index[:, None] >= ends[None, :]).astype(jnp.int32), axis=1)
    onehot = segment[:, None] == jnp.arange(lengths.shape[0], dtype=jnp.int32)[None, :]
    first = jnp.sum(jnp.where(onehot, starts[None, :], 0), axis=1)
    last = jnp.sum(jnp.where(onehot, ends[None, :], 0), axis=1)
    return (segment, index - first, first, last)


def rope_tables(place):
    freq = jnp.exp(
        -jnp.log(jnp.float32(160000.0)) * jnp.arange(HALF, dtype=F32) * (2.0 / HEAD_DIM)
    )
    angle = freq[:, None] * place.astype(F32)[None, :]
    return (jnp.cos(angle), jnp.sin(angle))


def pieces_of(row):
    high = row.astype(BF16).astype(F32)
    rest = row - high
    middle = rest.astype(BF16).astype(F32)
    return high, middle, rest - middle


def extend(body, rows):
    rest = WIDE - body.shape[0] - sum(row.shape[0] for row in rows)
    return jnp.concatenate([body, *rows, jnp.zeros((rest, body.shape[1]), F32)], axis=0)


def slot_of(at, me, split):
    return ((at // split) ^ me) * split + at % split


def tile(at):
    return pl.ds(pl.multiple_of(at * TILE, TILE), TILE)


def forward_kernel(blocks, low_ref, high_ref, me_ref, *refs):
    toks = refs[:4]
    seg_ref, cos_ref, sin_ref = refs[4:7]
    shards_in = refs[7 : 7 + blocks]
    normed_ref, query_ref, keys_ref, values_ref, ctx_ref, log_ref, wproj_ref = refs[
        7 + blocks : 14 + blocks
    ]
    nat_ref, flat_ref = refs[14 + blocks :]
    group = normed_ref.shape[0]
    heads = query_ref.shape[0]
    lanes = heads * HEAD_DIM
    parts = 8
    count = group // TILE
    split = count // 4
    slab = flat_ref.shape[0] // blocks
    me = me_ref[0]

    for index in range(blocks):
        place = pl.multiple_of((me_ref[1] ^ index) * slab, slab)
        flat_ref[pl.ds(place, slab), :] = shards_in[index][...]
    wproj_ref[...] = flat_ref[...].T
    gain = wproj_ref[3 * lanes : 3 * lanes + 16, :].astype(F32)[:1]

    for index in range(4):
        for part in range(split):
            slot = index * split + part
            here = slice(slot * TILE, (slot + 1) * TILE)
            there = tile(slot_of(slot, me, split))
            rows = toks[index][part * TILE : (part + 1) * TILE, :].astype(F32)
            center = rows - jnp.mean(rows, axis=-1, keepdims=True)
            spread = jnp.mean(center * center, axis=-1, keepdims=True)
            normed = (center * lax.rsqrt(spread + 1e-05) * gain).astype(BF16)
            normed_ref[here, :] = normed
            mixed = mm(wproj_ref[: 3 * lanes, :], normed, NT)
            cosine = cos_ref[:, there]
            sine = sin_ref[:, there]
            segment = seg_ref[:, there]
            same = (segment == lax.broadcasted_iota(jnp.int32, (parts, TILE), 0)).astype(F32)
            ones = jnp.ones((2 * parts, TILE), F32)

            def rotated(top):
                first = mixed[top : top + HALF]
                second = mixed[top + HALF : top + HEAD_DIM]
                return jnp.concatenate(
                    [first * cosine - second * sine, second * cosine + first * sine], axis=0
                )

            for head in range(heads):
                top = head * HEAD_DIM
                query = rotated(top) * (HEAD_DIM ** (-0.5))
                query_ref[head, :, here] = extend(query, [(1.0 - same) * FAR]).astype(BF16)
                key = extend(rotated(lanes + top), [same, ones[:parts]]).astype(BF16)
                keys_ref[head, :, here] = key[:HEAD_DIM]
                nat_ref[head, here, :] = key.T
                value = mixed[2 * lanes + top : 2 * lanes + top + HEAD_DIM]
                values_ref[head, :, here] = jnp.concatenate([value, ones], axis=0).astype(BF16)

    @pl.loop(0, count)
    def attend(step):
        here = tile(slot_of(step, me, split))

        def highest(at, tops):
            there = tile(slot_of(at, me, split))
            out = []
            for head in range(heads):
                scores = mm(nat_ref[head, there, :], query_ref[head, :, here])
                out.append(jnp.maximum(tops[head], jnp.max(scores, axis=0, keepdims=True)))
            return tuple(out)

        first = jnp.full((1, TILE), -jnp.inf, F32)
        tops = lax.fori_loop(low_ref[step], high_ref[step], highest, (first,) * heads)
        queries = []
        blank = jnp.zeros((parts - 3, TILE), F32)
        for head in range(heads):
            query = query_ref[head, : HEAD_DIM + parts, here].astype(F32)
            queries.append(extend(query, [*pieces_of(-tops[head]), blank]).astype(BF16))

        def inner(at, accs):
            there = tile(slot_of(at, me, split))
            out = []
            for head in range(heads):
                expo = jnp.exp(mm(nat_ref[head, there, :], queries[head]))
                out.append(accs[head] + mm(values_ref[head, :, there], expo.astype(BF16)))
            return tuple(out)

        zero = jnp.zeros((HEAD_DIM + 2 * parts, TILE), F32)
        accs = lax.fori_loop(low_ref[step], high_ref[step], inner, (zero,) * heads)
        totals = [acc[HEAD_DIM : HEAD_DIM + 1] for acc in accs]
        ctx = [acc[:HEAD_DIM] / total for acc, total in zip(accs, totals)]
        ctx_ref[:, here] = jnp.concatenate(ctx, axis=0).astype(BF16)
        logs = [top + jnp.log(total) for top, total in zip(tops, totals)]
        log_ref[:, here] = jnp.concatenate(
            logs + [jnp.zeros((8 - heads, TILE), F32)], axis=0
        )


def backward_kernel(blocks, low_ref, high_ref, me_ref, *refs):
    dattn = refs[:4]
    (
        normed_ref, query_ref, keys_ref, values_ref, ctx_ref, log_ref, wproj_ref,
        seg_ref, cos_ref, sin_ref, wback_ref, dnormed_ref,
    ) = refs[4:16]
    grads = refs[16 : 16 + blocks]
    (
        qx_ref, kx_ref, vx_ref, dx_ref, dq_ref, dmix_ref, all_ref, tall_ref, flat_ref,
    ) = refs[16 + blocks :]
    group = normed_ref.shape[0]
    lanes = wback_ref.shape[0]
    heads = lanes // HEAD_DIM
    parts = 8
    count = group // TILE
    split = count // 4
    slab = flat_ref.shape[0] // blocks
    me = me_ref[0]
    scale = HEAD_DIM ** (-0.5)

    for index in range(4):
        for part in range(split):
            slot = index * split + part
            here = slice(slot * TILE, (slot + 1) * TILE)
            there = tile(slot_of(slot, me, split))
            piece = dattn[index][part * TILE : (part + 1) * TILE, :]
            all_ref[here, :] = piece
            d_ctx = mm(wback_ref[...], piece, NT).astype(BF16).astype(F32)
            ctx = ctx_ref[:, here].astype(F32)
            segment = seg_ref[:, there]
            same = (segment == lax.broadcasted_iota(jnp.int32, (parts, TILE), 0)).astype(F32)
            ones = jnp.ones((parts, TILE), F32)
            blank = jnp.zeros((parts - 3, TILE), F32)
            logs = log_ref[:, here]
            for head in range(heads):
                rows = slice(head * HEAD_DIM, (head + 1) * HEAD_DIM)
                delta = -jnp.sum(d_ctx[rows] * ctx[rows], axis=0, keepdims=True)
                dx_ref[head, :, here] = extend(
                    d_ctx[rows], [*pieces_of(delta), blank]
                ).astype(BF16)
                log = -logs[head : head + 1]
                query = query_ref[head, : HEAD_DIM + parts, here].astype(F32)
                qx_ref[head, :, here] = extend(query, [*pieces_of(log), blank]).astype(BF16)
                key = keys_ref[head, :, here].astype(F32)
                kx_ref[head, here, :] = extend(key, [same, ones]).astype(BF16).T
                value = values_ref[head, :HEAD_DIM, here].astype(F32)
                vx_ref[head, here, :] = extend(value, [ones]).astype(BF16).T
                dq_ref[head, :, here] = jnp.zeros((HEAD_DIM, TILE), F32)

    def turned_back(grad, where):
        cosine = cos_ref[:, where]
        sine = sin_ref[:, where]
        first = grad[:HALF]
        second = grad[HALF:]
        return jnp.concatenate(
            [first * cosine + second * sine, second * cosine - first * sine], axis=0
        ).astype(BF16)

    @pl.loop(0, count)
    def attend(step):
        here = tile(slot_of(step, me, split))

        def inner(at, carry):
            there = tile(slot_of(at, me, split))
            out = []
            for head in range(heads):
                d_key, d_value = carry[head]
                query = qx_ref[head, :, there]
                d_out = dx_ref[head, :, there]
                probs = jnp.exp(mm(kx_ref[head, here, :], query))
                d_probs = mm(vx_ref[head, here, :], d_out)
                d_scores = (probs * d_probs).astype(BF16)
                d_value = d_value + mm(d_out[:HEAD_DIM], probs.astype(BF16), NT)
                d_key = d_key + mm(query[:HEAD_DIM], d_scores, NT)
                dq_ref[head, :, there] += mm(keys_ref[head, :, here], d_scores)
                out.append((d_key, d_value))
            return tuple(out)

        zero = jnp.zeros((HEAD_DIM, TILE), F32)
        done = lax.fori_loop(low_ref[step], high_ref[step], inner, ((zero, zero),) * heads)
        for head in range(heads):
            top = head * HEAD_DIM
            d_key, d_value = done[head]
            turned = turned_back(d_key, tile(step))
            dmix_ref[lanes + top : lanes + top + HEAD_DIM, here] = turned
            dmix_ref[2 * lanes + top : 2 * lanes + top + HEAD_DIM, here] = d_value.astype(BF16)

    for slot in range(count):
        here = slice(slot * TILE, (slot + 1) * TILE)
        there = tile(slot_of(slot, me, split))
        for head in range(heads):
            top = head * HEAD_DIM
            turned = turned_back(dq_ref[head, :, here] * scale, there)
            dmix_ref[top : top + HEAD_DIM, here] = turned
        d_normed = mm(dmix_ref[:, here].T, wproj_ref[: 3 * lanes, :])
        dnormed_ref[here, :] = d_normed.astype(BF16)

    for step in range(3):
        rows = slice(step * lanes, (step + 1) * lanes)
        tall_ref[rows, :] = mm(dmix_ref[rows, :], normed_ref[...]).astype(BF16)
    tall_ref[3 * lanes :, :] = mm(ctx_ref[...], all_ref[...]).astype(BF16)
    flat_ref[...] = tall_ref[...].T
    for index in range(blocks):
        place = pl.multiple_of((me_ref[1] ^ index) * slab, slab)
        grads[index][...] = flat_ref[pl.ds(place, slab), :]


def vmem_spec():
    return pl.BlockSpec(memory_space=pltpu.VMEM)


def smem_spec():
    return pl.BlockSpec(memory_space=pltpu.SMEM)


def attention_forward(low, high, me, toks, seg, cosine, sine, shards_in, lanes):
    rows, model = toks[0].shape
    group = 4 * rows
    heads = lanes // HEAD_DIM
    blocks = len(shards_in)
    width = shards_in[0].shape[1]
    shape = jax.ShapeDtypeStruct
    return pl.pallas_call(
        functools.partial(forward_kernel, blocks),
        out_shape=(
            shape((group, model), BF16),
            shape((heads, WIDE, group), BF16),
            shape((heads, HEAD_DIM, group), BF16),
            shape((heads, HEAD_DIM + 16, group), BF16),
            shape((lanes, group), BF16),
            shape((8, group), F32),
            shape((width, model), BF16),
        ),
        in_specs=[smem_spec()] * 3 + [vmem_spec()] * (7 + blocks),
        out_specs=[vmem_spec()] * 7,
        scratch_shapes=[
            pltpu.VMEM((heads, group, WIDE), BF16),
            pltpu.VMEM((model, width), BF16),
        ],
        compiler_params=pltpu.CompilerParams(vmem_limit_bytes=VMEM_BYTES),
        cost_estimate=pl.CostEstimate(
            flops=2 * group * model * lanes * 4 + 2 * group * group * lanes,
            bytes_accessed=group * model * 8,
            transcendentals=group * group,
        ),
        name="attention_forward",
    )(low, high, me, *toks, seg, cosine, sine, *shards_in)


def attention_backward(blocks, low, high, me, d_attn, kept, seg, cosine, sine, wback):
    rows, model = d_attn[0].shape
    group = 4 * rows
    lanes = wback.shape[0]
    heads = lanes // HEAD_DIM
    shape = jax.ShapeDtypeStruct
    return pl.pallas_call(
        functools.partial(backward_kernel, blocks),
        out_shape=(
            shape((group, model), BF16),
            *[shape((model // blocks, 4 * lanes), BF16) for _ in range(blocks)],
        ),
        in_specs=[smem_spec()] * 3 + [vmem_spec()] * 15,
        out_specs=[vmem_spec()] * (1 + blocks),
        scratch_shapes=[
            pltpu.VMEM((heads, WIDE, group), BF16),
            pltpu.VMEM((heads, group, WIDE), BF16),
            pltpu.VMEM((heads, group, WIDE), BF16),
            pltpu.VMEM((heads, WIDE, group), BF16),
            pltpu.VMEM((heads, HEAD_DIM, group), F32),
            pltpu.VMEM((3 * lanes, group), BF16),
            pltpu.VMEM((group, model), BF16),
            pltpu.VMEM((4 * lanes, model), BF16),
            pltpu.VMEM((model, 4 * lanes), BF16),
        ],
        compiler_params=pltpu.CompilerParams(vmem_limit_bytes=VMEM_BYTES),
        cost_estimate=pl.CostEstimate(
            flops=2 * group * model * lanes * 8 + 4 * group * group * lanes,
            bytes_accessed=group * model * 12,
            transcendentals=group * group,
        ),
        name="attention_backward",
    )(low, high, me, *d_attn, *kept, seg, cosine, sine, wback)


def swap(value, axis, bit):
    size = lax.axis_size(axis)
    return lax.ppermute(value, axis, [(i, i ^ bit) for i in range(size)])


def gather_rows(rows):
    far = swap(rows, "tp", 2)
    return (rows, swap(rows, "tp", 1), far, swap(far, "tp", 1))


def scatter_rows(partial):
    rows = partial.shape[0] // 4
    own, near, far, corner = (partial[k * rows : (k + 1) * rows] for k in range(4))
    far_sum = far.astype(F32) + swap(corner, "tp", 1).astype(F32)
    came = swap(far_sum.astype(BF16), "tp", 2)
    mine = own.astype(F32) + swap(near, "tp", 1).astype(F32)
    return mine + came.astype(F32)


def pair_rows(rows):
    return jnp.concatenate([rows, swap(rows, "tp", 1)], axis=0)


def scatter_pair(partial):
    rows = partial.shape[0] // 2
    came = swap(partial[rows:].astype(BF16), "tp", 1)
    return partial[:rows] + came.astype(F32)


def swaps_over(axis):
    size = lax.axis_size(axis)
    return size <= 8 and size & (size - 1) == 0


def center_rows(values):
    center = values - jnp.mean(values, axis=-1, keepdims=True)
    spread = jnp.mean(center * center, axis=-1, keepdims=True)
    inverse = lax.rsqrt(spread + 1e-05)
    return center * inverse, inverse


def norm_pull(normal, inverse, gain, grad):
    scaled = grad * gain
    mean = jnp.mean(scaled, axis=-1, keepdims=True)
    along = jnp.mean(scaled * normal, axis=-1, keepdims=True)
    return (scaled - mean - normal * along) * inverse


def geglu(up_in, gate_in):
    return jax.nn.gelu(up_in, approximate=False) * gate_in


def shards(tokens, seq_lengths, w_qkv, w_out, w_in, w_down, gains, cotangent):
    rows, model = tokens.shape
    slab = w_qkv.shape[1]
    lanes = w_qkv.shape[2]
    units = w_in.shape[2]
    group = rows * lax.axis_size("tp")
    ring = lax.axis_size("fsdp")
    direct = swaps_over("fsdp")

    own_proj = jnp.transpose(w_qkv, (1, 0, 2)).reshape(slab, 3 * lanes)
    spare = -(3 * lanes + gains.shape[0]) % WIDE
    first = jnp.concatenate([own_proj, gains.T, jnp.zeros((slab, spare), BF16)], axis=1)
    if direct:
        first_parts = [first] + [swap(first, "fsdp", k) for k in range(1, ring)]
        spot = lax.axis_index("fsdp")
    else:
        first_parts = [lax.all_gather(first, "fsdp", axis=0, tiled=True)]
        spot = jnp.int32(0)
    mine = jnp.concatenate([w_in[0], w_in[1], w_down.T], axis=1)
    other = swap(mine, "tp", 2)
    cut = (slice(0, units), slice(units, 2 * units), slice(2 * units, 3 * units))
    rest = jnp.concatenate(
        [part[:, where] for where in cut for part in (mine, other)] + [w_out.T], axis=1
    )
    whole_rest = lax.all_gather(rest, "fsdp", axis=0, tiled=True)
    pair_cat = whole_rest[:, : 4 * units]
    last_t = whole_rest[:, 4 * units : 6 * units]
    back_t = whole_rest[:, 6 * units :]

    segment, place, seq_first, seq_last = positions(seq_lengths[0], group)
    cosine, sine = rope_tables(place)
    low = seq_first[::TILE] // TILE
    high = (seq_last[TILE - 1 :: TILE] + TILE - 1) // TILE
    seg = segment[None, :]
    me = jnp.stack([lax.axis_index("tp"), spot]).astype(jnp.int32)

    toks = gather_rows(tokens)
    cots = pair_rows(cotangent)
    normed1, query, keys, values, ctx, logs, proj_t = attention_forward(
        low, high, me, toks, seg, cosine, sine, first_parts, lanes
    )
    gain_one = proj_t[3 * lanes : 3 * lanes + 1].astype(F32)
    gain_two = proj_t[3 * lanes + 1 : 3 * lanes + 2].astype(F32)
    inputs = tokens.astype(F32)
    attn_part = lax.dot_general(
        ctx, back_t, (((0,), (1,)), ((), ())), preferred_element_type=F32
    ).astype(BF16)
    h_mid = inputs + scatter_rows(attn_part)
    normal2, inverse2 = center_rows(h_mid)
    full2 = pair_rows((normal2 * gain_two).astype(BF16))
    both = mm(full2, pair_cat)
    up_in = both[:, : 2 * units]
    gate_in = both[:, 2 * units :]
    hidden = geglu(up_in, gate_in).astype(BF16)
    d_hid = mm(cots, last_t)
    _, geglu_pull = jax.vjp(geglu, up_in, gate_in)
    d_up, d_gate = geglu_pull(d_hid)
    d_both = jnp.concatenate([d_up, d_gate], axis=1).astype(BF16)
    d_normed2 = scatter_pair(mm(d_both, pair_cat, NT))
    d_mid = cotangent.astype(F32) + norm_pull(normal2, inverse2, gain_two, d_normed2)
    d_attn = gather_rows(d_mid.astype(BF16))

    output = (h_mid + scatter_pair(mm(hidden, last_t, NT))).astype(BF16)
    early = jnp.concatenate(
        [mm(full2, d_both, TN).astype(BF16), mm(cots, hidden, TN).astype(BF16)], axis=1
    )
    sum_early = lax.psum_scatter(early, "fsdp", scatter_dimension=0, tiled=True)
    halves = [
        jnp.concatenate(
            [sum_early[:, (2 * k + side) * units : (2 * k + side + 1) * units] for k in range(3)],
            axis=1,
        )
        for side in range(2)
    ]
    own_early = halves[0].astype(F32) + swap(halves[1], "tp", 2).astype(F32)

    d_part, *late = attention_backward(
        len(first_parts), low, high, me, d_attn,
        (normed1, query, keys, values, ctx, logs, proj_t), seg, cosine, sine, back_t.T,
    )
    if direct:
        own_late = late[0].astype(F32)
        for k in range(1, ring):
            own_late = own_late + swap(late[k], "fsdp", k).astype(F32)
    else:
        own_late = lax.psum_scatter(late[0], "fsdp", scatter_dimension=0, tiled=True).astype(F32)
    d_normed1 = scatter_rows(d_part)
    normal1, inverse1 = center_rows(inputs)
    grad_tokens = (d_mid + norm_pull(normal1, inverse1, gain_one, d_normed1)).astype(BF16)

    sum_proj = own_late[:, : 3 * lanes]
    terms = jnp.stack(
        [
            jnp.sum(sum_proj * own_proj.astype(F32), axis=1),
            jnp.sum(own_early[:, : 2 * units] * mine[:, : 2 * units].astype(F32), axis=1),
        ]
    ) / gains.astype(F32)
    grad_gains = terms + swap(terms, "tp", 1) + swap(terms, "tp", 2) + swap(terms, "tp", 3)
    grad_qkv = jnp.transpose(sum_proj.reshape(slab, 3, lanes), (1, 0, 2))
    grad_in = jnp.stack([own_early[:, :units], own_early[:, units : 2 * units]])
    grad_out = own_late[:, 3 * lanes :].T
    grad_down = own_early[:, 2 * units :].T
    return (output, grad_tokens, grad_qkv, grad_out, grad_in, grad_down, grad_gains)


def solution(mesh):
    rows = P(("fsdp", "tp"), None)
    weights = (P(None, "fsdp", "tp"), P("tp", "fsdp"), P(None, "fsdp", "tp"), P("tp", "fsdp"))
    gains = P(None, "fsdp")
    return jax.shard_map(
        shards,
        mesh=mesh,
        in_specs=(rows, P("fsdp", None), *weights, gains, rows),
        out_specs=(rows, rows, *weights, gains),
        check_vma=False,
    )
```

time: 394 us -> 322 us (0.82)
  the two profiles are of different devices: /device:TPU:0 before, /device:TPU:3 now
where the time goes in v2:
time: 322 us; the launch traced here: 318 us
  Pallas kernels  88.2 us (27%)
  waiting for transfers between devices  83.3 us (26%)
  starting transfers between devices  62.9 us (20%)
  other arithmetic  24.2 us (8%)
  local copies, waits for them, and re-layouts  23.4 us (7%)
  matrix products  20.9 us (6%)
  between operations  15.2 us (5%)
    ppermute x35, waiting for transfers between devices, swap(): return lax.ppermute(value, axis, [(i, i ^ bit) for i in range(size)])  83.2 us
    ppermute x35, starting transfers between devices, swap(): return lax.ppermute(value, axis, [(i, i ^ bit) for i in range(size)])  62.8 us
    pallas_call x1, Pallas kernels, attention_backward(): pl.pallas_call(functools.partial(backward_kernel, blocks), out_shape=(sha...  44.2 us
    pallas_call x1, Pallas kernels, attention_forward(): pl.pallas_call(functools.partial(forward_kernel, blocks), out_shape=(shap...  44 us
    dot_general x6, matrix products, mm(): return lax.dot_general(left, right, dims, preferred_element_type=F32)  18.4 us
    unnamed x81, local copies, waits for them, and re-layouts  11.5 us
  transfers between devices with their start and end apart: 37, of which 13 were waited for; matrix products, arithmetic and copies ran while one was open for 13% of the time, Pallas kernels for 28%

profile of v2, /device:TPU:3, one launch (start us, length us, event | category | flops | bytes accessed | tf_op | source)
XLA Modules:
  0.0 318.2 jit_solution(7419226243195116249)
XLA Ops:
  9.4 1.3 collective-permute-start.10
  11.6 3.1 collective-permute-done.10
  19.3 2.3 collective-permute-start.6
  21.6 1.2 collective-permute-start.1
  23.3 3.0 collective-permute-start
  26.3 11.8 %collective-permute-done.1.refs_2_ = bf16[512,768]{1,0:T(8,128)(2,1)S(1)} collective-permute-done((bf16[512,768]{1,0:T(8,128)(2,1)S(1)}, bf16[512,768]{1,0:T(8,128)(2,1)S(1)}, u32[]{:S(2)}, u32[]{:S(2)}) %collective-permute-start.1) | collective-permute-done | bytes 786464 | tf_op jit(solution)/shard_map/ppermute | solution.py:349
  38.1 3.5 %collective-permute-start.2 = (bf16[512,768]{1,0:T(8,128)(2,1)S(1)}, bf16[512,768]{1,0:T(8,128)(2,1)}, u32[]{:S(2)}, u32[]{:S(2)}) collective-permute-start(bf16[512,768]{1,0:T(8,128)(2,1)S(1)} %collective-permute-done.1.refs_2_), channel_id=1, source_target_pairs={{0,1},{1,0},{2,3},{3,2},{4,5},{5,4},{6,7},{7,6},{8,9},{9,8},{10,11... | collective-permute-start | bytes 2359304 | tf_op jit(solution)/shard_map/ppermute | solution.py:349
  41.5 1.8 multiply_sine_fusion
  43.7 3.2 %collective-permute-start.8 = (bf16[96,640]{1,0:T(8,128)(2,1)S(1)}, bf16[96,640]{1,0:T(8,128)(2,1)}, u32[]{:S(2)}, u32[]{:S(2)}) collective-permute-start(bf16[96,640]{1,0:T(8,128)(2,1)S(1)} %maximum_maximum_fusion.refs_7_), channel_id=1, source_target_pairs={{0,24},{4,28},{8,16},{12,20},{16,8},{20,12},{24,0},{28,4},{1,25},{... | collective-permute-start | bytes 368648 | tf_op jit(solution)/shard_map/ppermute | solution.py:349
  49.1 12.7 %collective-permute-done.7.refs_12_ = bf16[96,640]{1,0:T(8,128)(2,1)S(1)} collective-permute-done((bf16[96,640]{1,0:T(8,128)(2,1)S(1)}, bf16[96,640]{1,0:T(8,128)(2,1)S(1)}, u32[]{:S(2)}, u32[]{:S(2)}) %collective-permute-start.7) | collective-permute-done | bytes 122912 | tf_op jit(solution)/shard_map/ppermute | solution.py:349
  62.8 44.0 %attention_forward.1 = (bf16[2048,768]{1,0:T(8,128)(2,1)}, bf16[3,128,2048]{2,1,0:T(8,128)(2,1)}, bf16[3,64,2048]{2,1,0:T(8,128)(2,1)}, bf16[3,80,2048]{2,1,0:T(...) custom-call(s32[8]{0:T(128)} %get-tuple-element.116.low_ref, ...), custom_call_target="tpu_custom_call" | custom-call | flops 4026531840 | bytes 12582912 | tf_op jit(solution)/shard_map/attention_forward/pallas_call | solution.py:285
  106.9 2.5 convolution_convert_fusion.1
  109.5 3.3 %collective-permute-start.12 = (bf16[512,768]{1,0:T(8,128)(2,1)S(1)}, bf16[512,768]{1,0:T(8,128)(2,1)S(1)}, u32[]{:S(2)}, u32[]{:S(2)}) collective-permute-start(bf16[512,768]{1,0:T(8,128)(2,1)S(1)} %get-tuple-element.93), channel_id=1, source_target_pairs={{0,1},{1,0},{2,3},{3,2},{4,5},{5,4},{6,7},{7,6},{8,9},{9,8},{10,11... | collective-permute-start | bytes 2359304 | tf_op jit(solution)/shard_map/ppermute | solution.py:349
  112.9 1.8 collective-permute-done.12
  115.0 1.3 collective-permute-start.13
  118.0 15.8 %collective-permute-done.13 = bf16[512,768]{1,0:T(8,128)(2,1)S(1)} collective-permute-done((bf16[512,768]{1,0:T(8,128)(2,1)S(1)}, bf16[512,768]{1,0:T(8,128)(2,1)S(1)}, u32[]{:S(2)}, u32[]{:S(2)}) %collective-permute-start.13) | collective-permute-done | bytes 786464 | tf_op jit(solution)/shard_map/ppermute | solution.py:349
  135.2 1.3 collective-permute-start.14
  136.6 1.8 collective-permute-done.14
  138.4 2.2 fusion.22
  140.6 7.0 %add_convert_fusion = (bf16[1024,576]{1,0:T(8,128)(2,1)S(1)}, f32[1024,576]{1,0:T(8,128)S(1)}, f32[1024,576]{1,0:T(8,128)S(1)}) fusion(f32[1024,1152]{1,0:T(8,128)S(1)} %fusion.22, bf16[1024,768]{1,0:T(8,128)(2,1)S(1)} %constant_dynamic-update-slice_fusion, bf16[768,1920]{1,0:T(8,128)(2,1)S(1)} %copy-done.13), kind=kOutput, calls=%fused_computation.6 | convolution fusion | flops 949026816 | bytes 13697024 | tf_op jit(solution)/shard_map/dot_general | solution.py:25
  148.4 2.3 fusion.20
  152.1 1.4 fusion.26
  155.6 2.1 convolution_convert_fusion.2
  157.7 3.5 %convolution_convert_fusion = bf16[768,1152]{1,0:T(8,128)(2,1)} fusion(bf16[1024,576]{1,0:T(8,128)(2,1)S(1)} %get-tuple-element.88, bf16[1024,576]{1,0:T(8,128)(2,1)S(1)} %get-tuple-element.84, bf16[512,768]{1,0:T(8,128)(2,1)S(1)} %collective-permute-done.14, bf16[512,768]{1,0:T(8,128)(2,1)S(1)} %multiply_convert_fusion.2), kind=kOutput, calls=%fused_computation.1 | convolution fusion | flops 1820688384 | bytes 5701632 | tf_op jit(solution)/shard_map/dot_general | solution.py:25
  161.2 1.5 copy.104
  162.8 2.4 fusion.29
  165.5 3.7 %fusion.36 = (bf16[512,768]{1,0:T(8,128)(2,1)}, f32[512,768]{1,0:T(8,128)}, bf16[512,768]{1,0:T(8,128)(2,1)}) fusion(f32[512]{0:T(512)S(1)} %broadcast_multiply_fusion.3, f32[512]{0:T(512)S(1)} %add_rsqrt_fusion.1, f32[512,768]{1,0:T(8,128)S(1)} %get-tuple-element.87, f32[512]{0:T(512)S(1)} %broadcast_multiply_fusion.5, ...), kind=kLoop, calls=%fused_computation.117 | loop fusion | flops 6291456 | bytes 10234880 | tf_op jit(solution)/shard_map/convert_element_type | solution.py:459
  169.3 1.2 collective-permute-start.19
  170.5 1.8 pad_maximum_fusion
  173.1 15.1 %collective-permute-done.19.refs_2_ = bf16[512,768]{1,0:T(8,128)(2,1)S(1)} collective-permute-done((bf16[512,768]{1,0:T(8,128)(2,1)}, bf16[512,768]{1,0:T(8,128)(2,1)S(1)}, u32[]{:S(2)}, u32[]{:S(2)}) %collective-permute-start.19) | collective-permute-done | bytes 786464 | tf_op jit(solution)/shard_map/ppermute | solution.py:349
  188.2 1.2 collective-permute-start.20
  192.4 44.2 %attention_backward.1 = (bf16[2048,768]{1,0:T(8,128)(2,1)}, bf16[96,768]{1,0:T(8,128)(2,1)}, bf16[96,768]{1,0:T(8,128)(2,1)}, bf16[96,768]{1,0:T(8,128)(2,1)}, b...) custom-call(s32[8]{0:T(128)} %get-tuple-element.116.low_ref, ...), custom_call_target="tpu_custom_call" | custom-call | flops 8053063680 | bytes 18874368 | tf_op jit(solution)/shard_map/attention_backward/pallas_call | solution.py:318
  236.7 2.5 fusion.39
  239.4 4.0 %collective-permute-start.24 = (bf16[96,768]{1,0:T(8,128)(2,1)S(1)}, bf16[96,768]{1,0:T(8,128)(2,1)S(1)}, u32[]{:S(2)}, u32[]{:S(2)}) collective-permute-start(bf16[96,768]{1,0:T(8,128)(2,1)S(1)} %copy-done.29), channel_id=1, source_target_pairs={{0,4},{4,0},{8,12},{12,8},{16,20},{20,16},{24,28},{28,24},{1,5},{5... | collective-permute-start | bytes 442376 | tf_op jit(solution)/shard_map/ppermute | solution.py:349
  243.5 14.3 %collective-permute-start.25 = (bf16[96,768]{1,0:T(8,128)(2,1)S(1)}, bf16[96,768]{1,0:T(8,128)(2,1)S(1)}, u32[]{:S(2)}, u32[]{:S(2)}) collective-permute-start(bf16[96,768]{1,0:T(8,128)(2,1)S(1)} %copy-done.28), channel_id=1, source_target_pairs={{0,8},{4,12},{8,0},{12,4},{16,24},{20,28},{24,16},{28,20},{1,9},{5... | collective-permute-start | bytes 442376 | tf_op jit(solution)/shard_map/ppermute | solution.py:349
  259.0 2.4 collective-permute-start.28
  261.3 2.2 add_convert_fusion.1
  264.7 3.0 collective-permute-start.30
  269.9 7.4 %collective-permute-done.27 = bf16[96,768]{1,0:T(8,128)(2,1)S(1)} collective-permute-done((bf16[96,768]{1,0:T(8,128)(2,1)S(1)}, bf16[96,768]{1,0:T(8,128)(2,1)S(1)}, u32[]{:S(2)}, u32[]{:S(2)}) %collective-permute-start.27) | collective-permute-done | bytes 147488 | tf_op jit(solution)/shard_map/ppermute | solution.py:349
  277.3 3.1 collective-permute-done.28
  281.6 2.0 copy.113
  284.3 1.6 copy.114
  285.9 8.0 %collective-permute-done.23 = bf16[512,768]{1,0:T(8,128)(2,1)} collective-permute-done((bf16[512,768]{1,0:T(8,128)(2,1)}, bf16[512,768]{1,0:T(8,128)(2,1)}, u32[]{:S(2)}, u32[]{:S(2)}) %collective-permute-start.23) | collective-permute-done | bytes 786464 | tf_op jit(solution)/shard_map/ppermute | solution.py:349
  293.9 2.1 fusion.30
  296.0 1.3 fusion.41
  297.5 3.0 fusion.15
  302.1 4.9 %collective-permute-start.32 = (f32[2,96]{1,0:T(2,128)S(1)}, f32[2,96]{1,0:T(2,128)S(1)}, u32[]{:S(2)}, u32[]{:S(2)}) collective-permute-start(f32[2,96]{1,0:T(2,128)S(1)} %maximum_divide_fusion), channel_id=1, source_target_pairs={{0,1},{1,0},{2,3},{3,2},{4,5},{5,4},{6,7},{7,6},{8,9},{9,8},{10,11... | collective-permute-start | bytes 2312 | tf_op jit(solution)/shard_map/ppermute | solution.py:349
  307.0 1.7 collective-permute-start.34
  (177 shorter events, 34.1 us)
Async XLA Ops:
  7.2 99.7 %all-gather.2.cloned.1.call-start = ((), (), s32[]{:S(2)}) async-start(), calls=%async_computation.1 | async-start | bytes 3317760 | tf_op jit(solution)/shard_map/all_gather | solution.py:423
  8.3 98.6 %copy-start.9 = (bf16[96,288]{1,0:T(8,128)(2,1)}, bf16[96,288]{1,0:T(8,128)(2,1)S(1)}, u32[]{:S(2)}) copy-start(bf16[96,288]{1,0:T(8,128)(2,1)S(1)} %get-tuple-element.111) | copy-start | bytes 165892
  9.4 5.3 %collective-permute-start.10 = (bf16[96,864]{1,0:T(8,128)(2,1)S(1)}, bf16[96,864]{1,0:T(8,128)(2,1)S(1)}, u32[]{:S(2)}, u32[]{:S(2)}) collective-permute-start(bf16[96,864]{1,0:T(8,128)(2,1)S(1)} %pad_maximum_fusion.8), channel_id=1, source_target_pairs={{0,2},{1,3},{2,0},{3,1},{4,6},{5,7},{6,4},{7,5},{8,10},{9,11},{10,... | collective-permute-start | bytes 497672 | tf_op jit(solution)/shard_map/ppermute | solution.py:349
  15.9 280.2 %reduce-scatter.4.cloned.1.call-start = ((), (), s32[]{:S(2)}) async-start(), calls=%async_computation.2 | async-start | bytes 3096576 | tf_op jit(solution)/shard_map/reduce_scatter | solution.py:465
  16.2 90.6 %copy-start.11 = (bf16[96,576]{1,0:T(8,128)(2,1)}, bf16[96,576]{1,0:T(8,128)(2,1)S(1)}, u32[]{:S(2)}) copy-start(bf16[96,576]{1,0:T(8,128)(2,1)S(1)} %copy.94) | copy-start | bytes 331780
  16.5 45.4 %copy-start.16 = (bf16[96,640]{1,0:T(8,128)(2,1)}, bf16[96,640]{1,0:T(8,128)(2,1)S(1)}, u32[]{:S(2)}) copy-start(bf16[96,640]{1,0:T(8,128)(2,1)S(1)} %maximum_maximum_fusion.refs_7_) | copy-start | bytes 368644
  16.6 6.7 %collective-permute-start.3 = (bf16[96,640]{1,0:T(8,128)(2,1)S(1)}, bf16[96,640]{1,0:T(8,128)(2,1)S(1)}, u32[]{:S(2)}, u32[]{:S(2)}) collective-permute-start(bf16[96,640]{1,0:T(8,128)(2,1)S(1)} %maximum_maximum_fusion.refs_7_), channel_id=1, source_target_pairs={{0,4},{4,0},{8,12},{12,8},{16,20},{20,16},{24,28},{28,24},{1,5},{5... | collective-permute-start | bytes 368648 | tf_op jit(solution)/shard_map/ppermute | solution.py:349
  17.0 26.5 %collective-permute-start.4 = (bf16[96,640]{1,0:T(8,128)(2,1)S(1)}, bf16[96,640]{1,0:T(8,128)(2,1)S(1)}, u32[]{:S(2)}, u32[]{:S(2)}) collective-permute-start(bf16[96,640]{1,0:T(8,128)(2,1)S(1)} %maximum_maximum_fusion.refs_7_), channel_id=1, source_target_pairs={{0,8},{4,12},{8,0},{12,4},{16,24},{20,28},{24,16},{28,20},{1,9},{5... | collective-permute-start | bytes 368648 | tf_op jit(solution)/shard_map/ppermute | solution.py:349
  18.2 25.5 %collective-permute-start.5 = (bf16[96,640]{1,0:T(8,128)(2,1)S(1)}, bf16[96,640]{1,0:T(8,128)(2,1)S(1)}, u32[]{:S(2)}, u32[]{:S(2)}) collective-permute-start(bf16[96,640]{1,0:T(8,128)(2,1)S(1)} %maximum_maximum_fusion.refs_7_), channel_id=1, source_target_pairs={{0,12},{4,8},{8,4},{12,0},{16,28},{20,24},{24,20},{28,16},{1,13},{... | collective-permute-start | bytes 368648 | tf_op jit(solution)/shard_map/ppermute | solution.py:349
  19.3 27.7 %collective-permute-start.6 = (bf16[96,640]{1,0:T(8,128)(2,1)S(1)}, bf16[96,640]{1,0:T(8,128)(2,1)S(1)}, u32[]{:S(2)}, u32[]{:S(2)}) collective-permute-start(bf16[96,640]{1,0:T(8,128)(2,1)S(1)} %maximum_maximum_fusion.refs_7_), channel_id=1, source_target_pairs={{0,16},{4,20},{8,24},{12,28},{16,0},{20,4},{24,8},{28,12},{1,17},{... | collective-permute-start | bytes 368648 | tf_op jit(solution)/shard_map/ppermute | solution.py:349
  21.6 16.5 %collective-permute-start.1 = (bf16[512,768]{1,0:T(8,128)(2,1)S(1)}, bf16[512,768]{1,0:T(8,128)(2,1)S(1)}, u32[]{:S(2)}, u32[]{:S(2)}) collective-permute-start(bf16[512,768]{1,0:T(8,128)(2,1)S(1)} %copy-done), channel_id=1, source_target_pairs={{0,2},{1,3},{2,0},{3,1},{4,6},{5,7},{6,4},{7,5},{8,10},{9,11},{10,... | collective-permute-start | bytes 2359304 | tf_op jit(solution)/shard_map/ppermute | solution.py:349
  23.1 38.9 %copy-start.17 = (s32[2048]{0:T(1024)}, s32[2048]{0:T(1024)S(1)}, u32[]{:S(2)}) copy-start(s32[2048]{0:T(1024)S(1)} %convert_reduce_fusion.1) | copy-start | bytes 24580
  23.3 38.7 %copy-start.30 = (bf16[96,640]{1,0:T(8,128)(2,1)}, bf16[96,640]{1,0:T(8,128)(2,1)S(1)}, u32[]{:S(2)}) copy-start(bf16[96,640]{1,0:T(8,128)(2,1)S(1)} %collective-permute-done.3.refs_8_) | copy-start | bytes 368644
  23.3 38.7 %collective-permute-start = (bf16[512,768]{1,0:T(8,128)(2,1)S(1)}, bf16[512,768]{1,0:T(8,128)(2,1)S(1)}, u32[]{:S(2)}, u32[]{:S(2)}) collective-permute-start(bf16[512,768]{1,0:T(8,128)(2,1)S(1)} %copy-done), channel_id=1, source_target_pairs={{0,1},{1,0},{2,3},{3,2},{4,5},{5,4},{6,7},{7,6},{8,9},{9,8},{10,11... | collective-permute-start | bytes 2359304 | tf_op jit(solution)/shard_map/ppermute | solution.py:349
  38.1 23.9 %copy-start.19 = (bf16[512,768]{1,0:T(8,128)(2,1)}, bf16[512,768]{1,0:T(8,128)(2,1)S(1)}, u32[]{:S(2)}) copy-start(bf16[512,768]{1,0:T(8,128)(2,1)S(1)} %collective-permute-done.1.refs_2_) | copy-start | bytes 2359300
  38.1 23.9 %collective-permute-start.2 = (bf16[512,768]{1,0:T(8,128)(2,1)S(1)}, bf16[512,768]{1,0:T(8,128)(2,1)}, u32[]{:S(2)}, u32[]{:S(2)}) collective-permute-start(bf16[512,768]{1,0:T(8,128)(2,1)S(1)} %collective-permute-done.1.refs_2_), channel_id=1, source_target_pairs={{0,1},{1,0},{2,3},{3,2},{4,5},{5,4},{6,7},{7,6},{8,9},{9,8},{10,11... | collective-permute-start | bytes 2359304 | tf_op jit(solution)/shard_map/ppermute | solution.py:349
  43.5 18.2 %collective-permute-start.7 = (bf16[96,640]{1,0:T(8,128)(2,1)S(1)}, bf16[96,640]{1,0:T(8,128)(2,1)S(1)}, u32[]{:S(2)}, u32[]{:S(2)}) collective-permute-start(bf16[96,640]{1,0:T(8,128)(2,1)S(1)} %maximum_maximum_fusion.refs_7_), channel_id=1, source_target_pairs={{0,20},{4,16},{8,28},{12,24},{16,4},{20,0},{24,12},{28,8},{1,21},{... | collective-permute-start | bytes 368648 | tf_op jit(solution)/shard_map/ppermute | solution.py:349
  43.7 18.1 %collective-permute-start.8 = (bf16[96,640]{1,0:T(8,128)(2,1)S(1)}, bf16[96,640]{1,0:T(8,128)(2,1)}, u32[]{:S(2)}, u32[]{:S(2)}) collective-permute-start(bf16[96,640]{1,0:T(8,128)(2,1)S(1)} %maximum_maximum_fusion.refs_7_), channel_id=1, source_target_pairs={{0,24},{4,28},{8,16},{12,20},{16,8},{20,12},{24,0},{28,4},{1,25},{... | collective-permute-start | bytes 368648 | tf_op jit(solution)/shard_map/ppermute | solution.py:349
  46.9 15.0 %collective-permute-start.9 = (bf16[96,640]{1,0:T(8,128)(2,1)S(1)}, bf16[96,640]{1,0:T(8,128)(2,1)}, u32[]{:S(2)}, u32[]{:S(2)}) collective-permute-start(bf16[96,640]{1,0:T(8,128)(2,1)S(1)} %maximum_maximum_fusion.refs_7_), channel_id=1, source_target_pairs={{0,28},{4,24},{8,20},{12,16},{16,12},{20,8},{24,4},{28,0},{1,29},{... | collective-permute-start | bytes 368648 | tf_op jit(solution)/shard_map/ppermute | solution.py:349
  109.5 5.3 %collective-permute-start.12 = (bf16[512,768]{1,0:T(8,128)(2,1)S(1)}, bf16[512,768]{1,0:T(8,128)(2,1)S(1)}, u32[]{:S(2)}, u32[]{:S(2)}) collective-permute-start(bf16[512,768]{1,0:T(8,128)(2,1)S(1)} %get-tuple-element.93), channel_id=1, source_target_pairs={{0,1},{1,0},{2,3},{3,2},{4,5},{5,4},{6,7},{7,6},{8,9},{9,8},{10,11... | collective-permute-start | bytes 2359304 | tf_op jit(solution)/shard_map/ppermute | solution.py:349
  112.8 5.1 %collective-permute-start.11 = (bf16[512,768]{1,0:T(8,128)(2,1)S(1)}, bf16[512,768]{1,0:T(8,128)(2,1)S(1)}, u32[]{:S(2)}, u32[]{:S(2)}) collective-permute-start(bf16[512,768]{1,0:T(8,128)(2,1)S(1)} %get-tuple-element.92), channel_id=1, source_target_pairs={{0,1},{1,0},{2,3},{3,2},{4,5},{5,4},{6,7},{7,6},{8,9},{9,8},{10,11... | collective-permute-start | bytes 2359304 | tf_op jit(solution)/shard_map/ppermute | solution.py:349
  115.0 18.8 %collective-permute-start.13 = (bf16[512,768]{1,0:T(8,128)(2,1)S(1)}, bf16[512,768]{1,0:T(8,128)(2,1)S(1)}, u32[]{:S(2)}, u32[]{:S(2)}) collective-permute-start(bf16[512,768]{1,0:T(8,128)(2,1)S(1)} %add_convert_fusion.2), channel_id=1, source_target_pairs={{0,2},{1,3},{2,0},{3,1},{4,6},{5,7},{6,4},{7,5},{8,10},{9,11},{10,... | collective-permute-start | bytes 2359304 | tf_op jit(solution)/shard_map/ppermute | solution.py:349
  116.3 20.2 %collective-permute-start.16 = (bf16[512,768]{1,0:T(8,128)(2,1)S(1)}, bf16[512,768]{1,0:T(8,128)(2,1)S(1)}, u32[]{:S(2)}, u32[]{:S(2)}) collective-permute-start(bf16[512,768]{1,0:T(8,128)(2,1)S(1)} %copy-done.5), channel_id=1, source_target_pairs={{0,1},{1,0},{2,3},{3,2},{4,5},{5,4},{6,7},{7,6},{8,9},{9,8},{10,11... | collective-permute-start | bytes 2359304 | tf_op jit(solution)/shard_map/ppermute | solution.py:349
  135.2 3.2 collective-permute-start.14
  151.7 11.0 %collective-permute-start.17 = (bf16[512,768]{1,0:T(8,128)(2,1)}, bf16[512,768]{1,0:T(8,128)(2,1)}, u32[]{:S(2)}, u32[]{:S(2)}) collective-permute-start(bf16[512,768]{1,0:T(8,128)(2,1)} %slice.248), channel_id=1, source_target_pairs={{0,1},{1,0},{2,3},{3,2},{4,5},{5,4},{6,7},{7,6},{8,9},{9,8},{10,11... | collective-permute-start | bytes 2359304 | tf_op jit(solution)/shard_map/ppermute | solution.py:349
  155.5 9.7 %collective-permute-start.15 = (bf16[512,768]{1,0:T(8,128)(2,1)}, bf16[512,768]{1,0:T(8,128)(2,1)}, u32[]{:S(2)}, u32[]{:S(2)}) collective-permute-start(bf16[512,768]{1,0:T(8,128)(2,1)} %slice.249), channel_id=1, source_target_pairs={{0,1},{1,0},{2,3},{3,2},{4,5},{5,4},{6,7},{7,6},{8,9},{9,8},{10,11... | collective-permute-start | bytes 2359304 | tf_op jit(solution)/shard_map/ppermute | solution.py:349
  169.3 19.0 %collective-permute-start.19 = (bf16[512,768]{1,0:T(8,128)(2,1)}, bf16[512,768]{1,0:T(8,128)(2,1)S(1)}, u32[]{:S(2)}, u32[]{:S(2)}) collective-permute-start(bf16[512,768]{1,0:T(8,128)(2,1)} %get-tuple-element.82.refs_0_), channel_id=1, source_target_pairs={{0,2},{1,3},{2,0},{3,1},{4,6},{5,7},{6,4},{7,5},{8,10},{9,11},{10,... | collective-permute-start | bytes 2359304 | tf_op jit(solution)/shard_map/ppermute | solution.py:349
  172.4 19.1 %collective-permute-start.18 = (bf16[512,768]{1,0:T(8,128)(2,1)}, bf16[512,768]{1,0:T(8,128)(2,1)S(1)}, u32[]{:S(2)}, u32[]{:S(2)}) collective-permute-start(bf16[512,768]{1,0:T(8,128)(2,1)} %get-tuple-element.82.refs_0_), channel_id=1, source_target_pairs={{0,1},{1,0},{2,3},{3,2},{4,5},{5,4},{6,7},{7,6},{8,9},{9,8},{10,11... | collective-permute-start | bytes 2359304 | tf_op jit(solution)/shard_map/ppermute | solution.py:349
  188.2 3.3 %collective-permute-start.20 = (bf16[512,768]{1,0:T(8,128)(2,1)S(1)}, bf16[512,768]{1,0:T(8,128)(2,1)}, u32[]{:S(2)}, u32[]{:S(2)}) collective-permute-start(bf16[512,768]{1,0:T(8,128)(2,1)S(1)} %collective-permute-done.19.refs_2_), channel_id=1, source_target_pairs={{0,1},{1,0},{2,3},{3,2},{4,5},{5,4},{6,7},{7,6},{8,9},{9,8},{10,11... | collective-permute-start | bytes 2359304 | tf_op jit(solution)/shard_map/ppermute | solution.py:349
  236.6 22.4 %copy-start.25 = (bf16[96,768]{1,0:T(8,128)(2,1)S(1)}, bf16[96,768]{1,0:T(8,128)(2,1)}, u32[]{:S(2)}) copy-start(bf16[96,768]{1,0:T(8,128)(2,1)} %get-tuple-element.36) | copy-start | bytes 442372
  236.6 26.9 %copy-start.24 = (bf16[96,768]{1,0:T(8,128)(2,1)S(1)}, bf16[96,768]{1,0:T(8,128)(2,1)}, u32[]{:S(2)}) copy-start(bf16[96,768]{1,0:T(8,128)(2,1)} %get-tuple-element.37) | copy-start | bytes 442372
  236.6 28.0 %copy-start.23 = (bf16[96,768]{1,0:T(8,128)(2,1)S(1)}, bf16[96,768]{1,0:T(8,128)(2,1)}, u32[]{:S(2)}) copy-start(bf16[96,768]{1,0:T(8,128)(2,1)} %get-tuple-element.38) | copy-start | bytes 442372
  236.7 43.8 %copy-start.14 = (bf16[96,768]{1,0:T(8,128)(2,1)S(1)}, bf16[96,768]{1,0:T(8,128)(2,1)}, u32[]{:S(2)}) copy-start(bf16[96,768]{1,0:T(8,128)(2,1)} %get-tuple-element.31) | copy-start | bytes 442372
  239.1 41.4 %copy-start.12 = (bf16[96,576]{1,0:T(8,128)(2,1)S(1)}, bf16[96,576]{1,0:T(8,128)(2,1)}, u32[]{:S(2)}) copy-start(bf16[96,576]{1,0:T(8,128)(2,1)} %copy-done.11) | copy-start | bytes 331780
  239.1 19.8 %collective-permute-start.22 = (bf16[512,768]{1,0:T(8,128)(2,1)S(1)}, bf16[512,768]{1,0:T(8,128)(2,1)S(1)}, u32[]{:S(2)}, u32[]{:S(2)}) collective-permute-start(bf16[512,768]{1,0:T(8,128)(2,1)S(1)} %get-tuple-element.91), channel_id=1, source_target_pairs={{0,1},{1,0},{2,3},{3,2},{4,5},{5,4},{6,7},{7,6},{8,9},{9,8},{10,11... | collective-permute-start | bytes 2359304 | tf_op jit(solution)/shard_map/ppermute | solution.py:349
  239.4 24.1 %collective-permute-start.24 = (bf16[96,768]{1,0:T(8,128)(2,1)S(1)}, bf16[96,768]{1,0:T(8,128)(2,1)S(1)}, u32[]{:S(2)}, u32[]{:S(2)}) collective-permute-start(bf16[96,768]{1,0:T(8,128)(2,1)S(1)} %copy-done.29), channel_id=1, source_target_pairs={{0,4},{4,0},{8,12},{12,8},{16,20},{20,16},{24,28},{28,24},{1,5},{5... | collective-permute-start | bytes 442376 | tf_op jit(solution)/shard_map/ppermute | solution.py:349
  243.5 21.2 %collective-permute-start.25 = (bf16[96,768]{1,0:T(8,128)(2,1)S(1)}, bf16[96,768]{1,0:T(8,128)(2,1)S(1)}, u32[]{:S(2)}, u32[]{:S(2)}) collective-permute-start(bf16[96,768]{1,0:T(8,128)(2,1)S(1)} %copy-done.28), channel_id=1, source_target_pairs={{0,8},{4,12},{8,0},{12,4},{16,24},{20,28},{24,16},{28,20},{1,9},{5... | collective-permute-start | bytes 442376 | tf_op jit(solution)/shard_map/ppermute | solution.py:349
  257.8 11.1 %collective-permute-start.26 = (bf16[96,768]{1,0:T(8,128)(2,1)S(1)}, bf16[96,768]{1,0:T(8,128)(2,1)S(1)}, u32[]{:S(2)}, u32[]{:S(2)}) collective-permute-start(bf16[96,768]{1,0:T(8,128)(2,1)S(1)} %copy-done.27), channel_id=1, source_target_pairs={{0,12},{4,8},{8,4},{12,0},{16,28},{20,24},{24,20},{28,16},{1,13},{... | collective-permute-start | bytes 442376 | tf_op jit(solution)/shard_map/ppermute | solution.py:349
  259.0 18.3 %collective-permute-start.27 = (bf16[96,768]{1,0:T(8,128)(2,1)S(1)}, bf16[96,768]{1,0:T(8,128)(2,1)S(1)}, u32[]{:S(2)}, u32[]{:S(2)}) collective-permute-start(bf16[96,768]{1,0:T(8,128)(2,1)S(1)} %copy-done.26), channel_id=1, source_target_pairs={{0,16},{4,20},{8,24},{12,28},{16,0},{20,4},{24,8},{28,12},{1,17},{... | collective-permute-start | bytes 442376 | tf_op jit(solution)/shard_map/ppermute | solution.py:349
  259.0 21.4 %collective-permute-start.28 = (bf16[96,768]{1,0:T(8,128)(2,1)S(1)}, bf16[96,768]{1,0:T(8,128)(2,1)S(1)}, u32[]{:S(2)}, u32[]{:S(2)}) collective-permute-start(bf16[96,768]{1,0:T(8,128)(2,1)S(1)} %copy-done.25), channel_id=1, source_target_pairs={{0,20},{4,16},{8,28},{12,24},{16,4},{20,0},{24,12},{28,8},{1,21},{... | collective-permute-start | bytes 442376 | tf_op jit(solution)/shard_map/ppermute | solution.py:349
  263.5 16.8 %collective-permute-start.29 = (bf16[96,768]{1,0:T(8,128)(2,1)S(1)}, bf16[96,768]{1,0:T(8,128)(2,1)S(1)}, u32[]{:S(2)}, u32[]{:S(2)}) collective-permute-start(bf16[96,768]{1,0:T(8,128)(2,1)S(1)} %copy-done.24), channel_id=1, source_target_pairs={{0,24},{4,28},{8,16},{12,20},{16,8},{20,12},{24,0},{28,4},{1,25},{... | collective-permute-start | bytes 442376 | tf_op jit(solution)/shard_map/ppermute | solution.py:349
  264.7 15.7 %collective-permute-start.30 = (bf16[96,768]{1,0:T(8,128)(2,1)S(1)}, bf16[96,768]{1,0:T(8,128)(2,1)S(1)}, u32[]{:S(2)}, u32[]{:S(2)}) collective-permute-start(bf16[96,768]{1,0:T(8,128)(2,1)S(1)} %copy-done.23), channel_id=1, source_target_pairs={{0,28},{4,24},{8,20},{12,16},{16,12},{20,8},{24,4},{28,0},{1,29},{... | collective-permute-start | bytes 442376 | tf_op jit(solution)/shard_map/ppermute | solution.py:349
  268.9 17.0 %collective-permute-start.21 = (bf16[512,768]{1,0:T(8,128)(2,1)}, bf16[512,768]{1,0:T(8,128)(2,1)S(1)}, u32[]{:S(2)}, u32[]{:S(2)}) collective-permute-start(bf16[512,768]{1,0:T(8,128)(2,1)} %get-tuple-element.90), channel_id=1, source_target_pairs={{0,1},{1,0},{2,3},{3,2},{4,5},{5,4},{6,7},{7,6},{8,9},{9,8},{10,11... | collective-permute-start | bytes 2359304 | tf_op jit(solution)/shard_map/ppermute | solution.py:349
  277.3 16.6 %collective-permute-start.23 = (bf16[512,768]{1,0:T(8,128)(2,1)}, bf16[512,768]{1,0:T(8,128)(2,1)}, u32[]{:S(2)}, u32[]{:S(2)}) collective-permute-start(bf16[512,768]{1,0:T(8,128)(2,1)} %add_convert_fusion.1), channel_id=1, source_target_pairs={{0,2},{1,3},{2,0},{3,1},{4,6},{5,7},{6,4},{7,5},{8,10},{9,11},{10,... | collective-permute-start | bytes 2359304 | tf_op jit(solution)/shard_map/ppermute | solution.py:349
  297.4 4.3 %collective-permute-start.31 = (bf16[96,864]{1,0:T(8,128)(2,1)S(1)}, bf16[96,864]{1,0:T(8,128)(2,1)S(1)}, u32[]{:S(2)}, u32[]{:S(2)}) collective-permute-start(bf16[96,864]{1,0:T(8,128)(2,1)S(1)} %pad_maximum_fusion.9), channel_id=1, source_target_pairs={{0,2},{1,3},{2,0},{3,1},{4,6},{5,7},{6,4},{7,5},{8,10},{9,11},{10,... | collective-permute-start | bytes 497672 | tf_op jit(solution)/shard_map/ppermute | solution.py:349
  302.1 8.2 %collective-permute-start.32 = (f32[2,96]{1,0:T(2,128)S(1)}, f32[2,96]{1,0:T(2,128)S(1)}, u32[]{:S(2)}, u32[]{:S(2)}) collective-permute-start(f32[2,96]{1,0:T(2,128)S(1)} %maximum_divide_fusion), channel_id=1, source_target_pairs={{0,1},{1,0},{2,3},{3,2},{4,5},{5,4},{6,7},{7,6},{8,9},{9,8},{10,11... | collective-permute-start | bytes 2312 | tf_op jit(solution)/shard_map/ppermute | solution.py:349
  307.0 3.4 %collective-permute-start.33 = (f32[2,96]{1,0:T(2,128)S(1)}, f32[2,96]{1,0:T(2,128)S(1)}, u32[]{:S(2)}, u32[]{:S(2)}) collective-permute-start(f32[2,96]{1,0:T(2,128)S(1)} %maximum_divide_fusion), channel_id=1, source_target_pairs={{0,2},{1,3},{2,0},{3,1},{4,6},{5,7},{6,4},{7,5},{8,10},{9,11},{10,... | collective-permute-start | bytes 2312 | tf_op jit(solution)/shard_map/ppermute | solution.py:349
  307.0 3.4 %collective-permute-start.34 = (f32[2,96]{1,0:T(2,128)S(1)}, f32[2,96]{1,0:T(2,128)S(1)}, u32[]{:S(2)}, u32[]{:S(2)}) collective-permute-start(f32[2,96]{1,0:T(2,128)S(1)} %maximum_divide_fusion), channel_id=1, source_target_pairs={{0,3},{1,2},{2,1},{3,0},{4,7},{5,6},{6,5},{7,4},{8,11},{9,10},{10,... | collective-permute-start | bytes 2312 | tf_op jit(solution)/shard_map/ppermute | solution.py:349
  (25 other events, 212.5 us)
Sparse Core Ops, SparseCore 0:
  16.0 71.0 all-gather.1
  172.5 85.4 reduce-scatter.3

commit v3 on v2

v3 whole, which is shorter than its diff:
```python
import functools

import jax
import jax.numpy as jnp
from jax import lax
from jax.experimental import pallas as pl
from jax.experimental.pallas import tpu as pltpu
from jax.sharding import PartitionSpec as P

HEAD_DIM = 64
HALF = HEAD_DIM // 2
WIDE = 128
TILE = 256
FAR = -1e30
VMEM_BYTES = 56 * 1024 * 1024
BF16 = jnp.bfloat16
F32 = jnp.float32

NN = (((1,), (0,)), ((), ()))
NT = (((1,), (1,)), ((), ()))
TN = (((0,), (0,)), ((), ()))


def mm(left, right, dims=NN):
    return lax.dot_general(left, right, dims, preferred_element_type=F32)


def positions(lengths, total):
    ends = jnp.cumsum(lengths)
    starts = ends - lengths
    index = jnp.arange(total, dtype=jnp.int32)
    segment = jnp.sum((index[:, None] >= ends[None, :]).astype(jnp.int32), axis=1)
    onehot = segment[:, None] == jnp.arange(lengths.shape[0], dtype=jnp.int32)[None, :]
    first = jnp.sum(jnp.where(onehot, starts[None, :], 0), axis=1)
    last = jnp.sum(jnp.where(onehot, ends[None, :], 0), axis=1)
    return (segment, index - first, first, last)


def rope_tables(place):
    freq = jnp.exp(
        -jnp.log(jnp.float32(160000.0)) * jnp.arange(HALF, dtype=F32) * (2.0 / HEAD_DIM)
    )
    angle = freq[:, None] * place.astype(F32)[None, :]
    return (jnp.cos(angle), jnp.sin(angle))


def pieces_of(row):
    high = row.astype(BF16).astype(F32)
    rest = row - high
    middle = rest.astype(BF16).astype(F32)
    return high, middle, rest - middle


def extend(body, rows):
    rest = WIDE - body.shape[0] - sum(row.shape[0] for row in rows)
    return jnp.concatenate([body, *rows, jnp.zeros((rest, body.shape[1]), F32)], axis=0)


def slot_of(at, me, split):
    return ((at // split) ^ me) * split + at % split


def tile(at):
    return pl.ds(pl.multiple_of(at * TILE, TILE), TILE)


def place_shards(spot, shards_in, flat_ref):
    if len(shards_in) == 1:
        flat_ref[...] = shards_in[0][...]
        return
    slab = flat_ref.shape[0] // (2 * len(shards_in))
    for index in range(2 * len(shards_in)):
        place = pl.multiple_of((spot ^ index) * slab, slab)
        piece = shards_in[index // 2][index % 2 * slab : (index % 2 + 1) * slab, :]
        flat_ref[pl.ds(place, slab), :] = piece


def forward_kernel(blocks, low_ref, high_ref, me_ref, *refs):
    toks = refs[:4]
    seg_ref, cos_ref, sin_ref = refs[4:7]
    shards_in = refs[7 : 7 + blocks]
    normed_ref, query_ref, keys_ref, values_ref, ctx_ref, log_ref, wproj_ref = refs[
        7 + blocks : 14 + blocks
    ]
    nat_ref, flat_ref = refs[14 + blocks :]
    group = normed_ref.shape[0]
    heads = query_ref.shape[0]
    lanes = heads * HEAD_DIM
    parts = 8
    count = group // TILE
    split = count // 4
    wide = group // 4
    me = me_ref[0]

    place_shards(me_ref[1], shards_in, flat_ref)
    wproj_ref[...] = flat_ref[...].T
    gain = wproj_ref[3 * lanes : 3 * lanes + 16, :].astype(F32)[:1]

    for slot in range(count):
        rows = toks[slot // split][slot % split * TILE : (slot % split + 1) * TILE, :].astype(F32)
        center = rows - jnp.mean(rows, axis=-1, keepdims=True)
        spread = jnp.mean(center * center, axis=-1, keepdims=True)
        normed = (center * lax.rsqrt(spread + 1e-05) * gain).astype(BF16)
        normed_ref[slot * TILE : (slot + 1) * TILE, :] = normed

    def project(slot):
        return mm(wproj_ref[: 3 * lanes, :], normed_ref[slot * TILE : (slot + 1) * TILE, :], NT)

    upcoming = project(0)
    for slot in range(count):
        mixed = upcoming
        if slot + 1 < count:
            upcoming = project(slot + 1)
        here = slice(slot * TILE, (slot + 1) * TILE)
        there = tile(slot_of(slot, me, split))
        cosine = cos_ref[:, there]
        sine = sin_ref[:, there]
        segment = seg_ref[:, there]
        same = (segment == lax.broadcasted_iota(jnp.int32, (parts, TILE), 0)).astype(F32)
        ones = jnp.ones((2 * parts, TILE), F32)

        def rotated(top):
            first = mixed[top : top + HALF]
            second = mixed[top + HALF : top + HEAD_DIM]
            return jnp.concatenate(
                [first * cosine - second * sine, second * cosine + first * sine], axis=0
            )

        keys = []
        for head in range(heads):
            top = head * HEAD_DIM
            query = rotated(top) * (HEAD_DIM ** (-0.5))
            query_ref[head, :, here] = extend(query, [(1.0 - same) * FAR]).astype(BF16)
            keys.append(extend(rotated(lanes + top), [same, ones[:parts]]).astype(BF16))
            keys_ref[head, :, here] = keys[head][:HEAD_DIM]
            value = mixed[2 * lanes + top : 2 * lanes + top + HEAD_DIM]
            values_ref[head, :, here] = jnp.concatenate([value, ones], axis=0).astype(BF16)
        for head in range(heads):
            nat_ref[head, here, :] = keys[head].T

    every = range(heads)

    @pl.loop(0, 4)
    def attend(step):
        here = pl.ds(pl.multiple_of((step ^ me) * wide, wide), wide)

        def inner(at, carry):
            there = tile(slot_of(at, me, split))
            tops, accs = carry
            scores = [mm(nat_ref[h, there, :], query_ref[h, :, here]) for h in every]
            new = [jnp.maximum(tops[h], jnp.max(scores[h], axis=0, keepdims=True)) for h in every]
            expo = [jnp.exp(scores[h] - new[h]).astype(BF16) for h in every]
            scale = [jnp.exp(tops[h] - new[h]) for h in every]
            accs = [
                accs[h] * scale[h] + mm(values_ref[h, :, there], expo[h]) for h in every
            ]
            return new, accs

        start = (
            [jnp.full((1, wide), -jnp.inf, F32) for _ in every],
            [jnp.zeros((HEAD_DIM + 2 * parts, wide), F32) for _ in every],
        )
        tops, accs = lax.fori_loop(low_ref[step], high_ref[step], inner, start)
        totals = [acc[HEAD_DIM : HEAD_DIM + 1] for acc in accs]
        ctx = [acc[:HEAD_DIM] / total for acc, total in zip(accs, totals)]
        ctx_ref[:, here] = jnp.concatenate(ctx, axis=0).astype(BF16)
        logs = [top + jnp.log(total) for top, total in zip(tops, totals)]
        log_ref[:, here] = jnp.concatenate(
            logs + [jnp.zeros((8 - heads, wide), F32)], axis=0
        )


def backward_kernel(ring, low_ref, high_ref, me_ref, *refs):
    dattn = refs[:4]
    (
        normed_ref, query_ref, keys_ref, values_ref, ctx_ref, log_ref, wproj_ref,
        seg_ref, cos_ref, sin_ref, wback_ref, dnormed_ref,
    ) = refs[4:16]
    grads = refs[16:-9]
    qx_ref, kx_ref, vx_ref, dx_ref, dq_ref, dmix_ref, all_ref, tall_ref, flat_ref = refs[-9:]
    group = normed_ref.shape[0]
    lanes = wback_ref.shape[0]
    heads = lanes // HEAD_DIM
    parts = 8
    count = group // TILE
    split = count // 4
    me = me_ref[0]
    scale = HEAD_DIM ** (-0.5)
    every = range(heads)

    def pull_context(slot):
        piece = dattn[slot // split][slot % split * TILE : (slot % split + 1) * TILE, :]
        all_ref[slot * TILE : (slot + 1) * TILE, :] = piece
        return mm(wback_ref[...], piece, NT)

    upcoming = pull_context(0)
    for slot in range(count):
        here = slice(slot * TILE, (slot + 1) * TILE)
        there = tile(slot_of(slot, me, split))
        d_ctx = upcoming.astype(BF16).astype(F32)
        if slot + 1 < count:
            upcoming = pull_context(slot + 1)
        ctx = ctx_ref[:, here].astype(F32)
        segment = seg_ref[:, there]
        same = (segment == lax.broadcasted_iota(jnp.int32, (parts, TILE), 0)).astype(F32)
        ones = jnp.ones((parts, TILE), F32)
        blank = jnp.zeros((parts - 3, TILE), F32)
        logs = log_ref[:, here]
        natural = []
        for head in every:
            rows = slice(head * HEAD_DIM, (head + 1) * HEAD_DIM)
            delta = -jnp.sum(d_ctx[rows] * ctx[rows], axis=0, keepdims=True)
            dx_ref[head, :, here] = extend(d_ctx[rows], [*pieces_of(delta), blank]).astype(BF16)
            log = -logs[head : head + 1]
            query = query_ref[head, : HEAD_DIM + parts, here].astype(F32)
            qx_ref[head, :, here] = extend(query, [*pieces_of(log), blank]).astype(BF16)
            key = keys_ref[head, :, here].astype(F32)
            value = values_ref[head, :HEAD_DIM, here].astype(F32)
            natural.append(
                (extend(key, [same, ones]).astype(BF16), extend(value, [ones]).astype(BF16))
            )
            dq_ref[head, :, here] = jnp.zeros((HEAD_DIM, TILE), F32)
        for head in every:
            kx_ref[head, here, :] = natural[head][0].T
            vx_ref[head, here, :] = natural[head][1].T

    def turned_back(grad, where):
        cosine = cos_ref[:, where]
        sine = sin_ref[:, where]
        first = grad[:HALF]
        second = grad[HALF:]
        return jnp.concatenate(
            [first * cosine + second * sine, second * cosine - first * sine], axis=0
        ).astype(BF16)

    @pl.loop(0, count)
    def attend(step):
        here = tile(slot_of(step, me, split))

        def inner(at, carry):
            there = tile(slot_of(at, me, split))
            d_keys, d_values = carry
            scores = [mm(kx_ref[h, here, :], qx_ref[h, :, there]) for h in every]
            d_probs = [mm(vx_ref[h, here, :], dx_ref[h, :, there]) for h in every]
            probs = [jnp.exp(score) for score in scores]
            d_scores = [(probs[h] * d_probs[h]).astype(BF16) for h in every]
            low_probs = [prob.astype(BF16) for prob in probs]
            d_values = [
                d_values[h] + mm(dx_ref[h, :HEAD_DIM, there], low_probs[h], NT) for h in every
            ]
            d_keys = [
                d_keys[h] + mm(qx_ref[h, :HEAD_DIM, there], d_scores[h], NT) for h in every
            ]
            for h in every:
                dq_ref[h, :, there] += mm(keys_ref[h, :, here], d_scores[h])
            return d_keys, d_values

        zero = [jnp.zeros((HEAD_DIM, TILE), F32) for _ in every]
        d_keys, d_values = lax.fori_loop(low_ref[step], high_ref[step], inner, (zero, zero))
        for head in every:
            top = head * HEAD_DIM
            turned = turned_back(d_keys[head], tile(step))
            dmix_ref[lanes + top : lanes + top + HEAD_DIM, here] = turned
            d_value = d_values[head].astype(BF16)
            dmix_ref[2 * lanes + top : 2 * lanes + top + HEAD_DIM, here] = d_value

    for slot in range(count):
        here = slice(slot * TILE, (slot + 1) * TILE)
        there = tile(slot_of(slot, me, split))
        for head in every:
            top = head * HEAD_DIM
            turned = turned_back(dq_ref[head, :, here] * scale, there)
            dmix_ref[top : top + HEAD_DIM, here] = turned

    for step in range(3):
        rows = slice(step * lanes, (step + 1) * lanes)
        tall_ref[rows, :] = mm(dmix_ref[rows, :], normed_ref[...]).astype(BF16)
    tall_ref[3 * lanes :, :] = mm(ctx_ref[...], all_ref[...]).astype(BF16)
    flat_ref[...] = tall_ref[...].T
    if len(grads) == 1:
        grads[0][...] = flat_ref[...]
    else:
        slab = flat_ref.shape[0] // ring
        for index in range(ring):
            place = pl.multiple_of((me_ref[1] ^ index) * slab, slab)
            target = slice(index // 2 * slab, (index // 2 + 1) * slab)
            grads[index % 2][target, :] = flat_ref[pl.ds(place, slab), :]

    for slot in range(count):
        here = slice(slot * TILE, (slot + 1) * TILE)
        d_normed = mm(dmix_ref[:, here].T, wproj_ref[: 3 * lanes, :])
        dnormed_ref[here, :] = d_normed.astype(BF16)


def vmem_spec():
    return pl.BlockSpec(memory_space=pltpu.VMEM)


def smem_spec():
    return pl.BlockSpec(memory_space=pltpu.SMEM)


def attention_forward(low, high, me, toks, seg, cosine, sine, shards_in, lanes):
    rows, model = toks[0].shape
    group = 4 * rows
    heads = lanes // HEAD_DIM
    blocks = len(shards_in)
    width = shards_in[0].shape[1]
    shape = jax.ShapeDtypeStruct
    return pl.pallas_call(
        functools.partial(forward_kernel, blocks),
        out_shape=(
            shape((group, model), BF16),
            shape((heads, WIDE, group), BF16),
            shape((heads, HEAD_DIM, group), BF16),
            shape((heads, HEAD_DIM + 16, group), BF16),
            shape((lanes, group), BF16),
            shape((8, group), F32),
            shape((width, model), BF16),
        ),
        in_specs=[smem_spec()] * 3 + [vmem_spec()] * (7 + blocks),
        out_specs=[vmem_spec()] * 7,
        scratch_shapes=[
            pltpu.VMEM((heads, group, WIDE), BF16),
            pltpu.VMEM((model, width), BF16),
        ],
        compiler_params=pltpu.CompilerParams(vmem_limit_bytes=VMEM_BYTES),
        cost_estimate=pl.CostEstimate(
            flops=2 * group * model * lanes * 4 + 2 * group * group * lanes,
            bytes_accessed=group * model * 8,
            transcendentals=group * group,
        ),
        name="attention_forward",
    )(low, high, me, *toks, seg, cosine, sine, *shards_in)


def attention_backward(ring, direct, low, high, me, d_attn, kept, seg, cosine, sine, wback):
    rows, model = d_attn[0].shape
    group = 4 * rows
    lanes = wback.shape[0]
    heads = lanes // HEAD_DIM
    shape = jax.ShapeDtypeStruct
    outs = 2 if direct else 1
    return pl.pallas_call(
        functools.partial(backward_kernel, ring),
        out_shape=(
            shape((group, model), BF16),
            *[shape((model // outs, 4 * lanes), BF16) for _ in range(outs)],
        ),
        in_specs=[smem_spec()] * 3 + [vmem_spec()] * 15,
        out_specs=[vmem_spec()] * (1 + outs),
        scratch_shapes=[
            pltpu.VMEM((heads, WIDE, group), BF16),
            pltpu.VMEM((heads, group, WIDE), BF16),
            pltpu.VMEM((heads, group, WIDE), BF16),
            pltpu.VMEM((heads, WIDE, group), BF16),
            pltpu.VMEM((heads, HEAD_DIM, group), F32),
            pltpu.VMEM((3 * lanes, group), BF16),
            pltpu.VMEM((group, model), BF16),
            pltpu.VMEM((4 * lanes, model), BF16),
            pltpu.VMEM((model, 4 * lanes), BF16),
        ],
        compiler_params=pltpu.CompilerParams(vmem_limit_bytes=VMEM_BYTES),
        cost_estimate=pl.CostEstimate(
            flops=2 * group * model * lanes * 8 + 4 * group * group * lanes,
            bytes_accessed=group * model * 12,
            transcendentals=group * group,
        ),
        name="attention_backward",
    )(low, high, me, *d_attn, *kept, seg, cosine, sine, wback)


def swap(value, axis, bit):
    size = lax.axis_size(axis)
    return lax.ppermute(value, axis, [(i, i ^ bit) for i in range(size)])


def gather_rows(rows):
    far = swap(rows, "tp", 2)
    return (rows, swap(rows, "tp", 1), far, swap(far, "tp", 1))


def scatter_rows(partial):
    rows = partial.shape[0] // 4
    own, near, far, corner = (partial[k * rows : (k + 1) * rows] for k in range(4))
    far_sum = far.astype(F32) + swap(corner, "tp", 1).astype(F32)
    came = swap(far_sum.astype(BF16), "tp", 2)
    mine = own.astype(F32) + swap(near, "tp", 1).astype(F32)
    return mine + came.astype(F32)


def pair_rows(rows):
    return jnp.concatenate([rows, swap(rows, "tp", 1)], axis=0)


def scatter_pair(partial):
    rows = partial.shape[0] // 2
    came = swap(partial[rows:].astype(BF16), "tp", 1)
    return partial[:rows] + came.astype(F32)


def swaps_over(axis):
    size = lax.axis_size(axis)
    return size in (2, 4, 8)


def gather_slabs(slab):
    duo = jnp.concatenate([slab, swap(slab, "fsdp", 1)], axis=0)
    return [duo] + [swap(duo, "fsdp", bit) for bit in range(2, lax.axis_size("fsdp"), 2)]


def pair_slabs(keep, send):
    return (keep.astype(F32) + swap(send, "fsdp", 1).astype(F32)).astype(BF16)


def scatter_slabs(sums):
    ring = lax.axis_size("fsdp")
    slab = 2 * sums.shape[0] // ring
    own = sums[:slab].astype(F32)
    for at in range(1, ring // 2):
        own = own + swap(sums[at * slab : (at + 1) * slab], "fsdp", 2 * at).astype(F32)
    return own


def after(value, *others):
    return lax.optimization_barrier((value, *others))[0]


def center_rows(values):
    center = values - jnp.mean(values, axis=-1, keepdims=True)
    spread = jnp.mean(center * center, axis=-1, keepdims=True)
    inverse = lax.rsqrt(spread + 1e-05)
    return center * inverse, inverse


def norm_pull(normal, inverse, gain, grad):
    scaled = grad * gain
    mean = jnp.mean(scaled, axis=-1, keepdims=True)
    along = jnp.mean(scaled * normal, axis=-1, keepdims=True)
    return (scaled - mean - normal * along) * inverse


def geglu(up_in, gate_in):
    return jax.nn.gelu(up_in, approximate=False) * gate_in


def shards(tokens, seq_lengths, w_qkv, w_out, w_in, w_down, gains, cotangent):
    rows, model = tokens.shape
    slab = w_qkv.shape[1]
    lanes = w_qkv.shape[2]
    units = w_in.shape[2]
    group = rows * lax.axis_size("tp")
    ring = lax.axis_size("fsdp")
    direct = swaps_over("fsdp")
    at_fsdp = lax.axis_index("fsdp")

    own_proj = jnp.transpose(w_qkv, (1, 0, 2)).reshape(slab, 3 * lanes)
    spare = -(3 * lanes + gains.shape[0]) % WIDE
    first = jnp.concatenate([own_proj, gains.T, jnp.zeros((slab, spare), BF16)], axis=1)
    mine = jnp.concatenate([w_in[0], w_in[1], w_down.T], axis=1)
    other = swap(mine, "tp", 2)
    cut = (slice(0, units), slice(units, 2 * units), slice(2 * units, 3 * units))
    rest = jnp.concatenate([part[:, where] for where in cut for part in (mine, other)], axis=1)
    toks = gather_rows(tokens)
    if direct:
        first_parts = gather_slabs(first)
        out_parts = gather_slabs(after(w_out.T, first_parts[-1]))
        rest = after(rest, first_parts[-1])
        back_t = jnp.zeros((model, lanes), BF16)
        for index in range(ring):
            piece = out_parts[index // 2][index % 2 * slab : (index % 2 + 1) * slab]
            back_t = lax.dynamic_update_slice_in_dim(back_t, piece, (at_fsdp ^ index) * slab, 0)
    else:
        first_parts = [lax.all_gather(first, "fsdp", axis=0, tiled=True)]
        back_t = lax.all_gather(w_out.T, "fsdp", axis=0, tiled=True)
    whole_rest = lax.all_gather(rest, "fsdp", axis=0, tiled=True)
    pair_cat = whole_rest[:, : 4 * units]
    last_t = whole_rest[:, 4 * units :]

    segment, place, seq_first, seq_last = positions(seq_lengths[0], group)
    cosine, sine = rope_tables(place)
    low = seq_first[::TILE] // TILE
    high = (seq_last[TILE - 1 :: TILE] + TILE - 1) // TILE
    low_wide = seq_first[::rows] // TILE
    high_wide = (seq_last[rows - 1 :: rows] + TILE - 1) // TILE
    seg = segment[None, :]
    me = jnp.stack([lax.axis_index("tp"), at_fsdp]).astype(jnp.int32)

    normed1, query, keys, values, ctx, logs, proj_t = attention_forward(
        low_wide, high_wide, me, toks, seg, cosine, sine, first_parts, lanes
    )
    gain_one = proj_t[3 * lanes : 3 * lanes + 1].astype(F32)
    gain_two = proj_t[3 * lanes + 1 : 3 * lanes + 2].astype(F32)
    inputs = tokens.astype(F32)
    attn_part = lax.dot_general(
        ctx, back_t, (((0,), (1,)), ((), ())), preferred_element_type=F32
    ).astype(BF16)
    cots = pair_rows(cotangent)
    h_mid = inputs + scatter_rows(attn_part)
    normal2, inverse2 = center_rows(h_mid)
    full2 = pair_rows((normal2 * gain_two).astype(BF16))
    both = mm(full2, pair_cat)
    up_in = both[:, : 2 * units]
    gate_in = both[:, 2 * units :]
    hidden = geglu(up_in, gate_in).astype(BF16)
    d_hid = mm(cots, last_t)
    _, geglu_pull = jax.vjp(geglu, up_in, gate_in)
    d_up, d_gate = geglu_pull(d_hid)
    d_both = jnp.concatenate([d_up, d_gate], axis=1).astype(BF16)
    d_normed2 = scatter_pair(mm(d_both, pair_cat, NT))
    d_mid = cotangent.astype(F32) + norm_pull(normal2, inverse2, gain_two, d_normed2)
    d_low = d_mid.astype(BF16)
    d_attn = gather_rows(d_low)

    hidden = after(hidden, d_low)
    output = (h_mid + scatter_pair(mm(hidden, last_t, NT))).astype(BF16)
    early = jnp.concatenate(
        [
            mm(after(full2, d_low), d_both, TN).astype(BF16),
            mm(cots, hidden, TN).astype(BF16),
        ],
        axis=1,
    )
    if direct:
        grid = early.reshape(ring // 2, 2, slab, early.shape[1])
        take = functools.partial(lax.dynamic_index_in_dim, keepdims=False)
        keep, send = (take(grid, (at_fsdp & 1) ^ side, 1) for side in range(2))
        sums = pair_slabs(keep, send)
        sums = [take(sums, (at_fsdp >> 1) ^ at, 0) for at in range(ring // 2)]
        sum_early = scatter_slabs(jnp.concatenate(sums, axis=0))
    else:
        sum_early = lax.psum_scatter(early, "fsdp", scatter_dimension=0, tiled=True)

    d_part, *late = attention_backward(
        ring, direct, low, high, me, d_attn,
        (normed1, query, keys, values, ctx, logs, proj_t), seg, cosine, sine, back_t.T,
    )
    halves = [
        jnp.concatenate(
            [sum_early[:, (2 * k + side) * units : (2 * k + side + 1) * units] for k in range(3)],
            axis=1,
        )
        for side in range(2)
    ]
    own_early = halves[0].astype(F32) + swap(halves[1].astype(BF16), "tp", 2).astype(F32)
    if direct:
        own_late = scatter_slabs(pair_slabs(*late))
    else:
        own_late = lax.psum_scatter(late[0], "fsdp", scatter_dimension=0, tiled=True).astype(F32)
    d_normed1 = scatter_rows(d_part)
    normal1, inverse1 = center_rows(inputs)
    grad_tokens = (d_mid + norm_pull(normal1, inverse1, gain_one, d_normed1)).astype(BF16)

    sum_proj = own_late[:, : 3 * lanes]
    terms = jnp.stack(
        [
            jnp.sum(sum_proj * own_proj.astype(F32), axis=1),
            jnp.sum(own_early[:, : 2 * units] * mine[:, : 2 * units].astype(F32), axis=1),
        ]
    ) / gains.astype(F32)
    grad_gains = terms + swap(terms, "tp", 1) + swap(terms, "tp", 2) + swap(terms, "tp", 3)
    grad_qkv = jnp.transpose(sum_proj.reshape(slab, 3, lanes), (1, 0, 2))
    grad_in = jnp.stack([own_early[:, :units], own_early[:, units : 2 * units]])
    grad_out = own_late[:, 3 * lanes :].T
    grad_down = own_early[:, 2 * units :].T
    return (output, grad_tokens, grad_qkv, grad_out, grad_in, grad_down, grad_gains)


def solution(mesh):
    rows = P(("fsdp", "tp"), None)
    weights = (P(None, "fsdp", "tp"), P("tp", "fsdp"), P(None, "fsdp", "tp"), P("tp", "fsdp"))
    gains = P(None, "fsdp")
    return jax.shard_map(
        shards,
        mesh=mesh,
        in_specs=(rows, P("fsdp", None), *weights, gains, rows),
        out_specs=(rows, rows, *weights, gains),
        check_vma=False,
    )
```

time: 322 us -> 310 us (0.963)
  the two profiles are of different devices: /device:TPU:3 before, /device:TPU:0 now
where the time goes in v3:
time: 310 us; the launch traced here: 306 us
  waiting for transfers between devices  92.5 us (30%)
  Pallas kernels  60.2 us (19%)
  other arithmetic  43.8 us (14%)
  starting transfers between devices  42.3 us (14%)
  local copies, waits for them, and re-layouts  28.5 us (9%)
  matrix products  23.6 us (8%)
  between operations  15 us (5%)
    ppermute x37, waiting for transfers between devices, swap(): return lax.ppermute(value, axis, [(i, i ^ bit) for i in range(size)])  92.4 us
    ppermute x37, starting transfers between devices, swap(): return lax.ppermute(value, axis, [(i, i ^ bit) for i in range(size)])  42.2 us
    pallas_call x1, Pallas kernels, attention_backward(): pl.pallas_call(functools.partial(backward_kernel, ring), out_shape=(shape...  35.6 us
    pallas_call x1, Pallas kernels, attention_forward(): pl.pallas_call(functools.partial(forward_kernel, blocks), out_shape=(shap...  24.6 us
    dot_general x6, matrix products, mm(): return lax.dot_general(left, right, dims, preferred_element_type=F32)  21.4 us
    another operation x3, other arithmetic  12.3 us
    unnamed x72, local copies, waits for them, and re-layouts  9.85 us
  transfers between devices with their start and end apart: 38, of which 15 were waited for; matrix products, arithmetic and copies ran while one was open for 18% of the time, Pallas kernels for 20%

profile of v3, /device:TPU:0, one launch (start us, length us, event | category | flops | bytes accessed | tf_op | source)
XLA Modules:
  0.0 305.9 jit_solution(13015105678818225955)
XLA Ops:
  7.7 2.6 collective-permute-start.1
  12.4 1.6 collective-permute-start.3
  18.5 3.7 %collective-permute-start.6 = (bf16[192,640]{1,0:T(8,128)(2,1)S(1)}, bf16[192,640]{1,0:T(8,128)(2,1)S(1)}, u32[]{:S(2)}, u32[]{:S(2)}) collective-permute-start(bf16[192,640]{1,0:T(8,128)(2,1)S(1)} %pad_maximum_fusion.6.refs_7_), channel_id=1, source_target_pairs={{0,24},{4,28},{8,16},{12,20},{16,8},{20,12},{24,0},{28,4},{1,25},{... | collective-permute-start | bytes 737288 | tf_op jit(solution)/shard_map/ppermute | solution.py:375
  22.2 1.8 multiply_sine_fusion
  24.7 3.3 %collective-permute-done.6.refs_10_ = bf16[192,640]{1,0:T(8,128)(2,1)S(1)} collective-permute-done((bf16[192,640]{1,0:T(8,128)(2,1)S(1)}, bf16[192,640]{1,0:T(8,128)(2,1)S(1)}, u32[]{:S(2)}, u32[]{:S(2)}) %collective-permute-start.6) | collective-permute-done | bytes 245792 | tf_op jit(solution)/shard_map/ppermute | solution.py:375
  29.4 5.9 %collective-permute-start.5 = (bf16[192,640]{1,0:T(8,128)(2,1)S(1)}, bf16[192,640]{1,0:T(8,128)(2,1)S(1)}, u32[]{:S(2)}, u32[]{:S(2)}) collective-permute-start(bf16[192,640]{1,0:T(8,128)(2,1)S(1)} %pad_maximum_fusion.6.refs_7_), channel_id=1, source_target_pairs={{0,16},{4,20},{8,24},{12,28},{16,0},{20,4},{24,8},{28,12},{1,17},{... | collective-permute-start | bytes 737288 | tf_op jit(solution)/shard_map/ppermute | solution.py:375
  35.3 1.7 collective-permute-start.4
  40.2 8.9 %collective-permute-done.9 = bf16[192,192]{0,1:T(8,128)(2,1)S(1)} collective-permute-done((bf16[192,192]{0,1:T(8,128)(2,1)S(1)}, bf16[192,192]{0,1:T(8,128)(2,1)S(1)}, u32[]{:S(2)}, u32[]{:S(2)}) %collective-permute-start.9) | collective-permute-done | bytes 73760 | tf_op jit(solution)/shard_map/ppermute | solution.py:375
  49.4 7.7 %collective-permute-done.8 = bf16[192,192]{0,1:T(8,128)(2,1)S(1)} collective-permute-done((bf16[192,192]{0,1:T(8,128)(2,1)S(1)}, bf16[192,192]{0,1:T(8,128)(2,1)S(1)}, u32[]{:S(2)}, u32[]{:S(2)}) %collective-permute-start.8) | collective-permute-done | bytes 73760 | tf_op jit(solution)/shard_map/ppermute | solution.py:375
  57.1 3.1 %collective-permute-start.10 = (bf16[192,192]{0,1:T(8,128)(2,1)S(1)}, bf16[192,192]{0,1:T(8,128)(2,1)S(1)}, u32[]{:S(2)}, u32[]{:S(2)}) collective-permute-start(bf16[192,192]{0,1:T(8,128)(2,1)S(1)} %pad_maximum_fusion.10), channel_id=1, source_target_pairs={{0,24},{4,28},{8,16},{12,20},{16,8},{20,12},{24,0},{28,4},{1,25},{... | collective-permute-start | bytes 221192 | tf_op jit(solution)/shard_map/ppermute | solution.py:375
  62.2 3.3 %collective-permute-done.10 = bf16[192,192]{0,1:T(8,128)(2,1)S(1)} collective-permute-done((bf16[192,192]{0,1:T(8,128)(2,1)S(1)}, bf16[192,192]{0,1:T(8,128)(2,1)S(1)}, u32[]{:S(2)}, u32[]{:S(2)}) %collective-permute-start.10) | collective-permute-done | bytes 73760 | tf_op jit(solution)/shard_map/ppermute | solution.py:375
  67.7 24.6 %attention_forward.1 = (bf16[2048,768]{1,0:T(8,128)(2,1)}, bf16[3,128,2048]{2,1,0:T(8,128)(2,1)}, bf16[3,64,2048]{2,1,0:T(8,128)(2,1)}, bf16[3,80,2048]{2,1,0:T(...) custom-call(s32[4]{0:T(128)} %get-tuple-element.127.low_ref, ...), custom_call_target="tpu_custom_call" | custom-call | flops 4026531840 | bytes 12582912 | tf_op jit(solution)/shard_map/attention_forward/pallas_call | solution.py:310
  92.3 2.2 convolution_convert_fusion.1
  95.2 1.8 collective-permute-done.12
  97.2 1.5 collective-permute-start.13
  99.8 17.1 %collective-permute-done.13 = bf16[512,768]{1,0:T(8,128)(2,1)S(1)} collective-permute-done((bf16[512,768]{1,0:T(8,128)(2,1)S(1)}, bf16[512,768]{1,0:T(8,128)(2,1)S(1)}, u32[]{:S(2)}, u32[]{:S(2)}) %collective-permute-start.13) | collective-permute-done | bytes 786464 | tf_op jit(solution)/shard_map/ppermute | solution.py:375
  120.7 4.1 %fusion.23 = f32[1024,1152]{1,0:T(8,128)S(1)} fusion(bf16[768,1728]{1,0:T(8,128)(2,1)} %all-gather.2.cloned.1.call-done, bf16[512,768]{1,0:T(8,128)(2,1)} %collective-permute-done.14, bf16[512,768]{1,0:T(8,128)(2,1)S(1)} %multiply_convert_fusion.2), kind=kOutput, calls=%fused_computation.56 | convolution fusion | flops 1815085056 | bytes 8060928 | tf_op jit(solution)/shard_map/dot_general | solution.py:25
  124.8 6.8 %add_convert_fusion = (bf16[1024,576]{1,0:T(8,128)(2,1)S(1)}, f32[1024,576]{1,0:T(8,128)S(1)}, f32[1024,576]{1,0:T(8,128)S(1)}) fusion(f32[1024,1152]{1,0:T(8,128)S(1)} %fusion.23, bf16[1024,768]{1,0:T(8,128)(2,1)S(1)} %copy-done.18, bf16[768,1728]{1,0:T(8,128)(2,1)S(1)} %copy-done.26), kind=kOutput, calls=%fused_computation.8 | convolution fusion | flops 949026816 | bytes 13697024 | tf_op jit(solution)/shard_map/dot_general | solution.py:25
  131.7 11.3 %multiply_convert_fusion = (bf16[1024,576]{1,0:T(8,128)(2,1)S(1)}, bf16[1024,576]{1,0:T(8,128)(2,1)}) fusion(f32[1024,576]{1,0:T(8,128)S(1)} %get-tuple-element.123, f32[1024,576]{1,0:T(8,128)S(1)} %get-tuple-element.83, f32[1024,1152]{1,0:T(8,128)S(1)} %fusion.23), kind=kLoop, calls=%fused_computation.7 | loop fusion | flops 3538944 | bytes 11796480 | tf_op jit(solution)/shard_map/convert.13
  143.0 2.3 fusion.21
  145.2 1.7 copy-done.4
  150.5 1.8 fusion.32
  152.3 3.4 %fusion.39 = (bf16[512,768]{1,0:T(8,128)(2,1)}, f32[512,768]{1,0:T(8,128)}) fusion(f32[512]{0:T(512)S(1)} %broadcast_multiply_fusion.3, f32[512]{0:T(512)S(1)} %add_rsqrt_fusion.1, f32[512,768]{1,0:T(8,128)S(1)} %get-tuple-element.85, f32[512]{0:T(512)S(1)} %broadcast_multiply_fusion.5, f32[512]{0:T(512)S(1)} %broadcast_multiply_fusion.4, ...), kind=kLoop, calls=%fused_computation.136 | loop fusion | flops 4718592 | bytes 7089152 | tf_op jit(solution)/shard_map/convert_element_type | solution.py:512
  155.7 1.5 collective-permute-start.20
  157.2 3.6 %convolution_convert_fusion = bf16[768,1152]{1,0:T(8,128)(2,1)} fusion(bf16[1024,768]{1,0:T(8,128)(2,1)S(1)} %pad_maximum_fusion.2, bf16[1024,576]{1,0:T(8,128)(2,1)S(1)} %copy-done.12, bf16[1024,576]{1,0:T(8,128)(2,1)S(1)} %copy-done.32), kind=kOutput, calls=%fused_computation.1 | convolution fusion | flops 1817542656 | bytes 5701632 | tf_op jit(solution)/shard_map/dot_general | solution.py:25
  160.8 2.1 convolution_convert_fusion.2
  162.9 1.5 copy.90
  164.4 1.7 pad_maximum_fusion
  167.4 2.2 collective-permute-start.29
  169.5 2.6 fusion.25
  176.8 2.7 fusion.19
  179.5 20.6 %collective-permute-done.29 = bf16[4,96,1728]{2,1,0:T(8,128)(2,1)} collective-permute-done((bf16[4,96,1728]{2,1,0:T(8,128)(2,1)}, bf16[4,96,1728]{2,1,0:T(8,128)(2,1)}, u32[]{:S(2)}, u32[]{:S(2)}) %collective-permute-start.29) | collective-permute-done | bytes 1327136 | tf_op jit(solution)/shard_map/ppermute | solution.py:375
  200.0 1.8 fusion
  202.2 1.6 collective-permute-start.32
  203.9 1.6 collective-permute-start.31
  205.5 35.6 %attention_backward.1 = (bf16[2048,768]{1,0:T(8,128)(2,1)}, bf16[384,768]{1,0:T(8,128)(2,1)}, bf16[384,768]{1,0:T(8,128)(2,1)}) custom-call(s32[8]{0:T(128)} %get-tuple-element.125.low_ref, s32[8]{0:T(128)} %get-tuple-element.124.high_ref, s32[2]{0:T(128)} %pad_add_fusion.me_ref, bf16[512,768]{1,0:T(8,128)(2,1)} %get-tuple-element.80.refs_0_, ...), custom_call_target="tpu_custom_call" | custom-call | flops 8053063680 | bytes 18874368 | tf_op jit(solution)/shard_map/attention_backward/pallas_call | solution.py:344
  241.1 3.0 collective-permute-start.25
  244.1 2.6 fusion.42
  248.5 5.6 %collective-permute-done.33 = bf16[96,864]{1,0:T(8,128)(2,1)S(1)} collective-permute-done((bf16[96,864]{1,0:T(8,128)(2,1)S(1)}, bf16[96,864]{1,0:T(8,128)(2,1)S(1)}, u32[]{:S(2)}, u32[]{:S(2)}) %collective-permute-start.33) | collective-permute-done | bytes 165920 | tf_op jit(solution)/shard_map/ppermute | solution.py:375
  254.4 1.6 collective-permute-done.25
  256.8 2.1 collective-permute-start.28
  262.3 3.1 %collective-permute-done.28 = bf16[96,768]{1,0:T(8,128)(2,1)S(1)} collective-permute-done((bf16[96,768]{1,0:T(8,128)(2,1)S(1)}, bf16[96,768]{1,0:T(8,128)(2,1)S(1)}, u32[]{:S(2)}, u32[]{:S(2)}) %collective-permute-start.28) | collective-permute-done | bytes 147488 | tf_op jit(solution)/shard_map/ppermute | solution.py:375
  265.4 5.6 %collective-permute-done.27 = bf16[96,768]{1,0:T(8,128)(2,1)} collective-permute-done((bf16[96,768]{1,0:T(8,128)(2,1)S(1)}, bf16[96,768]{1,0:T(8,128)(2,1)}, u32[]{:S(2)}, u32[]{:S(2)}) %collective-permute-start.27) | collective-permute-done | bytes 147488 | tf_op jit(solution)/shard_map/ppermute | solution.py:375
  272.0 2.5 add_convert_fusion.1
  279.8 1.8 copy.93
  281.6 11.3 %collective-permute-done.35 = f32[2,96]{1,0:T(2,128)S(1)} collective-permute-done((f32[2,96]{1,0:T(2,128)S(1)}, f32[2,96]{1,0:T(2,128)S(1)}, u32[]{:S(2)}, u32[]{:S(2)}) %collective-permute-start.35) | collective-permute-done | bytes 800 | tf_op jit(solution)/shard_map/ppermute | solution.py:375
  293.5 2.1 fusion.33
  295.7 3.1 %fusion.16 = bf16[512,768]{1,0:T(8,128)(2,1)} fusion(f32[512,768]{1,0:T(8,128)S(1)} %copy-done.3, bf16[512,768]{1,0:T(8,128)(2,1)S(1)} %copy-done, f32[512]{0:T(512)S(1)} %broadcast_multiply_fusion, f32[512]{0:T(512)S(1)} %add_rsqrt_fusion, f32[512]{0:T(512)S(1)} %broadcast_multiply_fusion.1, f32[512]{0:T(512)S(1)} %broadcast_multiply_fusion.2, ...), kind=kLoop, calls=%fused_computation.37 | loop fusion | flops 5898240 | bytes 5516288 | tf_op jit(solution)/shard_map/convert_element_type | solution.py:552
  (194 shorter events, 45.4 us)
Async XLA Ops:
  7.2 113.6 %all-gather.2.cloned.1.call-start = ((), (), s32[]{:S(2)}) async-start(), calls=%async_computation | async-start | bytes 3096576 | tf_op jit(solution)/shard_map/all_gather | solution.py:476
  7.2 59.5 %collective-permute-start = (bf16[512,768]{1,0:T(8,128)(2,1)}, bf16[512,768]{1,0:T(8,128)(2,1)S(1)}, u32[]{:S(2)}, u32[]{:S(2)}) collective-permute-start(bf16[512,768]{1,0:T(8,128)(2,1)} %refs_0_.1), channel_id=1, source_target_pairs={{0,1},{1,0},{2,3},{3,2},{4,5},{5,4},{6,7},{7,6},{8,9},{9,8},{10,11... | collective-permute-start | bytes 2359304 | tf_op jit(solution)/shard_map/ppermute | solution.py:375
  7.7 30.4 %collective-permute-start.1 = (bf16[512,768]{1,0:T(8,128)(2,1)}, bf16[512,768]{1,0:T(8,128)(2,1)S(1)}, u32[]{:S(2)}, u32[]{:S(2)}) collective-permute-start(bf16[512,768]{1,0:T(8,128)(2,1)} %refs_0_.1), channel_id=1, source_target_pairs={{0,2},{1,3},{2,0},{3,1},{4,6},{5,7},{6,4},{7,5},{8,10},{9,11},{10,... | collective-permute-start | bytes 2359304 | tf_op jit(solution)/shard_map/ppermute | solution.py:375
  12.4 5.9 %collective-permute-start.3 = (bf16[96,640]{1,0:T(8,128)(2,1)S(1)}, bf16[96,640]{1,0:T(8,128)(2,1)S(1)}, u32[]{:S(2)}, u32[]{:S(2)}) collective-permute-start(bf16[96,640]{1,0:T(8,128)(2,1)S(1)} %pad_maximum_fusion.9), channel_id=1, source_target_pairs={{0,4},{4,0},{8,12},{12,8},{16,20},{20,16},{24,28},{28,24},{1,5},{5... | collective-permute-start | bytes 368648 | tf_op jit(solution)/shard_map/ppermute | solution.py:375
  15.9 76.4 %copy-start.13 = (bf16[96,288]{1,0:T(8,128)(2,1)}, bf16[96,288]{1,0:T(8,128)(2,1)S(1)}, u32[]{:S(2)}) copy-start(bf16[96,288]{1,0:T(8,128)(2,1)S(1)} %get-tuple-element.114) | copy-start | bytes 165892
  16.1 21.0 %collective-permute-start.15 = (bf16[96,864]{1,0:T(8,128)(2,1)S(1)}, bf16[96,864]{1,0:T(8,128)(2,1)S(1)}, u32[]{:S(2)}, u32[]{:S(2)}) collective-permute-start(bf16[96,864]{1,0:T(8,128)(2,1)S(1)} %pad_maximum_fusion.7), channel_id=1, source_target_pairs={{0,2},{1,3},{2,0},{3,1},{4,6},{5,7},{6,4},{7,5},{8,10},{9,11},{10,... | collective-permute-start | bytes 497672 | tf_op jit(solution)/shard_map/ppermute | solution.py:375
  18.2 48.5 %copy-start.22 = (s32[2048]{0:T(1024)}, s32[2048]{0:T(1024)S(1)}, u32[]{:S(2)}) copy-start(s32[2048]{0:T(1024)S(1)} %convert_reduce_fusion.1) | copy-start | bytes 24580
  18.4 74.0 %copy-start.23 = (s32[2048]{0:T(1024)}, s32[2048]{0:T(1024)S(1)}, u32[]{:S(2)}) copy-start(s32[2048]{0:T(1024)S(1)} %get-tuple-element.77) | copy-start | bytes 24580
  18.5 48.3 %copy-start.20 = (bf16[192,640]{1,0:T(8,128)(2,1)}, bf16[192,640]{1,0:T(8,128)(2,1)S(1)}, u32[]{:S(2)}) copy-start(bf16[192,640]{1,0:T(8,128)(2,1)S(1)} %pad_maximum_fusion.6.refs_7_) | copy-start | bytes 737284
  18.5 9.5 %collective-permute-start.6 = (bf16[192,640]{1,0:T(8,128)(2,1)S(1)}, bf16[192,640]{1,0:T(8,128)(2,1)S(1)}, u32[]{:S(2)}, u32[]{:S(2)}) collective-permute-start(bf16[192,640]{1,0:T(8,128)(2,1)S(1)} %pad_maximum_fusion.6.refs_7_), channel_id=1, source_target_pairs={{0,24},{4,28},{8,16},{12,20},{16,8},{20,12},{24,0},{28,4},{1,25},{... | collective-permute-start | bytes 737288 | tf_op jit(solution)/shard_map/ppermute | solution.py:375
  28.0 38.8 %copy-start.29 = (bf16[192,640]{1,0:T(8,128)(2,1)}, bf16[192,640]{1,0:T(8,128)(2,1)S(1)}, u32[]{:S(2)}) copy-start(bf16[192,640]{1,0:T(8,128)(2,1)S(1)} %collective-permute-done.6.refs_10_) | copy-start | bytes 737284
  28.0 7.3 %collective-permute-start.7 = (bf16[96,192]{0,1:T(8,128)(2,1)S(1)}, bf16[96,192]{0,1:T(8,128)(2,1)S(1)}, u32[]{:S(2)}, u32[]{:S(2)}) collective-permute-start(bf16[96,192]{0,1:T(8,128)(2,1)S(1)} %bitcast.68), channel_id=1, source_target_pairs={{0,4},{4,0},{8,12},{12,8},{16,20},{20,16},{24,28},{28,24},{1,5},{5... | collective-permute-start | bytes 110600 | tf_op jit(solution)/shard_map/ppermute | solution.py:375
  29.4 37.3 %collective-permute-start.5 = (bf16[192,640]{1,0:T(8,128)(2,1)S(1)}, bf16[192,640]{1,0:T(8,128)(2,1)S(1)}, u32[]{:S(2)}, u32[]{:S(2)}) collective-permute-start(bf16[192,640]{1,0:T(8,128)(2,1)S(1)} %pad_maximum_fusion.6.refs_7_), channel_id=1, source_target_pairs={{0,16},{4,20},{8,24},{12,28},{16,0},{20,4},{24,8},{28,12},{1,17},{... | collective-permute-start | bytes 737288 | tf_op jit(solution)/shard_map/ppermute | solution.py:375
  35.3 31.4 %collective-permute-start.4 = (bf16[192,640]{1,0:T(8,128)(2,1)S(1)}, bf16[192,640]{1,0:T(8,128)(2,1)}, u32[]{:S(2)}, u32[]{:S(2)}) collective-permute-start(bf16[192,640]{1,0:T(8,128)(2,1)S(1)} %pad_maximum_fusion.6.refs_7_), channel_id=1, source_target_pairs={{0,8},{4,12},{8,0},{12,4},{16,24},{20,28},{24,16},{28,20},{1,9},{5... | collective-permute-start | bytes 737288 | tf_op jit(solution)/shard_map/ppermute | solution.py:375
  37.1 12.0 %collective-permute-start.9 = (bf16[192,192]{0,1:T(8,128)(2,1)S(1)}, bf16[192,192]{0,1:T(8,128)(2,1)S(1)}, u32[]{:S(2)}, u32[]{:S(2)}) collective-permute-start(bf16[192,192]{0,1:T(8,128)(2,1)S(1)} %pad_maximum_fusion.10), channel_id=1, source_target_pairs={{0,16},{4,20},{8,24},{12,28},{16,0},{20,4},{24,8},{28,12},{1,17},{... | collective-permute-start | bytes 221192 | tf_op jit(solution)/shard_map/ppermute | solution.py:375
  38.2 28.6 %copy-start.28 = (bf16[512,768]{1,0:T(8,128)(2,1)}, bf16[512,768]{1,0:T(8,128)(2,1)S(1)}, u32[]{:S(2)}) copy-start(bf16[512,768]{1,0:T(8,128)(2,1)S(1)} %collective-permute-done.1.refs_2_) | copy-start | bytes 2359300
  38.2 28.6 %collective-permute-start.2 = (bf16[512,768]{1,0:T(8,128)(2,1)S(1)}, bf16[512,768]{1,0:T(8,128)(2,1)}, u32[]{:S(2)}, u32[]{:S(2)}) collective-permute-start(bf16[512,768]{1,0:T(8,128)(2,1)S(1)} %collective-permute-done.1.refs_2_), channel_id=1, source_target_pairs={{0,1},{1,0},{2,3},{3,2},{4,5},{5,4},{6,7},{7,6},{8,9},{9,8},{10,11... | collective-permute-start | bytes 2359304 | tf_op jit(solution)/shard_map/ppermute | solution.py:375
  49.1 8.0 %collective-permute-start.8 = (bf16[192,192]{0,1:T(8,128)(2,1)S(1)}, bf16[192,192]{0,1:T(8,128)(2,1)S(1)}, u32[]{:S(2)}, u32[]{:S(2)}) collective-permute-start(bf16[192,192]{0,1:T(8,128)(2,1)S(1)} %pad_maximum_fusion.10), channel_id=1, source_target_pairs={{0,8},{4,12},{8,0},{12,4},{16,24},{20,28},{24,16},{28,20},{1,9},{5... | collective-permute-start | bytes 221192 | tf_op jit(solution)/shard_map/ppermute | solution.py:375
  57.1 8.4 %collective-permute-start.10 = (bf16[192,192]{0,1:T(8,128)(2,1)S(1)}, bf16[192,192]{0,1:T(8,128)(2,1)S(1)}, u32[]{:S(2)}, u32[]{:S(2)}) collective-permute-start(bf16[192,192]{0,1:T(8,128)(2,1)S(1)} %pad_maximum_fusion.10), channel_id=1, source_target_pairs={{0,24},{4,28},{8,16},{12,20},{16,8},{20,12},{24,0},{28,4},{1,25},{... | collective-permute-start | bytes 221192 | tf_op jit(solution)/shard_map/ppermute | solution.py:375
  66.7 25.7 %copy-start.15 = (bf16[768,192]{0,1:T(8,128)(2,1)}, bf16[768,192]{0,1:T(8,128)(2,1)S(1)}, u32[]{:S(2)}) copy-start(bf16[768,192]{0,1:T(8,128)(2,1)S(1)} %dynamic_update_slice.31) | copy-start | bytes 884740
  94.7 2.4 collective-permute-start.12
  94.7 5.0 %collective-permute-start.11 = (bf16[512,768]{1,0:T(8,128)(2,1)S(1)}, bf16[512,768]{1,0:T(8,128)(2,1)S(1)}, u32[]{:S(2)}, u32[]{:S(2)}) collective-permute-start(bf16[512,768]{1,0:T(8,128)(2,1)S(1)} %get-tuple-element.90), channel_id=1, source_target_pairs={{0,1},{1,0},{2,3},{3,2},{4,5},{5,4},{6,7},{7,6},{8,9},{9,8},{10,11... | collective-permute-start | bytes 2359304 | tf_op jit(solution)/shard_map/ppermute | solution.py:375
  97.2 19.6 %collective-permute-start.13 = (bf16[512,768]{1,0:T(8,128)(2,1)S(1)}, bf16[512,768]{1,0:T(8,128)(2,1)S(1)}, u32[]{:S(2)}, u32[]{:S(2)}) collective-permute-start(bf16[512,768]{1,0:T(8,128)(2,1)S(1)} %add_convert_fusion.2), channel_id=1, source_target_pairs={{0,2},{1,3},{2,0},{3,1},{4,6},{5,7},{6,4},{7,5},{8,10},{9,11},{10,... | collective-permute-start | bytes 2359304 | tf_op jit(solution)/shard_map/ppermute | solution.py:375
  98.8 19.6 %collective-permute-start.16 = (bf16[512,768]{1,0:T(8,128)(2,1)S(1)}, bf16[512,768]{1,0:T(8,128)(2,1)S(1)}, u32[]{:S(2)}, u32[]{:S(2)}) collective-permute-start(bf16[512,768]{1,0:T(8,128)(2,1)S(1)} %copy-done.6), channel_id=1, source_target_pairs={{0,1},{1,0},{2,3},{3,2},{4,5},{5,4},{6,7},{7,6},{8,9},{9,8},{10,11... | collective-permute-start | bytes 2359304 | tf_op jit(solution)/shard_map/ppermute | solution.py:375
  118.2 2.5 collective-permute-start.14
  147.9 2.6 collective-permute-start.17
  155.7 21.0 %collective-permute-start.20 = (bf16[512,768]{1,0:T(8,128)(2,1)}, bf16[512,768]{1,0:T(8,128)(2,1)}, u32[]{:S(2)}, u32[]{:S(2)}) collective-permute-start(bf16[512,768]{1,0:T(8,128)(2,1)} %get-tuple-element.80.refs_0_), channel_id=1, source_target_pairs={{0,2},{1,3},{2,0},{3,1},{4,6},{5,7},{6,4},{7,5},{8,10},{9,11},{10,... | collective-permute-start | bytes 2359304 | tf_op jit(solution)/shard_map/ppermute | solution.py:375
  167.4 32.7 %collective-permute-start.29 = (bf16[4,96,1728]{2,1,0:T(8,128)(2,1)}, bf16[4,96,1728]{2,1,0:T(8,128)(2,1)}, u32[]{:S(2)}, u32[]{:S(2)}) collective-permute-start(bf16[4,96,1728]{2,1,0:T(8,128)(2,1)} %dynamic-slice_bitcast_fusion), channel_id=1, source_target_pairs={{0,4},{4,0},{8,12},{12,8},{16,20},{20,16},{24,28},{28,24},{1,5},{5... | collective-permute-start | bytes 3981320 | tf_op jit(solution)/shard_map/ppermute | solution.py:375
  174.1 2.7 collective-permute-start.18
  175.6 24.4 %copy-start.2 = (bf16[768,1728]{1,0:T(8,128)(2,1)S(1)}, bf16[768,1728]{1,0:T(8,128)(2,1)}, u32[]{:S(2)}) copy-start(bf16[768,1728]{1,0:T(8,128)(2,1)} %copy-done.1) | copy-start | bytes 7962628
  176.2 29.3 %collective-permute-start.19 = (bf16[512,768]{1,0:T(8,128)(2,1)}, bf16[512,768]{1,0:T(8,128)(2,1)}, u32[]{:S(2)}, u32[]{:S(2)}) collective-permute-start(bf16[512,768]{1,0:T(8,128)(2,1)} %get-tuple-element.80.refs_0_), channel_id=1, source_target_pairs={{0,1},{1,0},{2,3},{3,2},{4,5},{5,4},{6,7},{7,6},{8,9},{9,8},{10,11... | collective-permute-start | bytes 2359304 | tf_op jit(solution)/shard_map/ppermute | solution.py:375
  176.7 28.8 %collective-permute-start.21 = (bf16[512,768]{1,0:T(8,128)(2,1)}, bf16[512,768]{1,0:T(8,128)(2,1)}, u32[]{:S(2)}, u32[]{:S(2)}) collective-permute-start(bf16[512,768]{1,0:T(8,128)(2,1)} %collective-permute-done.20.refs_2_), channel_id=1, source_target_pairs={{0,1},{1,0},{2,3},{3,2},{4,5},{5,4},{6,7},{7,6},{8,9},{9,8},{10,11... | collective-permute-start | bytes 2359304 | tf_op jit(solution)/shard_map/ppermute | solution.py:375
  201.9 44.8 %collective-permute-start.30 = (bf16[96,1728]{1,0:T(8,128)(2,1)S(1)}, bf16[96,1728]{1,0:T(8,128)(2,1)S(1)}, u32[]{:S(2)}, u32[]{:S(2)}) collective-permute-start(bf16[96,1728]{1,0:T(8,128)(2,1)S(1)} %get-tuple-element.92), channel_id=1, source_target_pairs={{0,8},{4,12},{8,0},{12,4},{16,24},{20,28},{24,16},{28,20},{1,9},{5... | collective-permute-start | bytes 995336 | tf_op jit(solution)/shard_map/ppermute | solution.py:375
  202.2 45.0 %collective-permute-start.32 = (bf16[96,1728]{1,0:T(8,128)(2,1)S(1)}, bf16[96,1728]{1,0:T(8,128)(2,1)S(1)}, u32[]{:S(2)}, u32[]{:S(2)}) collective-permute-start(bf16[96,1728]{1,0:T(8,128)(2,1)S(1)} %get-tuple-element.93), channel_id=1, source_target_pairs={{0,24},{4,28},{8,16},{12,20},{16,8},{20,12},{24,0},{28,4},{1,25},{... | collective-permute-start | bytes 995336 | tf_op jit(solution)/shard_map/ppermute | solution.py:375
  203.9 43.4 %collective-permute-start.31 = (bf16[96,1728]{1,0:T(8,128)(2,1)S(1)}, bf16[96,1728]{1,0:T(8,128)(2,1)S(1)}, u32[]{:S(2)}, u32[]{:S(2)}) collective-permute-start(bf16[96,1728]{1,0:T(8,128)(2,1)S(1)} %get-tuple-element.94), channel_id=1, source_target_pairs={{0,16},{4,20},{8,24},{12,28},{16,0},{20,4},{24,8},{28,12},{1,17},{... | collective-permute-start | bytes 995336 | tf_op jit(solution)/shard_map/ppermute | solution.py:375
  241.1 14.9 %collective-permute-start.25 = (bf16[384,768]{1,0:T(8,128)(2,1)}, bf16[384,768]{1,0:T(8,128)(2,1)S(1)}, u32[]{:S(2)}, u32[]{:S(2)}) collective-permute-start(bf16[384,768]{1,0:T(8,128)(2,1)} %get-tuple-element.33), channel_id=1, source_target_pairs={{0,4},{4,0},{8,12},{12,8},{16,20},{20,16},{24,28},{28,24},{1,5},{5... | collective-permute-start | bytes 1769480 | tf_op jit(solution)/shard_map/ppermute | solution.py:375
  246.7 46.8 %collective-permute-start.22 = (bf16[512,768]{1,0:T(8,128)(2,1)}, bf16[512,768]{1,0:T(8,128)(2,1)S(1)}, u32[]{:S(2)}, u32[]{:S(2)}) collective-permute-start(bf16[512,768]{1,0:T(8,128)(2,1)} %get-tuple-element.88), channel_id=1, source_target_pairs={{0,1},{1,0},{2,3},{3,2},{4,5},{5,4},{6,7},{7,6},{8,9},{9,8},{10,11... | collective-permute-start | bytes 2359304 | tf_op jit(solution)/shard_map/ppermute | solution.py:375
  246.7 25.3 %collective-permute-start.23 = (bf16[512,768]{1,0:T(8,128)(2,1)}, bf16[512,768]{1,0:T(8,128)(2,1)}, u32[]{:S(2)}, u32[]{:S(2)}) collective-permute-start(bf16[512,768]{1,0:T(8,128)(2,1)} %get-tuple-element.89), channel_id=1, source_target_pairs={{0,1},{1,0},{2,3},{3,2},{4,5},{5,4},{6,7},{7,6},{8,9},{9,8},{10,11... | collective-permute-start | bytes 2359304 | tf_op jit(solution)/shard_map/ppermute | solution.py:375
  247.7 6.4 %collective-permute-start.33 = (bf16[96,864]{1,0:T(8,128)(2,1)S(1)}, bf16[96,864]{1,0:T(8,128)(2,1)S(1)}, u32[]{:S(2)}, u32[]{:S(2)}) collective-permute-start(bf16[96,864]{1,0:T(8,128)(2,1)S(1)} %pad_maximum_fusion.8), channel_id=1, source_target_pairs={{0,2},{1,3},{2,0},{3,1},{4,6},{5,7},{6,4},{7,5},{8,10},{9,11},{10,... | collective-permute-start | bytes 497672 | tf_op jit(solution)/shard_map/ppermute | solution.py:375
  256.8 5.5 %collective-permute-start.26 = (bf16[96,768]{1,0:T(8,128)(2,1)}, bf16[96,768]{1,0:T(8,128)(2,1)S(1)}, u32[]{:S(2)}, u32[]{:S(2)}) collective-permute-start(bf16[96,768]{1,0:T(8,128)(2,1)} %get-tuple-element.99), channel_id=1, source_target_pairs={{0,8},{4,12},{8,0},{12,4},{16,24},{20,28},{24,16},{28,20},{1,9},{5... | collective-permute-start | bytes 442376 | tf_op jit(solution)/shard_map/ppermute | solution.py:375
  256.8 8.6 %collective-permute-start.28 = (bf16[96,768]{1,0:T(8,128)(2,1)S(1)}, bf16[96,768]{1,0:T(8,128)(2,1)S(1)}, u32[]{:S(2)}, u32[]{:S(2)}) collective-permute-start(bf16[96,768]{1,0:T(8,128)(2,1)S(1)} %get-tuple-element.100), channel_id=1, source_target_pairs={{0,24},{4,28},{8,16},{12,20},{16,8},{20,12},{24,0},{28,4},{1,25},{... | collective-permute-start | bytes 442376 | tf_op jit(solution)/shard_map/ppermute | solution.py:375
  258.9 12.1 %collective-permute-start.27 = (bf16[96,768]{1,0:T(8,128)(2,1)S(1)}, bf16[96,768]{1,0:T(8,128)(2,1)}, u32[]{:S(2)}, u32[]{:S(2)}) collective-permute-start(bf16[96,768]{1,0:T(8,128)(2,1)S(1)} %get-tuple-element.101), channel_id=1, source_target_pairs={{0,16},{4,20},{8,24},{12,28},{16,0},{20,4},{24,8},{28,12},{1,17},{... | collective-permute-start | bytes 442376 | tf_op jit(solution)/shard_map/ppermute | solution.py:375
  262.0 30.9 %copy-start.25 = (bf16[2,96]{1,0:T(2,128)(2,1)S(1)}, bf16[2,96]{1,0:T(2,128)(2,1)}, u32[]{:S(2)}) copy-start(bf16[2,96]{1,0:T(2,128)(2,1)} %param.14) | copy-start | bytes 1156
  274.5 21.2 %copy-start.3 = (f32[512,768]{1,0:T(8,128)S(1)}, f32[512,768]{1,0:T(8,128)}, u32[]{:S(2)}) copy-start(f32[512,768]{1,0:T(8,128)} %get-tuple-element.81) | copy-start | bytes 4718596
  274.5 19.0 %collective-permute-start.24 = (bf16[512,768]{1,0:T(8,128)(2,1)}, bf16[512,768]{1,0:T(8,128)(2,1)}, u32[]{:S(2)}, u32[]{:S(2)}) collective-permute-start(bf16[512,768]{1,0:T(8,128)(2,1)} %add_convert_fusion.1), channel_id=1, source_target_pairs={{0,2},{1,3},{2,0},{3,1},{4,6},{5,7},{6,4},{7,5},{8,10},{9,11},{10,... | collective-permute-start | bytes 2359304 | tf_op jit(solution)/shard_map/ppermute | solution.py:375
  275.9 17.0 %collective-permute-start.35 = (f32[2,96]{1,0:T(2,128)S(1)}, f32[2,96]{1,0:T(2,128)S(1)}, u32[]{:S(2)}, u32[]{:S(2)}) collective-permute-start(f32[2,96]{1,0:T(2,128)S(1)} %maximum_divide_fusion), channel_id=1, source_target_pairs={{0,2},{1,3},{2,0},{3,1},{4,6},{5,7},{6,4},{7,5},{8,10},{9,11},{10,... | collective-permute-start | bytes 2312 | tf_op jit(solution)/shard_map/ppermute | solution.py:375
  277.3 15.6 %collective-permute-start.36 = (f32[2,96]{1,0:T(2,128)S(1)}, f32[2,96]{1,0:T(2,128)S(1)}, u32[]{:S(2)}, u32[]{:S(2)}) collective-permute-start(f32[2,96]{1,0:T(2,128)S(1)} %maximum_divide_fusion), channel_id=1, source_target_pairs={{0,3},{1,2},{2,1},{3,0},{4,7},{5,6},{6,5},{7,4},{8,11},{9,10},{10,... | collective-permute-start | bytes 2312 | tf_op jit(solution)/shard_map/ppermute | solution.py:375
  277.3 15.6 %collective-permute-start.34 = (f32[2,96]{1,0:T(2,128)S(1)}, f32[2,96]{1,0:T(2,128)S(1)}, u32[]{:S(2)}, u32[]{:S(2)}) collective-permute-start(f32[2,96]{1,0:T(2,128)S(1)} %maximum_divide_fusion), channel_id=1, source_target_pairs={{0,1},{1,0},{2,3},{3,2},{4,5},{5,4},{6,7},{7,6},{8,9},{9,8},{10,11... | collective-permute-start | bytes 2312 | tf_op jit(solution)/shard_map/ppermute | solution.py:375
  (23 other events, 126.2 us)
Sparse Core Ops, SparseCore 0:
  39.4 58.5 all-gather.1

commit v4 on v3

--- a/solution.py
+++ b/solution.py
@@ -65,14 +65,21 @@
 
 
 def place_shards(spot, shards_in, flat_ref):
-    if len(shards_in) == 1:
-        flat_ref[...] = shards_in[0][...]
+    slab = shards_in[0].shape[0]
+    for index, shard in enumerate(shards_in):
+        place = pl.multiple_of((spot ^ index) * slab, slab)
+        flat_ref[pl.ds(place, slab), :] = shard[...]
+
+
+def store_slabs(spot, ring, flat_ref, outs):
+    if len(outs) == 1:
+        outs[0][...] = flat_ref[...]
         return
-    slab = flat_ref.shape[0] // (2 * len(shards_in))
-    for index in range(2 * len(shards_in)):
+    slab = flat_ref.shape[0] // ring
+    for index in range(ring):
         place = pl.multiple_of((spot ^ index) * slab, slab)
-        piece = shards_in[index // 2][index % 2 * slab : (index % 2 + 1) * slab, :]
-        flat_ref[pl.ds(place, slab), :] = piece
+        target = slice(index // 2 * slab, (index // 2 + 1) * slab)
+        outs[index % 2][target, :] = flat_ref[pl.ds(place, slab), :]
 
 
 def forward_kernel(blocks, low_ref, high_ref, me_ref, *refs):
@@ -82,7 +89,8 @@
     normed_ref, query_ref, keys_ref, values_ref, ctx_ref, log_ref, wproj_ref = refs[
         7 + blocks : 14 + blocks
     ]
-    nat_ref, flat_ref = refs[14 + blocks :]
+    attns = refs[14 + blocks : 18 + blocks]
+    nat_ref, flat_ref, part_ref = refs[18 + blocks :]
     group = normed_ref.shape[0]
     heads = query_ref.shape[0]
     lanes = heads * HEAD_DIM
@@ -92,9 +100,9 @@
     wide = group // 4
     me = me_ref[0]
 
-    place_shards(me_ref[1], shards_in, flat_ref)
+    place_shards(me_ref[1] if blocks > 1 else 0, shards_in, flat_ref)
     wproj_ref[...] = flat_ref[...].T
-    gain = wproj_ref[3 * lanes : 3 * lanes + 16, :].astype(F32)[:1]
+    gain = wproj_ref[4 * lanes : 4 * lanes + 16, :].astype(F32)[:1]
 
     for slot in range(count):
         rows = toks[slot // split][slot % split * TILE : (slot % split + 1) * TILE, :].astype(F32)
@@ -163,23 +171,29 @@
         tops, accs = lax.fori_loop(low_ref[step], high_ref[step], inner, start)
         totals = [acc[HEAD_DIM : HEAD_DIM + 1] for acc in accs]
         ctx = [acc[:HEAD_DIM] / total for acc, total in zip(accs, totals)]
-        ctx_ref[:, here] = jnp.concatenate(ctx, axis=0).astype(BF16)
+        ctx = jnp.concatenate(ctx, axis=0).astype(BF16)
+        ctx_ref[:, here] = ctx
         logs = [top + jnp.log(total) for top, total in zip(tops, totals)]
         log_ref[:, here] = jnp.concatenate(
             logs + [jnp.zeros((8 - heads, wide), F32)], axis=0
         )
+        part_ref[here, :] = mm(ctx.T, wproj_ref[3 * lanes : 4 * lanes, :]).astype(BF16)
+
+    for index in range(4):
+        attns[index][...] = part_ref[index * wide : (index + 1) * wide, :]
 
 
 def backward_kernel(ring, low_ref, high_ref, me_ref, *refs):
     dattn = refs[:4]
     (
         normed_ref, query_ref, keys_ref, values_ref, ctx_ref, log_ref, wproj_ref,
-        seg_ref, cos_ref, sin_ref, wback_ref, dnormed_ref,
-    ) = refs[4:16]
-    grads = refs[16:-9]
+        seg_ref, cos_ref, sin_ref,
+    ) = refs[4:14]
+    dnormeds = refs[14:18]
+    grads = refs[18:-9]
     qx_ref, kx_ref, vx_ref, dx_ref, dq_ref, dmix_ref, all_ref, tall_ref, flat_ref = refs[-9:]
     group = normed_ref.shape[0]
-    lanes = wback_ref.shape[0]
+    lanes = ctx_ref.shape[0]
     heads = lanes // HEAD_DIM
     parts = 8
     count = group // TILE
@@ -191,7 +205,7 @@
     def pull_context(slot):
         piece = dattn[slot // split][slot % split * TILE : (slot % split + 1) * TILE, :]
         all_ref[slot * TILE : (slot + 1) * TILE, :] = piece
-        return mm(wback_ref[...], piece, NT)
+        return mm(wproj_ref[3 * lanes : 4 * lanes, :], piece, NT)
 
     upcoming = pull_context(0)
     for slot in range(count):
@@ -277,19 +291,72 @@
         tall_ref[rows, :] = mm(dmix_ref[rows, :], normed_ref[...]).astype(BF16)
     tall_ref[3 * lanes :, :] = mm(ctx_ref[...], all_ref[...]).astype(BF16)
     flat_ref[...] = tall_ref[...].T
-    if len(grads) == 1:
-        grads[0][...] = flat_ref[...]
-    else:
-        slab = flat_ref.shape[0] // ring
-        for index in range(ring):
-            place = pl.multiple_of((me_ref[1] ^ index) * slab, slab)
-            target = slice(index // 2 * slab, (index // 2 + 1) * slab)
-            grads[index % 2][target, :] = flat_ref[pl.ds(place, slab), :]
+    store_slabs(me_ref[1], ring, flat_ref, grads)
 
     for slot in range(count):
         here = slice(slot * TILE, (slot + 1) * TILE)
         d_normed = mm(dmix_ref[:, here].T, wproj_ref[: 3 * lanes, :])
-        dnormed_ref[here, :] = d_normed.astype(BF16)
+        inside = slice(slot % split * TILE, (slot % split + 1) * TILE)
+        dnormeds[slot // split][inside, :] = d_normed.astype(BF16)
+
+
+def mlp_kernel(ring, me_ref, *refs):
+    own_ref, near_ref, cot_ref, cot_near_ref, rest_ref = refs[:5]
+    d_own_ref, d_near_ref, hidden_ref, d_both_ref = refs[5:9]
+    grads = refs[9:-3]
+    pair_ref, cots_ref, flat_ref = refs[-3:]
+    rows, model = own_ref.shape
+    wide = hidden_ref.shape[1]
+    units = flat_ref.shape[1]
+    count = 2 * rows // TILE
+    half = count // 2
+
+    def start(slot):
+        inside = slice(slot % half * TILE, (slot % half + 1) * TILE)
+        normed = (own_ref, near_ref)[slot // half][inside, :]
+        cot = (cot_ref, cot_near_ref)[slot // half][inside, :]
+        cots_ref[:, slot * TILE : (slot + 1) * TILE] = cot.T
+        return mm(normed, rest_ref[:, : 2 * wide]), mm(cot, rest_ref[:, 2 * wide :])
+
+    upcoming = start(0)
+    pair_ref[...] = rest_ref[:, : 2 * wide].T
+    for slot in range(count):
+        both, d_hid = upcoming
+        if slot + 1 < count:
+            upcoming = start(slot + 1)
+        here = slice(slot * TILE, (slot + 1) * TILE)
+        inside = slice(slot % half * TILE, (slot % half + 1) * TILE)
+        up_in = both[:, :wide]
+        gate_in = both[:, wide:]
+        share = 0.5 + 0.5 * lax.erf(up_in * (0.5**0.5))
+        slope = share + up_in * jnp.exp(-0.5 * up_in * up_in) * 0.3989422804014327
+        curve = up_in * share
+        hidden_ref[here, :] = (curve * gate_in).astype(BF16)
+        d_up = (d_hid * gate_in * slope).astype(BF16)
+        d_gate = (d_hid * curve).astype(BF16)
+        d_both_ref[here, :wide] = d_up
+        d_both_ref[here, wide:] = d_gate
+        d_normed = mm(d_up, pair_ref[:wide, :]) + mm(d_gate, pair_ref[wide:, :])
+        (d_own_ref, d_near_ref)[slot // half][inside, :] = d_normed.astype(BF16)
+    flat_ref[...] = mm(cots_ref[...], hidden_ref[...])[:, :units].astype(BF16)
+    store_slabs(me_ref[0], ring, flat_ref, grads)
+
+
+def mlp_late_kernel(ring, me_ref, *refs):
+    own_ref, near_ref, hidden_ref, d_both_ref, rest_ref, out_own_ref, out_near_ref = refs[:7]
+    grads = refs[7:-3]
+    rows_ref, last_ref, flat_ref = refs[-3:]
+    rows = own_ref.shape[0]
+    wide = hidden_ref.shape[1]
+    units = flat_ref.shape[1] // 2
+    rows_ref[:, :rows] = own_ref[...].T
+    rows_ref[:, rows:] = near_ref[...].T
+    grad = mm(rows_ref[...], d_both_ref[...]).astype(BF16)
+    flat_ref[...] = jnp.concatenate([grad[:, :units], grad[:, wide : wide + units]], axis=1)
+    store_slabs(me_ref[0], ring, flat_ref, grads)
+    last_ref[...] = rest_ref[:, 2 * wide :].T
+    out_own_ref[...] = mm(hidden_ref[:rows, :], last_ref[...]).astype(BF16)
+    out_near_ref[...] = mm(hidden_ref[rows:, :], last_ref[...]).astype(BF16)
 
 
 def vmem_spec():
@@ -317,12 +384,14 @@
             shape((lanes, group), BF16),
             shape((8, group), F32),
             shape((width, model), BF16),
+            *[shape((rows, model), BF16) for _ in range(4)],
         ),
         in_specs=[smem_spec()] * 3 + [vmem_spec()] * (7 + blocks),
-        out_specs=[vmem_spec()] * 7,
+        out_specs=[vmem_spec()] * 11,
         scratch_shapes=[
             pltpu.VMEM((heads, group, WIDE), BF16),
             pltpu.VMEM((model, width), BF16),
+            pltpu.VMEM((group, model), BF16),
         ],
         compiler_params=pltpu.CompilerParams(vmem_limit_bytes=VMEM_BYTES),
         cost_estimate=pl.CostEstimate(
@@ -334,21 +403,21 @@
     )(low, high, me, *toks, seg, cosine, sine, *shards_in)
 
 
-def attention_backward(ring, direct, low, high, me, d_attn, kept, seg, cosine, sine, wback):
+def attention_backward(ring, direct, low, high, me, d_attn, kept, seg, cosine, sine):
     rows, model = d_attn[0].shape
     group = 4 * rows
-    lanes = wback.shape[0]
+    lanes = kept[4].shape[0]
     heads = lanes // HEAD_DIM
     shape = jax.ShapeDtypeStruct
     outs = 2 if direct else 1
     return pl.pallas_call(
         functools.partial(backward_kernel, ring),
         out_shape=(
-            shape((group, model), BF16),
+            *[shape((rows, model), BF16) for _ in range(4)],
             *[shape((model // outs, 4 * lanes), BF16) for _ in range(outs)],
         ),
-        in_specs=[smem_spec()] * 3 + [vmem_spec()] * 15,
-        out_specs=[vmem_spec()] * (1 + outs),
+        in_specs=[smem_spec()] * 3 + [vmem_spec()] * 14,
+        out_specs=[vmem_spec()] * (4 + outs),
         scratch_shapes=[
             pltpu.VMEM((heads, WIDE, group), BF16),
             pltpu.VMEM((heads, group, WIDE), BF16),
@@ -362,12 +431,68 @@
         ],
         compiler_params=pltpu.CompilerParams(vmem_limit_bytes=VMEM_BYTES),
         cost_estimate=pl.CostEstimate(
-            flops=2 * group * model * lanes * 8 + 4 * group * group * lanes,
+            flops=2 * group * model * lanes * 64,
             bytes_accessed=group * model * 12,
             transcendentals=group * group,
         ),
         name="attention_backward",
-    )(low, high, me, *d_attn, *kept, seg, cosine, sine, wback)
+    )(low, high, me, *d_attn, *kept, seg, cosine, sine)
+
+
+def mlp(ring, direct, spot, rows_in, cots, rest, units):
+    rows, model = rows_in[0].shape
+    wide = rest.shape[1] // 3
+    outs = 2 if direct else 1
+    shape = jax.ShapeDtypeStruct
+    return pl.pallas_call(
+        functools.partial(mlp_kernel, ring),
+        out_shape=(
+            shape((rows, model), BF16),
+            shape((rows, model), BF16),
+            shape((2 * rows, wide), BF16),
+            shape((2 * rows, 2 * wide), BF16),
+            *[shape((model // outs, units), BF16) for _ in range(outs)],
+        ),
+        in_specs=[smem_spec()] + [vmem_spec()] * 5,
+        out_specs=[vmem_spec()] * (4 + outs),
+        scratch_shapes=[
+            pltpu.VMEM((2 * wide, model), BF16),
+            pltpu.VMEM((model, 2 * rows), BF16),
+            pltpu.VMEM((model, units), BF16),
+        ],
+        compiler_params=pltpu.CompilerParams(vmem_limit_bytes=VMEM_BYTES),
+        cost_estimate=pl.CostEstimate(
+            flops=24 * rows * model * wide, bytes_accessed=rows * model * 16, transcendentals=0
+        ),
+        name="mlp",
+    )(spot, *rows_in, *cots, rest)
+
+
+def mlp_late(ring, direct, spot, rows_in, hidden, d_both, rest, units):
+    rows, model = rows_in[0].shape
+    wide = hidden.shape[1]
+    outs = 2 if direct else 1
+    shape = jax.ShapeDtypeStruct
+    return pl.pallas_call(
+        functools.partial(mlp_late_kernel, ring),
+        out_shape=(
+            shape((rows, model), BF16),
+            shape((rows, model), BF16),
+            *[shape((model // outs, 2 * units), BF16) for _ in range(outs)],
+        ),
+        in_specs=[smem_spec()] + [vmem_spec()] * 5,
+        out_specs=[vmem_spec()] * (2 + outs),
+        scratch_shapes=[
+            pltpu.VMEM((model, 2 * rows), BF16),
+            pltpu.VMEM((wide, model), BF16),
+            pltpu.VMEM((model, 2 * units), BF16),
+        ],
+        compiler_params=pltpu.CompilerParams(vmem_limit_bytes=VMEM_BYTES),
+        cost_estimate=pl.CostEstimate(
+            flops=12 * rows * model * wide, bytes_accessed=rows * model * 16, transcendentals=0
+        ),
+        name="mlp_late",
+    )(spot, *rows_in, hidden, d_both, rest)
 
 
 def swap(value, axis, bit):
@@ -380,23 +505,15 @@
     return (rows, swap(rows, "tp", 1), far, swap(far, "tp", 1))
 
 
-def scatter_rows(partial):
-    rows = partial.shape[0] // 4
-    own, near, far, corner = (partial[k * rows : (k + 1) * rows] for k in range(4))
-    far_sum = far.astype(F32) + swap(corner, "tp", 1).astype(F32)
-    came = swap(far_sum.astype(BF16), "tp", 2)
+def scatter_rows(own, near, far, corner):
+    far_sum = (far.astype(F32) + swap(corner, "tp", 1).astype(F32)).astype(BF16)
+    came = swap(far_sum, "tp", 2)
     mine = own.astype(F32) + swap(near, "tp", 1).astype(F32)
-    return mine + came.astype(F32)
-
-
-def pair_rows(rows):
-    return jnp.concatenate([rows, swap(rows, "tp", 1)], axis=0)
-
-
-def scatter_pair(partial):
-    rows = partial.shape[0] // 2
-    came = swap(partial[rows:].astype(BF16), "tp", 1)
-    return partial[:rows] + came.astype(F32)
+    return mine + came.astype(F32), far_sum
+
+
+def pair_sum(own, near):
+    return own.astype(F32) + swap(near, "tp", 1).astype(F32)
 
 
 def swaps_over(axis):
@@ -405,8 +522,8 @@
 
 
 def gather_slabs(slab):
-    duo = jnp.concatenate([slab, swap(slab, "fsdp", 1)], axis=0)
-    return [duo] + [swap(duo, "fsdp", bit) for bit in range(2, lax.axis_size("fsdp"), 2)]
+    evens = [slab] + [swap(slab, "fsdp", bit) for bit in range(2, lax.axis_size("fsdp"), 2)]
+    return [block for even in evens for block in (even, swap(even, "fsdp", 1))]
 
 
 def pair_slabs(keep, send):
@@ -438,10 +555,6 @@
     mean = jnp.mean(scaled, axis=-1, keepdims=True)
     along = jnp.mean(scaled * normal, axis=-1, keepdims=True)
     return (scaled - mean - normal * along) * inverse
-
-
-def geglu(up_in, gate_in):
-    return jax.nn.gelu(up_in, approximate=False) * gate_in
 
 
 def shards(tokens, seq_lengths, w_qkv, w_out, w_in, w_down, gains, cotangent):
@@ -455,27 +568,31 @@
     at_fsdp = lax.axis_index("fsdp")
 
     own_proj = jnp.transpose(w_qkv, (1, 0, 2)).reshape(slab, 3 * lanes)
-    spare = -(3 * lanes + gains.shape[0]) % WIDE
-    first = jnp.concatenate([own_proj, gains.T, jnp.zeros((slab, spare), BF16)], axis=1)
-    mine = jnp.concatenate([w_in[0], w_in[1], w_down.T], axis=1)
-    other = swap(mine, "tp", 2)
-    cut = (slice(0, units), slice(units, 2 * units), slice(2 * units, 3 * units))
-    rest = jnp.concatenate([part[:, where] for where in cut for part in (mine, other)], axis=1)
-    toks = gather_rows(tokens)
+    spare = -(4 * lanes + gains.shape[0]) % WIDE
+    first = jnp.concatenate(
+        [own_proj, w_out.T, gains.T, jnp.zeros((slab, spare), BF16)], axis=1
+    )
+    far = swap(tokens, "tp", 2)
+    near = swap(tokens, "tp", 1)
     if direct:
-        first_parts = gather_slabs(first)
-        out_parts = gather_slabs(after(w_out.T, first_parts[-1]))
-        rest = after(rest, first_parts[-1])
-        back_t = jnp.zeros((model, lanes), BF16)
-        for index in range(ring):
-            piece = out_parts[index // 2][index % 2 * slab : (index % 2 + 1) * slab]
-            back_t = lax.dynamic_update_slice_in_dim(back_t, piece, (at_fsdp ^ index) * slab, 0)
+        first_parts = gather_slabs(after(first, near))
     else:
         first_parts = [lax.all_gather(first, "fsdp", axis=0, tiled=True)]
-        back_t = lax.all_gather(w_out.T, "fsdp", axis=0, tiled=True)
+    corner = swap(after(far, *first_parts), "tp", 1)
+    toks = (tokens, near, far, corner)
+    mine = jnp.concatenate([w_in[0], w_in[1], w_down.T], axis=1)
+    other = swap(after(mine, far), "tp", 2)
+    spare = jnp.zeros((slab, -2 * units % WIDE), BF16)
+    rest = jnp.concatenate(
+        [
+            part
+            for k in range(3)
+            for part in (mine[:, k * units : (k + 1) * units], other[:, k * units : (k + 1) * units], spare)
+        ],
+        axis=1,
+    )
+    rest = after(rest, *first_parts)
     whole_rest = lax.all_gather(rest, "fsdp", axis=0, tiled=True)
-    pair_cat = whole_rest[:, : 4 * units]
-    last_t = whole_rest[:, 4 * units :]
 
     segment, place, seq_first, seq_last = positions(seq_lengths[0], group)
     cosine, sine = rope_tables(place)
@@ -486,55 +603,55 @@
     seg = segment[None, :]
     me = jnp.stack([lax.axis_index("tp"), at_fsdp]).astype(jnp.int32)
 
-    normed1, query, keys, values, ctx, logs, proj_t = attention_forward(
+    *kept, proj_t, own, near, far, corner = attention_forward(
         low_wide, high_wide, me, toks, seg, cosine, sine, first_parts, lanes
     )
-    gain_one = proj_t[3 * lanes : 3 * lanes + 1].astype(F32)
-    gain_two = proj_t[3 * lanes + 1 : 3 * lanes + 2].astype(F32)
+    gain_one = proj_t[4 * lanes : 4 * lanes + 1].astype(F32)
+    gain_two = proj_t[4 * lanes + 1 : 4 * lanes + 2].astype(F32)
     inputs = tokens.astype(F32)
-    attn_part = lax.dot_general(
-        ctx, back_t, (((0,), (1,)), ((), ())), preferred_element_type=F32
-    ).astype(BF16)
-    cots = pair_rows(cotangent)
-    h_mid = inputs + scatter_rows(attn_part)
+    cots = (cotangent, swap(cotangent, "tp", 1))
+    h_mid = inputs + scatter_rows(own, near, far, corner)[0]
     normal2, inverse2 = center_rows(h_mid)
-    full2 = pair_rows((normal2 * gain_two).astype(BF16))
-    both = mm(full2, pair_cat)
-    up_in = both[:, : 2 * units]
-    gate_in = both[:, 2 * units :]
-    hidden = geglu(up_in, gate_in).astype(BF16)
-    d_hid = mm(cots, last_t)
-    _, geglu_pull = jax.vjp(geglu, up_in, gate_in)
-    d_up, d_gate = geglu_pull(d_hid)
-    d_both = jnp.concatenate([d_up, d_gate], axis=1).astype(BF16)
-    d_normed2 = scatter_pair(mm(d_both, pair_cat, NT))
+    normed2 = (normal2 * gain_two).astype(BF16)
+    full2 = (normed2, swap(normed2, "tp", 1))
+    spot = me[1:]
+    d_own, d_near, hidden, d_both, *last_halves = mlp(
+        ring, direct, spot, full2, cots, whole_rest, 2 * units
+    )
+    d_normed2 = pair_sum(d_own, d_near)
     d_mid = cotangent.astype(F32) + norm_pull(normal2, inverse2, gain_two, d_normed2)
     d_low = d_mid.astype(BF16)
     d_attn = gather_rows(d_low)
 
-    hidden = after(hidden, d_low)
-    output = (h_mid + scatter_pair(mm(hidden, last_t, NT))).astype(BF16)
-    early = jnp.concatenate(
-        [
-            mm(after(full2, d_low), d_both, TN).astype(BF16),
-            mm(cots, hidden, TN).astype(BF16),
-        ],
-        axis=1,
-    )
+    out_own, out_near, *pair_halves = mlp_late(
+        ring, direct, spot, full2, after(hidden, d_attn[1]), d_both, whole_rest, 2 * units
+    )
+    output = (h_mid + pair_sum(out_own, out_near)).astype(BF16)
     if direct:
-        grid = early.reshape(ring // 2, 2, slab, early.shape[1])
-        take = functools.partial(lax.dynamic_index_in_dim, keepdims=False)
-        keep, send = (take(grid, (at_fsdp & 1) ^ side, 1) for side in range(2))
-        sums = pair_slabs(keep, send)
-        sums = [take(sums, (at_fsdp >> 1) ^ at, 0) for at in range(ring // 2)]
-        sum_early = scatter_slabs(jnp.concatenate(sums, axis=0))
+        pair_sums = pair_slabs(*pair_halves).reshape(ring // 2, slab, 4 * units)
+        last_sums = pair_slabs(*last_halves).reshape(ring // 2, slab, 2 * units)
+        sums = [
+            jnp.concatenate([pair_sums[at], last_sums[at]], axis=1) for at in range(ring // 2)
+        ]
+        d_attn, sums, output = lax.optimization_barrier((d_attn, sums, output))
+        sums = [sums[0]] + [swap(sums[at], "fsdp", 2 * at) for at in range(1, ring // 2)]
+
+    d_parts = attention_backward(
+        ring, direct, low, high, me, d_attn, (*kept, proj_t), seg, cosine, sine
+    )
+    if direct:
+        d_parts, sums = lax.optimization_barrier((d_parts, sums))
+    late = d_parts[4:]
+    d_normed1, far_sum = scatter_rows(*d_parts[:4])
+    if direct:
+        sum_early = after(sums[0], far_sum).astype(F32)
+        for at in range(1, ring // 2):
+            sum_early = sum_early + sums[at].astype(F32)
+        own_late = scatter_slabs(pair_slabs(after(late[0], far_sum), late[1]))
     else:
+        early = jnp.concatenate([pair_halves[0], last_halves[0]], axis=1)
         sum_early = lax.psum_scatter(early, "fsdp", scatter_dimension=0, tiled=True)
-
-    d_part, *late = attention_backward(
-        ring, direct, low, high, me, d_attn,
-        (normed1, query, keys, values, ctx, logs, proj_t), seg, cosine, sine, back_t.T,
-    )
+        own_late = lax.psum_scatter(late[0], "fsdp", scatter_dimension=0, tiled=True).astype(F32)
     halves = [
         jnp.concatenate(
             [sum_early[:, (2 * k + side) * units : (2 * k + side + 1) * units] for k in range(3)],
@@ -543,11 +660,6 @@
         for side in range(2)
     ]
     own_early = halves[0].astype(F32) + swap(halves[1].astype(BF16), "tp", 2).astype(F32)
-    if direct:
-        own_late = scatter_slabs(pair_slabs(*late))
-    else:
-        own_late = lax.psum_scatter(late[0], "fsdp", scatter_dimension=0, tiled=True).astype(F32)
-    d_normed1 = scatter_rows(d_part)
     normal1, inverse1 = center_rows(inputs)
     grad_tokens = (d_mid + norm_pull(normal1, inverse1, gain_one, d_normed1)).astype(BF16)
 

time: 310 us -> 250 us (0.81); the launches traced: 306 us -> 249 us
  matrix products: 23.6 us -> 0 us
  Pallas kernels: 60.2 us -> 82.3 us
  other arithmetic: 43.8 us -> 26 us
  waiting for transfers between devices: 92.5 us -> 77.6 us
  local copies, waits for them, and re-layouts: 28.5 us -> 13.6 us
  starting transfers between devices: 42.3 us -> 35 us
    dot_general x7 -> x0, matrix products: 23.6 us -> none  [the longest x6 21.4 us: mm(): return lax.dot_general(left, right, dims, preferred_element_type=F32)]
    pallas_call x1 -> x3, Pallas kernels: 35.6 us -> 55 us  [the longest x1 35.4 us: attention_backward(): pl.pallas_call(functools.partial(backward_kernel, ring), out_shape=(*[sha...]
    ppermute x37, waiting for transfers between devices: 92.4 us -> 77.5 us  [swap(): return lax.ppermute(value, axis, [(i, i ^ bit) for i in range(size)])]
    another operation x3 -> x2, other arithmetic: 12.3 us -> 1 us
    ppermute x37, starting transfers between devices: 42.2 us -> 35 us  [swap(): return lax.ppermute(value, axis, [(i, i ^ bit) for i in range(size)])]
    slice x8 -> x3, local copies, waits for them, and re-layouts: 5.11 us -> 0.22 us  [the longest x1 0.11 us: shards(): other[:, k * units:(k + 1) * units]]
    dynamic_update_slice x8 -> x0, local copies, waits for them, and re-layouts: 3.73 us -> none  [shards(): lax.dynamic_update_slice_in_dim(back_t, piece, (at_fsdp ^ index) * slab, 0)]
    concatenate x5, other arithmetic: 3.37 us -> 0.22 us  [the longest x4 0.13 us: shards(): jnp.concatenate([pair_sums[at], last_sums[at]], axis=1)]
  transfers between devices with their start and end apart: 38 -> 38, of which waited for: 15 -> 16; matrix products, arithmetic and copies ran while one was open for 18% -> 12% of each run, Pallas kernels for 20% -> 29%
where the time goes in v4:
time: 250 us; the launch traced here: 249 us
  Pallas kernels  82.3 us (33%)
  waiting for transfers between devices  77.6 us (31%)
  starting transfers between devices  35 us (14%)
  other arithmetic  26 us (10%)
  between operations  14.6 us (6%)
  local copies, waits for them, and re-layouts  13.6 us (5%)
    ppermute x37, waiting for transfers between devices, swap(): return lax.ppermute(value, axis, [(i, i ^ bit) for i in range(size)])  77.5 us
    pallas_call x1, Pallas kernels, attention_backward(): pl.pallas_call(functools.partial(backward_kernel, ring), out_shape=(*[sha...  35.4 us
    ppermute x37, starting transfers between devices, swap(): return lax.ppermute(value, axis, [(i, i ^ bit) for i in range(size)])  35 us
    pallas_call x1, Pallas kernels, attention_forward(): pl.pallas_call(functools.partial(forward_kernel, blocks), out_shape=(shap...  27.2 us
    pallas_call x1, Pallas kernels, mlp(): pl.pallas_call(functools.partial(mlp_kernel, ring), out_shape=(shape((row...  11.2 us
    unnamed x56, local copies, waits for them, and re-layouts  8.48 us
    pallas_call x1, Pallas kernels, mlp_late(): pl.pallas_call(functools.partial(mlp_late_kernel, ring), out_shape=(shape...  8.45 us
  transfers between devices with their start and end apart: 38, of which 16 were waited for; matrix products, arithmetic and copies ran while one was open for 12% of the time, Pallas kernels for 29%

profile of v4, /device:TPU:0, one launch (start us, length us, event | category | flops | bytes accessed | tf_op | source)
XLA Modules:
  0.0 249.1 jit_solution(2001208816263462145)
XLA Ops:
  7.7 2.6 %collective-permute-start.1 = (bf16[512,768]{1,0:T(8,128)(2,1)}, bf16[512,768]{1,0:T(8,128)(2,1)S(1)}, u32[]{:S(2)}, u32[]{:S(2)}) collective-permute-start(bf16[512,768]{1,0:T(8,128)(2,1)} %refs_0_.1), channel_id=1, source_target_pairs={{0,2},{1,3},{2,0},{3,1},{4,6},{5,7},{6,4},{7,5},{8,10},{9,11},{10,... | collective-permute-start | bytes 2359304 | tf_op jit(solution)/shard_map/ppermute | solution.py:500
  10.3 1.1 copy.32
  11.6 0.9 copy.33
  15.1 1.0 copy.36
  16.2 0.9 slice_bitcast_fusion.4
  17.4 1.6 collective-permute-start.3
  19.0 2.6 %collective-permute-start.5 = (bf16[96,896]{1,0:T(8,128)(2,1)S(1)}, bf16[96,896]{1,0:T(8,128)(2,1)S(1)}, u32[]{:S(2)}, u32[]{:S(2)}) collective-permute-start(bf16[96,896]{1,0:T(8,128)(2,1)S(1)} %maximum_maximum_fusion.refs_7_), channel_id=1, source_target_pairs={{0,16},{4,20},{8,24},{12,28},{16,0},{20,4},{24,8},{28,12},{1,17},{... | collective-permute-start | bytes 516104 | tf_op jit(solution)/shard_map/ppermute | solution.py:500
  21.8 6.8 %collective-permute-done.1.refs_2_ = bf16[512,768]{1,0:T(8,128)(2,1)S(1)} collective-permute-done((bf16[512,768]{1,0:T(8,128)(2,1)}, bf16[512,768]{1,0:T(8,128)(2,1)S(1)}, u32[]{:S(2)}, u32[]{:S(2)}) %collective-permute-start.1) | collective-permute-done | bytes 786464 | tf_op jit(solution)/shard_map/ppermute | solution.py:500
  28.7 1.8 collective-permute-start.15
  31.0 1.5 collective-permute-start.2
  33.0 1.6 collective-permute-done.5.refs_11_
  34.6 1.5 collective-permute-start.6
  36.7 1.0 concatenate.33
  38.3 3.8 %collective-permute-done.4.refs_10_ = bf16[96,896]{1,0:T(8,128)(2,1)} collective-permute-done((bf16[96,896]{1,0:T(8,128)(2,1)S(1)}, bf16[96,896]{1,0:T(8,128)(2,1)}, u32[]{:S(2)}, u32[]{:S(2)}) %collective-permute-start.4) | collective-permute-done | bytes 172064 | tf_op jit(solution)/shard_map/ppermute | solution.py:500
  42.1 3.7 %collective-permute-done.6.refs_12_ = bf16[96,896]{1,0:T(8,128)(2,1)} collective-permute-done((bf16[96,896]{1,0:T(8,128)(2,1)S(1)}, bf16[96,896]{1,0:T(8,128)(2,1)}, u32[]{:S(2)}, u32[]{:S(2)}) %collective-permute-start.6) | collective-permute-done | bytes 172064 | tf_op jit(solution)/shard_map/ppermute | solution.py:500
  45.8 2.0 collective-permute-done.8.refs_14_
  48.6 1.8 multiply_sine_fusion
  51.3 27.2 %attention_forward.1 = (bf16[2048,768]{1,0:T(8,128)(2,1)}, bf16[3,128,2048]{2,1,0:T(8,128)(2,1)}, bf16[3,64,2048]{2,1,0:T(8,128)(2,1)}, bf16[3,80,2048]{2,1,0:T(...) custom-call(s32[4]{0:T(128)} %get-tuple-element.179.low_ref, ...), custom_call_target="tpu_custom_call" | custom-call | flops 4026531840 | bytes 12582912 | tf_op jit(solution)/shard_map/attention_forward/pallas_call | solution.py:377
  79.2 2.0 collective-permute-done.11
  81.2 1.4 add_convert_fusion.3
  84.4 18.2 %collective-permute-done.12 = bf16[512,768]{1,0:T(8,128)(2,1)S(1)} collective-permute-done((bf16[512,768]{1,0:T(8,128)(2,1)S(1)}, bf16[512,768]{1,0:T(8,128)(2,1)S(1)}, u32[]{:S(2)}, u32[]{:S(2)}) %collective-permute-start.12) | collective-permute-done | bytes 786464 | tf_op jit(solution)/shard_map/ppermute | solution.py:500
  104.1 1.0 copy-done.19
  105.1 1.4 collective-permute-done.13.refs_1_
  106.4 11.2 %mlp.1 = (bf16[512,768]{1,0:T(8,128)(2,1)}, bf16[512,768]{1,0:T(8,128)(2,1)}, bf16[1024,640]{1,0:T(8,128)(2,1)}, bf16[1024,1280]{1,0:T(8,128)(2,1)}, bf16[384,576]{1,0:T(8,128)(2,1)}, /*index=5*/bf16[384,576]{1,0:T(8,128)(2,1)}) custom-call(s32[1]{0:T(128)} %bitcast.me_ref, bf16[512,768]{1,0:T(8,128)(2,1)} %copy-done.6, ...), custom_call_target="tpu_custom_call" | custom-call | flops 6039797760 | bytes 6291456 | tf_op jit(solution)/shard_map/mlp/pallas_call | solution.py:447
  117.8 2.4 collective-permute-done.16
  120.2 1.9 fusion.10
  122.1 1.8 fusion.15
  124.1 2.3 collective-permute-start.21
  126.9 0.9 copy-done.17
  127.8 8.4 %mlp_late.1 = (bf16[512,768]{1,0:T(8,128)(2,1)}, bf16[512,768]{1,0:T(8,128)(2,1)}, bf16[384,1152]{1,0:T(8,128)(2,1)}, bf16[384,1152]{1,0:T(8,128)(2,1)}) custom-call(s32[1]{0:T(128)} %bitcast.me_ref, bf16[512,768]{1,0:T(8,128)(2,1)} %copy-done.6, bf16[512,768]{1,0:T(8,128)(2,1)} %collective-permute-done.13.refs_1_, ...), custom_call_target="tpu_custom_call" | custom-call | flops 3019898880 | bytes 6291456 | tf_op jit(solution)/shard_map/mlp_late/pallas_call | solution.py:476
  136.4 1.8 collective-permute-start.20
  138.8 1.3 add_convert_fusion.5
  140.2 5.8 %collective-permute-done.18.refs_2_ = bf16[512,768]{1,0:T(8,128)(2,1)} collective-permute-done((bf16[512,768]{1,0:T(8,128)(2,1)S(1)}, bf16[512,768]{1,0:T(8,128)(2,1)}, u32[]{:S(2)}, u32[]{:S(2)}) %collective-permute-start.18) | collective-permute-done | bytes 786464 | tf_op jit(solution)/shard_map/ppermute | solution.py:500
  146.0 2.4 add_convert_fusion.2
  148.5 10.3 %collective-permute-done.20 = bf16[384,1152]{1,0:T(8,128)(2,1)S(1)} collective-permute-done((bf16[384,1152]{1,0:T(8,128)(2,1)}, bf16[384,1152]{1,0:T(8,128)(2,1)S(1)}, u32[]{:S(2)}, u32[]{:S(2)}) %collective-permute-start.20) | collective-permute-done | bytes 884768 | tf_op jit(solution)/shard_map/ppermute | solution.py:500
  159.2 1.7 collective-permute-start.23
  160.9 1.9 collective-permute-start.24
  163.7 35.4 %attention_backward.1 = (bf16[512,768]{1,0:T(8,128)(2,1)}, bf16[512,768]{1,0:T(8,128)(2,1)}, bf16[512,768]{1,0:T(8,128)(2,1)}, bf16[512,768]{1,0:T(8,128)(2,1)},...) custom-call(s32[8]{0:T(128)} %get-tuple-element.181.low_ref, s32[8]{0:T(128)} %get-tuple-element.180.high_ref, ...), custom_call_target="tpu_custom_call" | custom-call | flops 38654705664 | bytes 18874368 | tf_op jit(solution)/shard_map/attention_backward/pallas_call | solution.py:413
  199.2 3.0 %collective-permute-start.29 = (bf16[384,768]{1,0:T(8,128)(2,1)}, bf16[384,768]{1,0:T(8,128)(2,1)S(1)}, u32[]{:S(2)}, u32[]{:S(2)}) collective-permute-start(bf16[384,768]{1,0:T(8,128)(2,1)} %get-tuple-element.107), channel_id=1, source_target_pairs={{0,4},{4,0},{8,12},{12,8},{16,20},{20,16},{24,28},{28,24},{1,5},{5... | collective-permute-start | bytes 1769480 | tf_op jit(solution)/shard_map/ppermute | solution.py:500
  202.3 2.3 add_convert_fusion.1
  206.4 9.9 %collective-permute-done.29 = bf16[384,768]{1,0:T(8,128)(2,1)S(1)} collective-permute-done((bf16[384,768]{1,0:T(8,128)(2,1)}, bf16[384,768]{1,0:T(8,128)(2,1)S(1)}, u32[]{:S(2)}, u32[]{:S(2)}) %collective-permute-start.29) | collective-permute-done | bytes 589856 | tf_op jit(solution)/shard_map/ppermute | solution.py:500
  217.2 1.7 collective-permute-start.31
  218.9 2.0 collective-permute-start.32
  221.8 2.7 %collective-permute-done.30 = bf16[96,768]{1,0:T(8,128)(2,1)S(1)} collective-permute-done((bf16[96,768]{1,0:T(8,128)(2,1)S(1)}, bf16[96,768]{1,0:T(8,128)(2,1)S(1)}, u32[]{:S(2)}, u32[]{:S(2)}) %collective-permute-start.30) | collective-permute-done | bytes 147488 | tf_op jit(solution)/shard_map/ppermute | solution.py:500
  224.9 6.3 %collective-permute-done.31 = bf16[96,768]{1,0:T(8,128)(2,1)S(1)} collective-permute-done((bf16[96,768]{1,0:T(8,128)(2,1)S(1)}, bf16[96,768]{1,0:T(8,128)(2,1)S(1)}, u32[]{:S(2)}, u32[]{:S(2)}) %collective-permute-start.31) | collective-permute-done | bytes 147488 | tf_op jit(solution)/shard_map/ppermute | solution.py:500
  233.3 1.4 maximum_add_fusion
  235.5 1.3 collective-permute-start.36
  240.6 1.7 fusion.8
  (157 shorter events, 25.5 us)
Async XLA Ops:
  7.2 99.3 %all-gather.2.cloned.1.call-start = ((), (), s32[]{:S(2)}) async-start(), calls=%async_computation | async-start | bytes 3317760 | tf_op jit(solution)/shard_map/all_gather | solution.py:595
  7.2 10.2 %collective-permute-start = (bf16[512,768]{1,0:T(8,128)(2,1)}, bf16[512,768]{1,0:T(8,128)(2,1)S(1)}, u32[]{:S(2)}, u32[]{:S(2)}) collective-permute-start(bf16[512,768]{1,0:T(8,128)(2,1)} %refs_0_.1), channel_id=1, source_target_pairs={{0,1},{1,0},{2,3},{3,2},{4,5},{5,4},{6,7},{7,6},{8,9},{9,8},{10,11... | collective-permute-start | bytes 2359304 | tf_op jit(solution)/shard_map/ppermute | solution.py:500
  7.7 20.9 %collective-permute-start.1 = (bf16[512,768]{1,0:T(8,128)(2,1)}, bf16[512,768]{1,0:T(8,128)(2,1)S(1)}, u32[]{:S(2)}, u32[]{:S(2)}) collective-permute-start(bf16[512,768]{1,0:T(8,128)(2,1)} %refs_0_.1), channel_id=1, source_target_pairs={{0,2},{1,3},{2,0},{3,1},{4,6},{5,7},{6,4},{7,5},{8,10},{9,11},{10,... | collective-permute-start | bytes 2359304 | tf_op jit(solution)/shard_map/ppermute | solution.py:500
  14.8 35.6 %copy-start.13 = (s32[2048]{0:T(1024)}, s32[2048]{0:T(1024)S(1)}, u32[]{:S(2)}) copy-start(s32[2048]{0:T(1024)S(1)} %convert_reduce_fusion.1) | copy-start | bytes 24580
  17.4 33.1 %copy-start.12 = (bf16[96,896]{1,0:T(8,128)(2,1)}, bf16[96,896]{1,0:T(8,128)(2,1)S(1)}, u32[]{:S(2)}) copy-start(bf16[96,896]{1,0:T(8,128)(2,1)S(1)} %maximum_maximum_fusion.refs_7_) | copy-start | bytes 516100
  17.4 33.1 %copy-start.15 = (bf16[512,768]{1,0:T(8,128)(2,1)}, bf16[512,768]{1,0:T(8,128)(2,1)S(1)}, u32[]{:S(2)}) copy-start(bf16[512,768]{1,0:T(8,128)(2,1)S(1)} %collective-permute-done.refs_1_) | copy-start | bytes 2359300
  17.4 15.1 %collective-permute-start.3 = (bf16[96,896]{1,0:T(8,128)(2,1)S(1)}, bf16[96,896]{1,0:T(8,128)(2,1)S(1)}, u32[]{:S(2)}, u32[]{:S(2)}) collective-permute-start(bf16[96,896]{1,0:T(8,128)(2,1)S(1)} %maximum_maximum_fusion.refs_7_), channel_id=1, source_target_pairs={{0,8},{4,12},{8,0},{12,4},{16,24},{20,28},{24,16},{28,20},{1,9},{5... | collective-permute-start | bytes 516104 | tf_op jit(solution)/shard_map/ppermute | solution.py:500
  19.0 15.5 %collective-permute-start.5 = (bf16[96,896]{1,0:T(8,128)(2,1)S(1)}, bf16[96,896]{1,0:T(8,128)(2,1)S(1)}, u32[]{:S(2)}, u32[]{:S(2)}) collective-permute-start(bf16[96,896]{1,0:T(8,128)(2,1)S(1)} %maximum_maximum_fusion.refs_7_), channel_id=1, source_target_pairs={{0,16},{4,20},{8,24},{12,28},{16,0},{20,4},{24,8},{28,12},{1,17},{... | collective-permute-start | bytes 516104 | tf_op jit(solution)/shard_map/ppermute | solution.py:500
  21.6 14.4 %collective-permute-start.7 = (bf16[96,896]{1,0:T(8,128)(2,1)S(1)}, bf16[96,896]{1,0:T(8,128)(2,1)S(1)}, u32[]{:S(2)}, u32[]{:S(2)}) collective-permute-start(bf16[96,896]{1,0:T(8,128)(2,1)S(1)} %maximum_maximum_fusion.refs_7_), channel_id=1, source_target_pairs={{0,24},{4,28},{8,16},{12,20},{16,8},{20,12},{24,0},{28,4},{1,25},{... | collective-permute-start | bytes 516104 | tf_op jit(solution)/shard_map/ppermute | solution.py:500
  28.7 21.8 %copy-start.16 = (bf16[512,768]{1,0:T(8,128)(2,1)}, bf16[512,768]{1,0:T(8,128)(2,1)S(1)}, u32[]{:S(2)}) copy-start(bf16[512,768]{1,0:T(8,128)(2,1)S(1)} %collective-permute-done.1.refs_2_) | copy-start | bytes 2359300
  28.7 7.9 %collective-permute-start.15 = (bf16[96,864]{1,0:T(8,128)(2,1)S(1)}, bf16[96,864]{1,0:T(8,128)(2,1)S(1)}, u32[]{:S(2)}, u32[]{:S(2)}) collective-permute-start(bf16[96,864]{1,0:T(8,128)(2,1)S(1)} %pad_maximum_fusion.5), channel_id=1, source_target_pairs={{0,2},{1,3},{2,0},{3,1},{4,6},{5,7},{6,4},{7,5},{8,10},{9,11},{10,... | collective-permute-start | bytes 497672 | tf_op jit(solution)/shard_map/ppermute | solution.py:500
  31.0 7.3 %collective-permute-start.2 = (bf16[96,896]{1,0:T(8,128)(2,1)S(1)}, bf16[96,896]{1,0:T(8,128)(2,1)S(1)}, u32[]{:S(2)}, u32[]{:S(2)}) collective-permute-start(bf16[96,896]{1,0:T(8,128)(2,1)S(1)} %maximum_maximum_fusion.refs_7_), channel_id=1, source_target_pairs={{0,4},{4,0},{8,12},{12,8},{16,20},{20,16},{24,28},{28,24},{1,5},{5... | collective-permute-start | bytes 516104 | tf_op jit(solution)/shard_map/ppermute | solution.py:500
  32.5 15.4 %copy-start.21 = (bf16[96,896]{1,0:T(8,128)(2,1)}, bf16[96,896]{1,0:T(8,128)(2,1)S(1)}, u32[]{:S(2)}) copy-start(bf16[96,896]{1,0:T(8,128)(2,1)S(1)} %collective-permute-done.3.refs_9_) | copy-start | bytes 516100
  32.5 9.6 %collective-permute-start.4 = (bf16[96,896]{1,0:T(8,128)(2,1)S(1)}, bf16[96,896]{1,0:T(8,128)(2,1)}, u32[]{:S(2)}, u32[]{:S(2)}) collective-permute-start(bf16[96,896]{1,0:T(8,128)(2,1)S(1)} %collective-permute-done.3.refs_9_), channel_id=1, source_target_pairs={{0,4},{4,0},{8,12},{12,8},{16,20},{20,16},{24,28},{28,24},{1,5},{5... | collective-permute-start | bytes 516104 | tf_op jit(solution)/shard_map/ppermute | solution.py:500
  34.6 13.3 %copy-start.22 = (bf16[96,896]{1,0:T(8,128)(2,1)}, bf16[96,896]{1,0:T(8,128)(2,1)S(1)}, u32[]{:S(2)}) copy-start(bf16[96,896]{1,0:T(8,128)(2,1)S(1)} %collective-permute-done.5.refs_11_) | copy-start | bytes 516100
  34.6 11.2 %collective-permute-start.6 = (bf16[96,896]{1,0:T(8,128)(2,1)S(1)}, bf16[96,896]{1,0:T(8,128)(2,1)}, u32[]{:S(2)}, u32[]{:S(2)}) collective-permute-start(bf16[96,896]{1,0:T(8,128)(2,1)S(1)} %collective-permute-done.5.refs_11_), channel_id=1, source_target_pairs={{0,4},{4,0},{8,12},{12,8},{16,20},{20,16},{24,28},{28,24},{1,5},{5... | collective-permute-start | bytes 516104 | tf_op jit(solution)/shard_map/ppermute | solution.py:500
  36.1 11.8 %copy-start.23 = (bf16[96,896]{1,0:T(8,128)(2,1)}, bf16[96,896]{1,0:T(8,128)(2,1)S(1)}, u32[]{:S(2)}) copy-start(bf16[96,896]{1,0:T(8,128)(2,1)S(1)} %collective-permute-done.7.refs_13_) | copy-start | bytes 516100
  36.1 11.7 %collective-permute-start.8 = (bf16[96,896]{1,0:T(8,128)(2,1)S(1)}, bf16[96,896]{1,0:T(8,128)(2,1)}, u32[]{:S(2)}, u32[]{:S(2)}) collective-permute-start(bf16[96,896]{1,0:T(8,128)(2,1)S(1)} %collective-permute-done.7.refs_13_), channel_id=1, source_target_pairs={{0,4},{4,0},{8,12},{12,8},{16,20},{20,16},{24,28},{28,24},{1,5},{5... | collective-permute-start | bytes 516104 | tf_op jit(solution)/shard_map/ppermute | solution.py:500
  47.9 2.5 %collective-permute-start.9 = (bf16[512,768]{1,0:T(8,128)(2,1)S(1)}, bf16[512,768]{1,0:T(8,128)(2,1)S(1)}, u32[]{:S(2)}, u32[]{:S(2)}) collective-permute-start(bf16[512,768]{1,0:T(8,128)(2,1)S(1)} %collective-permute-done.1.refs_2_), channel_id=1, source_target_pairs={{0,1},{1,0},{2,3},{3,2},{4,5},{5,4},{6,7},{7,6},{8,9},{9,8},{10,11... | collective-permute-start | bytes 2359304 | tf_op jit(solution)/shard_map/ppermute | solution.py:500
  78.6 2.7 %collective-permute-start.11 = (bf16[512,768]{1,0:T(8,128)(2,1)}, bf16[512,768]{1,0:T(8,128)(2,1)S(1)}, u32[]{:S(2)}, u32[]{:S(2)}) collective-permute-start(bf16[512,768]{1,0:T(8,128)(2,1)} %get-tuple-element.65), channel_id=1, source_target_pairs={{0,1},{1,0},{2,3},{3,2},{4,5},{5,4},{6,7},{7,6},{8,9},{9,8},{10,11... | collective-permute-start | bytes 2359304 | tf_op jit(solution)/shard_map/ppermute | solution.py:500
  79.1 5.3 %collective-permute-start.10 = (bf16[512,768]{1,0:T(8,128)(2,1)}, bf16[512,768]{1,0:T(8,128)(2,1)S(1)}, u32[]{:S(2)}, u32[]{:S(2)}) collective-permute-start(bf16[512,768]{1,0:T(8,128)(2,1)} %get-tuple-element.63), channel_id=1, source_target_pairs={{0,1},{1,0},{2,3},{3,2},{4,5},{5,4},{6,7},{7,6},{8,9},{9,8},{10,11... | collective-permute-start | bytes 2359304 | tf_op jit(solution)/shard_map/ppermute | solution.py:500
  81.2 21.3 %copy-start.5 = (bf16[512,768]{1,0:T(8,128)(2,1)S(1)}, bf16[512,768]{1,0:T(8,128)(2,1)}, u32[]{:S(2)}) copy-start(bf16[512,768]{1,0:T(8,128)(2,1)} %get-tuple-element.62) | copy-start | bytes 2359300
  82.7 19.9 %collective-permute-start.12 = (bf16[512,768]{1,0:T(8,128)(2,1)S(1)}, bf16[512,768]{1,0:T(8,128)(2,1)S(1)}, u32[]{:S(2)}, u32[]{:S(2)}) collective-permute-start(bf16[512,768]{1,0:T(8,128)(2,1)S(1)} %add_convert_fusion.3), channel_id=1, source_target_pairs={{0,2},{1,3},{2,0},{3,1},{4,6},{5,7},{6,4},{7,5},{8,10},{9,11},{10,... | collective-permute-start | bytes 2359304 | tf_op jit(solution)/shard_map/ppermute | solution.py:500
  83.3 20.8 %collective-permute-start.14 = (bf16[512,768]{1,0:T(8,128)(2,1)S(1)}, bf16[512,768]{1,0:T(8,128)(2,1)S(1)}, u32[]{:S(2)}, u32[]{:S(2)}) collective-permute-start(bf16[512,768]{1,0:T(8,128)(2,1)S(1)} %copy-done.7), channel_id=1, source_target_pairs={{0,1},{1,0},{2,3},{3,2},{4,5},{5,4},{6,7},{7,6},{8,9},{9,8},{10,11... | collective-permute-start | bytes 2359304 | tf_op jit(solution)/shard_map/ppermute | solution.py:500
  104.0 2.5 collective-permute-start.13
  117.7 2.5 %collective-permute-start.16 = (bf16[512,768]{1,0:T(8,128)(2,1)}, bf16[512,768]{1,0:T(8,128)(2,1)S(1)}, u32[]{:S(2)}, u32[]{:S(2)}) collective-permute-start(bf16[512,768]{1,0:T(8,128)(2,1)} %get-tuple-element.70), channel_id=1, source_target_pairs={{0,1},{1,0},{2,3},{3,2},{4,5},{5,4},{6,7},{7,6},{8,9},{9,8},{10,11... | collective-permute-start | bytes 2359304 | tf_op jit(solution)/shard_map/ppermute | solution.py:500
  124.0 12.3 %copy-start.9 = (bf16[512,768]{1,0:T(8,128)(2,1)}, bf16[512,768]{1,0:T(8,128)(2,1)S(1)}, u32[]{:S(2)}) copy-start(bf16[512,768]{1,0:T(8,128)(2,1)S(1)} %get-tuple-element.81.refs_0_) | copy-start | bytes 2359300
  124.0 2.9 %collective-permute-start.17 = (bf16[512,768]{1,0:T(8,128)(2,1)S(1)}, bf16[512,768]{1,0:T(8,128)(2,1)S(1)}, u32[]{:S(2)}, u32[]{:S(2)}) collective-permute-start(bf16[512,768]{1,0:T(8,128)(2,1)S(1)} %get-tuple-element.81.refs_0_), channel_id=1, source_target_pairs={{0,1},{1,0},{2,3},{3,2},{4,5},{5,4},{6,7},{7,6},{8,9},{9,8},{10,11... | collective-permute-start | bytes 2359304 | tf_op jit(solution)/shard_map/ppermute | solution.py:500
  124.1 14.7 %collective-permute-start.21 = (bf16[384,576]{1,0:T(8,128)(2,1)}, bf16[384,576]{1,0:T(8,128)(2,1)}, u32[]{:S(2)}, u32[]{:S(2)}) collective-permute-start(bf16[384,576]{1,0:T(8,128)(2,1)} %get-tuple-element.77), channel_id=1, source_target_pairs={{0,4},{4,0},{8,12},{12,8},{16,20},{20,16},{24,28},{28,24},{1,5},{5... | collective-permute-start | bytes 1327112 | tf_op jit(solution)/shard_map/ppermute | solution.py:500
  126.4 19.6 %collective-permute-start.18 = (bf16[512,768]{1,0:T(8,128)(2,1)S(1)}, bf16[512,768]{1,0:T(8,128)(2,1)}, u32[]{:S(2)}, u32[]{:S(2)}) collective-permute-start(bf16[512,768]{1,0:T(8,128)(2,1)S(1)} %get-tuple-element.81.refs_0_), channel_id=1, source_target_pairs={{0,2},{1,3},{2,0},{3,1},{4,6},{5,7},{6,4},{7,5},{8,10},{9,11},{10,... | collective-permute-start | bytes 2359304 | tf_op jit(solution)/shard_map/ppermute | solution.py:500
  136.2 9.8 %collective-permute-start.22 = (bf16[512,768]{1,0:T(8,128)(2,1)}, bf16[512,768]{1,0:T(8,128)(2,1)}, u32[]{:S(2)}, u32[]{:S(2)}) collective-permute-start(bf16[512,768]{1,0:T(8,128)(2,1)} %get-tuple-element.79), channel_id=1, source_target_pairs={{0,1},{1,0},{2,3},{3,2},{4,5},{5,4},{6,7},{7,6},{8,9},{9,8},{10,11... | collective-permute-start | bytes 2359304 | tf_op jit(solution)/shard_map/ppermute | solution.py:500
  136.4 22.3 %collective-permute-start.20 = (bf16[384,1152]{1,0:T(8,128)(2,1)}, bf16[384,1152]{1,0:T(8,128)(2,1)S(1)}, u32[]{:S(2)}, u32[]{:S(2)}) collective-permute-start(bf16[384,1152]{1,0:T(8,128)(2,1)} %get-tuple-element.75), channel_id=1, source_target_pairs={{0,4},{4,0},{8,12},{12,8},{16,20},{20,16},{24,28},{28,24},{1,5},{5... | collective-permute-start | bytes 2654216 | tf_op jit(solution)/shard_map/ppermute | solution.py:500
  146.0 13.2 %collective-permute-start.19 = (bf16[512,768]{1,0:T(8,128)(2,1)}, bf16[512,768]{1,0:T(8,128)(2,1)S(1)}, u32[]{:S(2)}, u32[]{:S(2)}) collective-permute-start(bf16[512,768]{1,0:T(8,128)(2,1)} %collective-permute-done.18.refs_2_), channel_id=1, source_target_pairs={{0,1},{1,0},{2,3},{3,2},{4,5},{5,4},{6,7},{7,6},{8,9},{9,8},{10,11... | collective-permute-start | bytes 2359304 | tf_op jit(solution)/shard_map/ppermute | solution.py:500
  146.0 12.7 %copy-start.4 = (bf16[384,1152]{1,0:T(8,128)(2,1)S(1)}, bf16[384,1152]{1,0:T(8,128)(2,1)}, u32[]{:S(2)}) copy-start(bf16[384,1152]{1,0:T(8,128)(2,1)} %get-tuple-element.74) | copy-start | bytes 2654212
  159.2 39.8 %collective-permute-start.23 = (bf16[96,1728]{1,0:T(8,128)(2,1)S(1)}, bf16[96,1728]{1,0:T(8,128)(2,1)S(1)}, u32[]{:S(2)}, u32[]{:S(2)}) collective-permute-start(bf16[96,1728]{1,0:T(8,128)(2,1)S(1)} %pad_maximum_fusion.1), channel_id=1, source_target_pairs={{0,8},{4,12},{8,0},{12,4},{16,24},{20,28},{24,16},{28,20},{1,9},{5... | collective-permute-start | bytes 995336 | tf_op jit(solution)/shard_map/ppermute | solution.py:500
  160.9 38.2 %collective-permute-start.24 = (bf16[96,1728]{1,0:T(8,128)(2,1)S(1)}, bf16[96,1728]{1,0:T(8,128)(2,1)S(1)}, u32[]{:S(2)}, u32[]{:S(2)}) collective-permute-start(bf16[96,1728]{1,0:T(8,128)(2,1)S(1)} %pad_maximum_fusion.2), channel_id=1, source_target_pairs={{0,16},{4,20},{8,24},{12,28},{16,0},{20,4},{24,8},{28,12},{1,17},{... | collective-permute-start | bytes 995336 | tf_op jit(solution)/shard_map/ppermute | solution.py:500
  162.8 36.2 %collective-permute-start.25 = (bf16[96,1728]{1,0:T(8,128)(2,1)S(1)}, bf16[96,1728]{1,0:T(8,128)(2,1)S(1)}, u32[]{:S(2)}, u32[]{:S(2)}) collective-permute-start(bf16[96,1728]{1,0:T(8,128)(2,1)S(1)} %pad_maximum_fusion.3), channel_id=1, source_target_pairs={{0,24},{4,28},{8,16},{12,20},{16,8},{20,12},{24,0},{28,4},{1,25},{... | collective-permute-start | bytes 995336 | tf_op jit(solution)/shard_map/ppermute | solution.py:500
  199.1 3.2 %collective-permute-start.27 = (bf16[512,768]{1,0:T(8,128)(2,1)}, bf16[512,768]{1,0:T(8,128)(2,1)S(1)}, u32[]{:S(2)}, u32[]{:S(2)}) collective-permute-start(bf16[512,768]{1,0:T(8,128)(2,1)} %get-tuple-element.104), channel_id=1, source_target_pairs={{0,1},{1,0},{2,3},{3,2},{4,5},{5,4},{6,7},{7,6},{8,9},{9,8},{10,11... | collective-permute-start | bytes 2359304 | tf_op jit(solution)/shard_map/ppermute | solution.py:500
  199.2 17.1 %collective-permute-start.29 = (bf16[384,768]{1,0:T(8,128)(2,1)}, bf16[384,768]{1,0:T(8,128)(2,1)S(1)}, u32[]{:S(2)}, u32[]{:S(2)}) collective-permute-start(bf16[384,768]{1,0:T(8,128)(2,1)} %get-tuple-element.107), channel_id=1, source_target_pairs={{0,4},{4,0},{8,12},{12,8},{16,20},{20,16},{24,28},{28,24},{1,5},{5... | collective-permute-start | bytes 1769480 | tf_op jit(solution)/shard_map/ppermute | solution.py:500
  202.1 37.0 %collective-permute-start.26 = (bf16[512,768]{1,0:T(8,128)(2,1)}, bf16[512,768]{1,0:T(8,128)(2,1)S(1)}, u32[]{:S(2)}, u32[]{:S(2)}) collective-permute-start(bf16[512,768]{1,0:T(8,128)(2,1)} %get-tuple-element.102), channel_id=1, source_target_pairs={{0,1},{1,0},{2,3},{3,2},{4,5},{5,4},{6,7},{7,6},{8,9},{9,8},{10,11... | collective-permute-start | bytes 2359304 | tf_op jit(solution)/shard_map/ppermute | solution.py:500
  204.6 34.6 %collective-permute-start.28 = (bf16[512,768]{1,0:T(8,128)(2,1)}, bf16[512,768]{1,0:T(8,128)(2,1)S(1)}, u32[]{:S(2)}, u32[]{:S(2)}) collective-permute-start(bf16[512,768]{1,0:T(8,128)(2,1)} %add_convert_fusion.1), channel_id=1, source_target_pairs={{0,2},{1,3},{2,0},{3,1},{4,6},{5,7},{6,4},{7,5},{8,10},{9,11},{10,... | collective-permute-start | bytes 2359304 | tf_op jit(solution)/shard_map/ppermute | solution.py:500
  216.5 8.1 %collective-permute-start.30 = (bf16[96,768]{1,0:T(8,128)(2,1)S(1)}, bf16[96,768]{1,0:T(8,128)(2,1)S(1)}, u32[]{:S(2)}, u32[]{:S(2)}) collective-permute-start(bf16[96,768]{1,0:T(8,128)(2,1)S(1)} %get-tuple-element.156), channel_id=1, source_target_pairs={{0,8},{4,12},{8,0},{12,4},{16,24},{20,28},{24,16},{28,20},{1,9},{5... | collective-permute-start | bytes 442376 | tf_op jit(solution)/shard_map/ppermute | solution.py:500
  217.2 14.0 %collective-permute-start.31 = (bf16[96,768]{1,0:T(8,128)(2,1)S(1)}, bf16[96,768]{1,0:T(8,128)(2,1)S(1)}, u32[]{:S(2)}, u32[]{:S(2)}) collective-permute-start(bf16[96,768]{1,0:T(8,128)(2,1)S(1)} %get-tuple-element.158), channel_id=1, source_target_pairs={{0,16},{4,20},{8,24},{12,28},{16,0},{20,4},{24,8},{28,12},{1,17},{... | collective-permute-start | bytes 442376 | tf_op jit(solution)/shard_map/ppermute | solution.py:500
  218.9 12.3 %collective-permute-start.32 = (bf16[96,768]{1,0:T(8,128)(2,1)S(1)}, bf16[96,768]{1,0:T(8,128)(2,1)S(1)}, u32[]{:S(2)}, u32[]{:S(2)}) collective-permute-start(bf16[96,768]{1,0:T(8,128)(2,1)S(1)} %get-tuple-element.157), channel_id=1, source_target_pairs={{0,24},{4,28},{8,16},{12,20},{16,8},{20,12},{24,0},{28,4},{1,25},{... | collective-permute-start | bytes 442376 | tf_op jit(solution)/shard_map/ppermute | solution.py:500
  224.5 8.8 %collective-permute-start.33 = (bf16[96,864]{1,0:T(8,128)(2,1)}, bf16[96,864]{1,0:T(8,128)(2,1)}, u32[]{:S(2)}, u32[]{:S(2)}) collective-permute-start(bf16[96,864]{1,0:T(8,128)(2,1)} %pad_maximum_fusion.6), channel_id=1, source_target_pairs={{0,2},{1,3},{2,0},{3,1},{4,6},{5,7},{6,4},{7,5},{8,10},{9,11},{10,... | collective-permute-start | bytes 497672 | tf_op jit(solution)/shard_map/ppermute | solution.py:500
  234.8 3.6 %collective-permute-start.34 = (f32[2,96]{1,0:T(2,128)S(1)}, f32[2,96]{1,0:T(2,128)S(1)}, u32[]{:S(2)}, u32[]{:S(2)}) collective-permute-start(f32[2,96]{1,0:T(2,128)S(1)} %maximum_divide_fusion), channel_id=1, source_target_pairs={{0,1},{1,0},{2,3},{3,2},{4,5},{5,4},{6,7},{7,6},{8,9},{9,8},{10,11... | collective-permute-start | bytes 2312 | tf_op jit(solution)/shard_map/ppermute | solution.py:500
  234.9 3.6 %collective-permute-start.35 = (f32[2,96]{1,0:T(2,128)S(1)}, f32[2,96]{1,0:T(2,128)S(1)}, u32[]{:S(2)}, u32[]{:S(2)}) collective-permute-start(f32[2,96]{1,0:T(2,128)S(1)} %maximum_divide_fusion), channel_id=1, source_target_pairs={{0,2},{1,3},{2,0},{3,1},{4,6},{5,7},{6,4},{7,5},{8,10},{9,11},{10,... | collective-permute-start | bytes 2312 | tf_op jit(solution)/shard_map/ppermute | solution.py:500
  235.5 3.0 %collective-permute-start.36 = (f32[2,96]{1,0:T(2,128)S(1)}, f32[2,96]{1,0:T(2,128)S(1)}, u32[]{:S(2)}, u32[]{:S(2)}) collective-permute-start(f32[2,96]{1,0:T(2,128)S(1)} %maximum_divide_fusion), channel_id=1, source_target_pairs={{0,3},{1,2},{2,1},{3,0},{4,7},{5,6},{6,5},{7,4},{8,11},{9,10},{10,... | collective-permute-start | bytes 2312 | tf_op jit(solution)/shard_map/ppermute | solution.py:500
  (15 other events, 64.8 us)
Sparse Core Ops, SparseCore 0:
  47.9 58.4 all-gather.1

commit v5 on v4

--- a/solution.py
+++ b/solution.py
@@ -86,11 +86,11 @@
     toks = refs[:4]
     seg_ref, cos_ref, sin_ref = refs[4:7]
     shards_in = refs[7 : 7 + blocks]
-    normed_ref, query_ref, keys_ref, values_ref, ctx_ref, log_ref, wproj_ref = refs[
-        7 + blocks : 14 + blocks
+    normed_ref, query_ref, keys_ref, nat_ref, values_ref, wproj_ref = refs[
+        7 + blocks : 13 + blocks
     ]
-    attns = refs[14 + blocks : 18 + blocks]
-    nat_ref, flat_ref, part_ref = refs[18 + blocks :]
+    attended = refs[13 + blocks : 17 + blocks]
+    flat_ref = refs[17 + blocks]
     group = normed_ref.shape[0]
     heads = query_ref.shape[0]
     lanes = heads * HEAD_DIM
@@ -146,11 +146,30 @@
         for head in range(heads):
             nat_ref[head, here, :] = keys[head].T
 
+    attend_slots(
+        (2, 3), me, low_ref, high_ref, query_ref, nat_ref, values_ref, wproj_ref, *attended
+    )
+
+
+def forward_own_kernel(low_ref, high_ref, me_ref, query_ref, nat_ref, values_ref, wproj_ref, *outs):
+    attend_slots(
+        (0, 1), me_ref[0], low_ref, high_ref, query_ref, nat_ref, values_ref, wproj_ref, *outs
+    )
+
+
+def attend_slots(
+    slots, me, low_ref, high_ref, query_ref, nat_ref, values_ref, wproj_ref, ctx_ref, log_ref, *attns
+):
+    heads, _, group = query_ref.shape
+    lanes = heads * HEAD_DIM
+    parts = 8
+    wide = group // 4
+    split = wide // TILE
     every = range(heads)
 
-    @pl.loop(0, 4)
-    def attend(step):
-        here = pl.ds(pl.multiple_of((step ^ me) * wide, wide), wide)
+    for index, slot in enumerate(slots):
+        step = slot ^ me
+        here = slice(slot * wide, (slot + 1) * wide)
 
         def inner(at, carry):
             there = tile(slot_of(at, me, split))
@@ -172,28 +191,26 @@
         totals = [acc[HEAD_DIM : HEAD_DIM + 1] for acc in accs]
         ctx = [acc[:HEAD_DIM] / total for acc, total in zip(accs, totals)]
         ctx = jnp.concatenate(ctx, axis=0).astype(BF16)
-        ctx_ref[:, here] = ctx
+        where = slice(index * wide, (index + 1) * wide)
+        ctx_ref[:, where] = ctx
         logs = [top + jnp.log(total) for top, total in zip(tops, totals)]
-        log_ref[:, here] = jnp.concatenate(
+        log_ref[:, where] = jnp.concatenate(
             logs + [jnp.zeros((8 - heads, wide), F32)], axis=0
         )
-        part_ref[here, :] = mm(ctx.T, wproj_ref[3 * lanes : 4 * lanes, :]).astype(BF16)
-
-    for index in range(4):
-        attns[index][...] = part_ref[index * wide : (index + 1) * wide, :]
+        attns[index][...] = mm(ctx.T, wproj_ref[3 * lanes : 4 * lanes, :]).astype(BF16)
 
 
 def backward_kernel(ring, low_ref, high_ref, me_ref, *refs):
     dattn = refs[:4]
-    (
-        normed_ref, query_ref, keys_ref, values_ref, ctx_ref, log_ref, wproj_ref,
-        seg_ref, cos_ref, sin_ref,
-    ) = refs[4:14]
-    dnormeds = refs[14:18]
-    grads = refs[18:-9]
-    qx_ref, kx_ref, vx_ref, dx_ref, dq_ref, dmix_ref, all_ref, tall_ref, flat_ref = refs[-9:]
+    normed_ref, query_ref, keys_ref, kx_ref, values_ref, wproj_ref = refs[4:10]
+    ctxs = refs[10:14:2]
+    log_refs = refs[11:14:2]
+    cos_ref, sin_ref = refs[14:16]
+    dnormeds = refs[16:20]
+    grads = refs[20:-8]
+    qx_ref, vx_ref, dx_ref, dq_ref, dmix_ref, all_ref, tall_ref, flat_ref = refs[-8:]
     group = normed_ref.shape[0]
-    lanes = ctx_ref.shape[0]
+    lanes = ctxs[0].shape[0]
     heads = lanes // HEAD_DIM
     parts = 8
     count = group // TILE
@@ -210,16 +227,14 @@
     upcoming = pull_context(0)
     for slot in range(count):
         here = slice(slot * TILE, (slot + 1) * TILE)
-        there = tile(slot_of(slot, me, split))
         d_ctx = upcoming.astype(BF16).astype(F32)
         if slot + 1 < count:
             upcoming = pull_context(slot + 1)
-        ctx = ctx_ref[:, here].astype(F32)
-        segment = seg_ref[:, there]
-        same = (segment == lax.broadcasted_iota(jnp.int32, (parts, TILE), 0)).astype(F32)
+        inside = slice(slot % (2 * split) * TILE, (slot % (2 * split) + 1) * TILE)
+        ctx = ctxs[slot // (2 * split)][:, inside].astype(F32)
+        logs = log_refs[slot // (2 * split)][:, inside]
         ones = jnp.ones((parts, TILE), F32)
         blank = jnp.zeros((parts - 3, TILE), F32)
-        logs = log_ref[:, here]
         natural = []
         for head in every:
             rows = slice(head * HEAD_DIM, (head + 1) * HEAD_DIM)
@@ -228,15 +243,11 @@
             log = -logs[head : head + 1]
             query = query_ref[head, : HEAD_DIM + parts, here].astype(F32)
             qx_ref[head, :, here] = extend(query, [*pieces_of(log), blank]).astype(BF16)
-            key = keys_ref[head, :, here].astype(F32)
             value = values_ref[head, :HEAD_DIM, here].astype(F32)
-            natural.append(
-                (extend(key, [same, ones]).astype(BF16), extend(value, [ones]).astype(BF16))
-            )
+            natural.append(extend(value, [ones]).astype(BF16))
             dq_ref[head, :, here] = jnp.zeros((HEAD_DIM, TILE), F32)
         for head in every:
-            kx_ref[head, here, :] = natural[head][0].T
-            vx_ref[head, here, :] = natural[head][1].T
+            vx_ref[head, here, :] = natural[head].T
 
     def turned_back(grad, where):
         cosine = cos_ref[:, where]
@@ -289,7 +300,10 @@
     for step in range(3):
         rows = slice(step * lanes, (step + 1) * lanes)
         tall_ref[rows, :] = mm(dmix_ref[rows, :], normed_ref[...]).astype(BF16)
-    tall_ref[3 * lanes :, :] = mm(ctx_ref[...], all_ref[...]).astype(BF16)
+    tall_ref[3 * lanes :, :] = sum(
+        mm(ctx[...], all_ref[index * group // 2 : (index + 1) * group // 2, :])
+        for index, ctx in enumerate(ctxs)
+    ).astype(BF16)
     flat_ref[...] = tall_ref[...].T
     store_slabs(me_ref[1], ring, flat_ref, grads)
 
@@ -302,12 +316,12 @@
 
 def mlp_kernel(ring, me_ref, *refs):
     own_ref, near_ref, cot_ref, cot_near_ref, rest_ref = refs[:5]
-    d_own_ref, d_near_ref, hidden_ref, d_both_ref = refs[5:9]
-    grads = refs[9:-3]
-    pair_ref, cots_ref, flat_ref = refs[-3:]
+    d_own_ref, d_near_ref, hidden_ref = refs[5:8]
+    grads = refs[8:-5]
+    pair_ref, rows_ref, cots_ref, d_both_ref, flat_ref = refs[-5:]
     rows, model = own_ref.shape
     wide = hidden_ref.shape[1]
-    units = flat_ref.shape[1]
+    units = flat_ref.shape[1] // 3
     count = 2 * rows // TILE
     half = count // 2
 
@@ -316,6 +330,7 @@
         normed = (own_ref, near_ref)[slot // half][inside, :]
         cot = (cot_ref, cot_near_ref)[slot // half][inside, :]
         cots_ref[:, slot * TILE : (slot + 1) * TILE] = cot.T
+        rows_ref[:, slot * TILE : (slot + 1) * TILE] = normed.T
         return mm(normed, rest_ref[:, : 2 * wide]), mm(cot, rest_ref[:, 2 * wide :])
 
     upcoming = start(0)
@@ -338,25 +353,28 @@
         d_both_ref[here, wide:] = d_gate
         d_normed = mm(d_up, pair_ref[:wide, :]) + mm(d_gate, pair_ref[wide:, :])
         (d_own_ref, d_near_ref)[slot // half][inside, :] = d_normed.astype(BF16)
-    flat_ref[...] = mm(cots_ref[...], hidden_ref[...])[:, :units].astype(BF16)
-    store_slabs(me_ref[0], ring, flat_ref, grads)
-
-
-def mlp_late_kernel(ring, me_ref, *refs):
-    own_ref, near_ref, hidden_ref, d_both_ref, rest_ref, out_own_ref, out_near_ref = refs[:7]
-    grads = refs[7:-3]
-    rows_ref, last_ref, flat_ref = refs[-3:]
+    grad = mm(rows_ref[...], d_both_ref[...]).astype(BF16)
+    last = mm(cots_ref[...], hidden_ref[...]).astype(BF16)
+    flat_ref[:, : 2 * units] = jnp.concatenate(
+        [grad[:, :units], grad[:, wide : wide + units]], axis=1
+    )
+    flat_ref[:, 2 * units :] = last[:, :units]
+    store_slabs(me_ref[0], ring, flat_ref.at[:, : 2 * units], grads[:2] if len(grads) > 2 else grads[:1])
+    if len(grads) == 2:
+        grads[1][...] = flat_ref[:, 2 * units :]
+    else:
+        slab = model // ring
+        for index in range(ring):
+            place = pl.multiple_of((me_ref[0] ^ index) * slab, slab)
+            target = slice(index % 2 * slab, (index % 2 + 1) * slab)
+            grads[2 + index // 2][target, :] = flat_ref[pl.ds(place, slab), 2 * units :]
+
+
+def down_kernel(hidden_ref, rest_ref, own_ref, near_ref, last_ref):
     rows = own_ref.shape[0]
-    wide = hidden_ref.shape[1]
-    units = flat_ref.shape[1] // 2
-    rows_ref[:, :rows] = own_ref[...].T
-    rows_ref[:, rows:] = near_ref[...].T
-    grad = mm(rows_ref[...], d_both_ref[...]).astype(BF16)
-    flat_ref[...] = jnp.concatenate([grad[:, :units], grad[:, wide : wide + units]], axis=1)
-    store_slabs(me_ref[0], ring, flat_ref, grads)
-    last_ref[...] = rest_ref[:, 2 * wide :].T
-    out_own_ref[...] = mm(hidden_ref[:rows, :], last_ref[...]).astype(BF16)
-    out_near_ref[...] = mm(hidden_ref[rows:, :], last_ref[...]).astype(BF16)
+    last_ref[...] = rest_ref[:, 2 * hidden_ref.shape[1] :].T
+    own_ref[...] = mm(hidden_ref[:rows, :], last_ref[...]).astype(BF16)
+    near_ref[...] = mm(hidden_ref[rows:, :], last_ref[...]).astype(BF16)
 
 
 def vmem_spec():
@@ -380,33 +398,54 @@
             shape((group, model), BF16),
             shape((heads, WIDE, group), BF16),
             shape((heads, HEAD_DIM, group), BF16),
+            shape((heads, group, WIDE), BF16),
             shape((heads, HEAD_DIM + 16, group), BF16),
-            shape((lanes, group), BF16),
-            shape((8, group), F32),
             shape((width, model), BF16),
-            *[shape((rows, model), BF16) for _ in range(4)],
+            shape((lanes, group // 2), BF16),
+            shape((8, group // 2), F32),
+            *[shape((rows, model), BF16) for _ in range(2)],
         ),
         in_specs=[smem_spec()] * 3 + [vmem_spec()] * (7 + blocks),
-        out_specs=[vmem_spec()] * 11,
-        scratch_shapes=[
-            pltpu.VMEM((heads, group, WIDE), BF16),
-            pltpu.VMEM((model, width), BF16),
-            pltpu.VMEM((group, model), BF16),
-        ],
+        out_specs=[vmem_spec()] * 10,
+        scratch_shapes=[pltpu.VMEM((model, width), BF16)],
         compiler_params=pltpu.CompilerParams(vmem_limit_bytes=VMEM_BYTES),
         cost_estimate=pl.CostEstimate(
-            flops=2 * group * model * lanes * 4 + 2 * group * group * lanes,
-            bytes_accessed=group * model * 8,
-            transcendentals=group * group,
+            flops=group * model * lanes,
+            bytes_accessed=group * model,
+            transcendentals=0,
         ),
         name="attention_forward",
     )(low, high, me, *toks, seg, cosine, sine, *shards_in)
 
 
-def attention_backward(ring, direct, low, high, me, d_attn, kept, seg, cosine, sine):
+def attention_forward_own(low, high, me, query, nat, values, proj_t):
+    heads, _, group = query.shape
+    model = proj_t.shape[1]
+    rows = group // 4
+    shape = jax.ShapeDtypeStruct
+    return pl.pallas_call(
+        forward_own_kernel,
+        out_shape=(
+            shape((heads * HEAD_DIM, group // 2), BF16),
+            shape((8, group // 2), F32),
+            *[shape((rows, model), BF16) for _ in range(2)],
+        ),
+        in_specs=[smem_spec()] * 3 + [vmem_spec()] * 4,
+        out_specs=[vmem_spec()] * 4,
+        compiler_params=pltpu.CompilerParams(vmem_limit_bytes=VMEM_BYTES),
+        cost_estimate=pl.CostEstimate(
+            flops=group * model * heads * HEAD_DIM,
+            bytes_accessed=group * model,
+            transcendentals=0,
+        ),
+        name="attention_forward_own",
+    )(low, high, me, query, nat, values, proj_t)
+
+
+def attention_backward(ring, direct, low, high, me, d_attn, kept, cosine, sine):
     rows, model = d_attn[0].shape
     group = 4 * rows
-    lanes = kept[4].shape[0]
+    lanes = kept[6].shape[0]
     heads = lanes // HEAD_DIM
     shape = jax.ShapeDtypeStruct
     outs = 2 if direct else 1
@@ -416,11 +455,10 @@
             *[shape((rows, model), BF16) for _ in range(4)],
             *[shape((model // outs, 4 * lanes), BF16) for _ in range(outs)],
         ),
-        in_specs=[smem_spec()] * 3 + [vmem_spec()] * 14,
+        in_specs=[smem_spec()] * 3 + [vmem_spec()] * 16,
         out_specs=[vmem_spec()] * (4 + outs),
         scratch_shapes=[
             pltpu.VMEM((heads, WIDE, group), BF16),
-            pltpu.VMEM((heads, group, WIDE), BF16),
             pltpu.VMEM((heads, group, WIDE), BF16),
             pltpu.VMEM((heads, WIDE, group), BF16),
             pltpu.VMEM((heads, HEAD_DIM, group), F32),
@@ -436,13 +474,14 @@
             transcendentals=group * group,
         ),
         name="attention_backward",
-    )(low, high, me, *d_attn, *kept, seg, cosine, sine)
+    )(low, high, me, *d_attn, *kept, cosine, sine)
 
 
 def mlp(ring, direct, spot, rows_in, cots, rest, units):
     rows, model = rows_in[0].shape
     wide = rest.shape[1] // 3
     outs = 2 if direct else 1
+    lasts = ring // 2 if direct else 1
     shape = jax.ShapeDtypeStruct
     return pl.pallas_call(
         functools.partial(mlp_kernel, ring),
@@ -450,15 +489,17 @@
             shape((rows, model), BF16),
             shape((rows, model), BF16),
             shape((2 * rows, wide), BF16),
-            shape((2 * rows, 2 * wide), BF16),
-            *[shape((model // outs, units), BF16) for _ in range(outs)],
+            *[shape((model // outs, 2 * units), BF16) for _ in range(outs)],
+            *[shape((model // lasts, units), BF16) for _ in range(lasts)],
         ),
         in_specs=[smem_spec()] + [vmem_spec()] * 5,
-        out_specs=[vmem_spec()] * (4 + outs),
+        out_specs=[vmem_spec()] * (3 + outs + lasts),
         scratch_shapes=[
             pltpu.VMEM((2 * wide, model), BF16),
             pltpu.VMEM((model, 2 * rows), BF16),
-            pltpu.VMEM((model, units), BF16),
+            pltpu.VMEM((model, 2 * rows), BF16),
+            pltpu.VMEM((2 * rows, 2 * wide), BF16),
+            pltpu.VMEM((model, 3 * units), BF16),
         ],
         compiler_params=pltpu.CompilerParams(vmem_limit_bytes=VMEM_BYTES),
         cost_estimate=pl.CostEstimate(
@@ -468,31 +509,22 @@
     )(spot, *rows_in, *cots, rest)
 
 
-def mlp_late(ring, direct, spot, rows_in, hidden, d_both, rest, units):
-    rows, model = rows_in[0].shape
-    wide = hidden.shape[1]
-    outs = 2 if direct else 1
-    shape = jax.ShapeDtypeStruct
+def down(hidden, rest):
+    rows, wide = hidden.shape
+    model = rest.shape[0]
+    out = jax.ShapeDtypeStruct((rows // 2, model), BF16)
     return pl.pallas_call(
-        functools.partial(mlp_late_kernel, ring),
-        out_shape=(
-            shape((rows, model), BF16),
-            shape((rows, model), BF16),
-            *[shape((model // outs, 2 * units), BF16) for _ in range(outs)],
-        ),
-        in_specs=[smem_spec()] + [vmem_spec()] * 5,
-        out_specs=[vmem_spec()] * (2 + outs),
-        scratch_shapes=[
-            pltpu.VMEM((model, 2 * rows), BF16),
-            pltpu.VMEM((wide, model), BF16),
-            pltpu.VMEM((model, 2 * units), BF16),
-        ],
+        down_kernel,
+        out_shape=(out, out),
+        in_specs=[vmem_spec()] * 2,
+        out_specs=[vmem_spec()] * 2,
+        scratch_shapes=[pltpu.VMEM((wide, model), BF16)],
         compiler_params=pltpu.CompilerParams(vmem_limit_bytes=VMEM_BYTES),
         cost_estimate=pl.CostEstimate(
-            flops=12 * rows * model * wide, bytes_accessed=rows * model * 16, transcendentals=0
-        ),
-        name="mlp_late",
-    )(spot, *rows_in, hidden, d_both, rest)
+            flops=2 * rows * model * wide, bytes_accessed=rows * model * 6, transcendentals=0
+        ),
+        name="down",
+    )(hidden, rest)
 
 
 def swap(value, axis, bit):
@@ -505,11 +537,12 @@
     return (rows, swap(rows, "tp", 1), far, swap(far, "tp", 1))
 
 
-def scatter_rows(own, near, far, corner):
-    far_sum = (far.astype(F32) + swap(corner, "tp", 1).astype(F32)).astype(BF16)
-    came = swap(far_sum, "tp", 2)
-    mine = own.astype(F32) + swap(near, "tp", 1).astype(F32)
-    return mine + came.astype(F32), far_sum
+def sum_far(far, corner):
+    return (far.astype(F32) + swap(corner, "tp", 1).astype(F32)).astype(BF16)
+
+
+def sum_rows(own, near, came):
+    return own.astype(F32) + swap(near, "tp", 1).astype(F32) + came.astype(F32)
 
 
 def pair_sum(own, near):
@@ -574,14 +607,13 @@
     )
     far = swap(tokens, "tp", 2)
     near = swap(tokens, "tp", 1)
+    seq_lengths, w_in, w_down = lax.optimization_barrier((seq_lengths, w_in, w_down, far))[:3]
     if direct:
         first_parts = gather_slabs(after(first, near))
     else:
         first_parts = [lax.all_gather(first, "fsdp", axis=0, tiled=True)]
-    corner = swap(after(far, *first_parts), "tp", 1)
-    toks = (tokens, near, far, corner)
     mine = jnp.concatenate([w_in[0], w_in[1], w_down.T], axis=1)
-    other = swap(after(mine, far), "tp", 2)
+    other = swap(mine, "tp", 2)
     spare = jnp.zeros((slab, -2 * units % WIDE), BF16)
     rest = jnp.concatenate(
         [
@@ -591,7 +623,9 @@
         ],
         axis=1,
     )
-    rest = after(rest, *first_parts)
+    rest = after(rest, *first_parts[::2])
+    corner = swap(after(far, rest, *first_parts), "tp", 1)
+    toks = (tokens, near, far, corner)
     whole_rest = lax.all_gather(rest, "fsdp", axis=0, tiled=True)
 
     segment, place, seq_first, seq_last = positions(seq_lengths[0], group)
@@ -603,19 +637,26 @@
     seg = segment[None, :]
     me = jnp.stack([lax.axis_index("tp"), at_fsdp]).astype(jnp.int32)
 
-    *kept, proj_t, own, near, far, corner = attention_forward(
+    *kept, proj_t, ctx_far, log_far, far, corner = attention_forward(
         low_wide, high_wide, me, toks, seg, cosine, sine, first_parts, lanes
     )
+    far_sum = sum_far(far, corner)
+    normed1, query, keys, nat, values = kept
+    ctx_own, log_own, own, near = attention_forward_own(
+        low_wide, high_wide, me, after(query, far_sum), nat, values, proj_t
+    )
+    kept = (normed1, query, keys, nat, values, proj_t, ctx_own, log_own, ctx_far, log_far)
     gain_one = proj_t[4 * lanes : 4 * lanes + 1].astype(F32)
     gain_two = proj_t[4 * lanes + 1 : 4 * lanes + 2].astype(F32)
     inputs = tokens.astype(F32)
     cots = (cotangent, swap(cotangent, "tp", 1))
-    h_mid = inputs + scatter_rows(own, near, far, corner)[0]
+    near, came = lax.optimization_barrier((near, swap(far_sum, "tp", 2)))
+    h_mid = inputs + sum_rows(own, near, came)
     normal2, inverse2 = center_rows(h_mid)
     normed2 = (normal2 * gain_two).astype(BF16)
     full2 = (normed2, swap(normed2, "tp", 1))
     spot = me[1:]
-    d_own, d_near, hidden, d_both, *last_halves = mlp(
+    d_own, d_near, hidden, *early = mlp(
         ring, direct, spot, full2, cots, whole_rest, 2 * units
     )
     d_normed2 = pair_sum(d_own, d_near)
@@ -623,34 +664,42 @@
     d_low = d_mid.astype(BF16)
     d_attn = gather_rows(d_low)
 
-    out_own, out_near, *pair_halves = mlp_late(
-        ring, direct, spot, full2, after(hidden, d_attn[1]), d_both, whole_rest, 2 * units
-    )
+    out_own, out_near = down(after(hidden, d_attn[1]), whole_rest)
     output = (h_mid + pair_sum(out_own, out_near)).astype(BF16)
     if direct:
-        pair_sums = pair_slabs(*pair_halves).reshape(ring // 2, slab, 4 * units)
-        last_sums = pair_slabs(*last_halves).reshape(ring // 2, slab, 2 * units)
-        sums = [
-            jnp.concatenate([pair_sums[at], last_sums[at]], axis=1) for at in range(ring // 2)
-        ]
-        d_attn, sums, output = lax.optimization_barrier((d_attn, sums, output))
+        came = lax.optimization_barrier((early[3:], d_attn[1]))[0]
+        came = [swap(part, "fsdp", 2 * at) for at, part in enumerate(came, 1)]
+        sent = swap(early[1], "fsdp", 1)
+        sent, came, out_own = lax.optimization_barrier((sent, came, out_own))
+        sums = (early[0].astype(F32) + sent.astype(F32)).astype(BF16)
+        sums = [sums[at * slab : (at + 1) * slab] for at in range(ring // 2)]
+        last_sums = sum([part.astype(F32) for part in came], early[2].astype(F32)).astype(BF16)
+        d_attn, sums, last_sums, output = lax.optimization_barrier(
+            (d_attn, sums, last_sums, output)
+        )
         sums = [sums[0]] + [swap(sums[at], "fsdp", 2 * at) for at in range(1, ring // 2)]
+        sums = sums + [last_sums[:slab], swap(last_sums[slab:], "fsdp", 1)]
 
     d_parts = attention_backward(
-        ring, direct, low, high, me, d_attn, (*kept, proj_t), seg, cosine, sine
+        ring, direct, low, high, me, d_attn, kept, cosine, sine
     )
     if direct:
         d_parts, sums = lax.optimization_barrier((d_parts, sums))
     late = d_parts[4:]
-    d_normed1, far_sum = scatter_rows(*d_parts[:4])
+    far_sum = sum_far(*d_parts[2:4])
+    d_normed1 = sum_rows(*d_parts[:2], swap(far_sum, "tp", 2))
     if direct:
-        sum_early = after(sums[0], far_sum).astype(F32)
-        for at in range(1, ring // 2):
-            sum_early = sum_early + sums[at].astype(F32)
+        sums = lax.optimization_barrier((sums, far_sum))[0]
+        sum_early = jnp.concatenate(
+            [
+                sum(part.astype(F32) for part in sums[: ring // 2]),
+                sums[-2].astype(F32) + sums[-1].astype(F32),
+            ],
+            axis=1,
+        )
         own_late = scatter_slabs(pair_slabs(after(late[0], far_sum), late[1]))
     else:
-        early = jnp.concatenate([pair_halves[0], last_halves[0]], axis=1)
-        sum_early = lax.psum_scatter(early, "fsdp", scatter_dimension=0, tiled=True)
+        sum_early = lax.psum_scatter(jnp.concatenate(early, axis=1), "fsdp", scatter_dimension=0, tiled=True)
         own_late = lax.psum_scatter(late[0], "fsdp", scatter_dimension=0, tiled=True).astype(F32)
     halves = [
         jnp.concatenate(

time: 250 us -> 261 us (1.044)
  starting transfers between devices: 35 us -> 48.1 us
  local copies, waits for them, and re-layouts: 13.6 us -> 24 us
  waiting for transfers between devices: 77.6 us -> 71.1 us
  Pallas kernels: 82.3 us -> 76.3 us
    ppermute x37 -> x40, waiting for transfers between devices: 77.5 us -> 63.1 us  [swap(): return lax.ppermute(value, axis, [(i, i ^ bit) for i in range(size)])]
    ppermute x37 -> x40, starting transfers between devices: 35 us -> 48.1 us  [swap(): return lax.ppermute(value, axis, [(i, i ^ bit) for i in range(size)])]
    pallas_call x1, Pallas kernels: 27.2 us -> 15.5 us  [attention_forward(): pl.pallas_call(functools.partial(forward_kernel, blocks), out_shape=(shap...]
    slice x1, local copies, waits for them, and re-layouts: 0.09 us -> 9.72 us  [shards(): low = seq_first[::TILE] // TILE]
    all_gather x1, waiting for transfers between devices: 0.01 us -> 7.95 us  [shards(): whole_rest = lax.all_gather(rest, 'fsdp', axis=0, tiled=True)]
    pallas_call x1 -> x2, Pallas kernels: 8.45 us -> 15.7 us  [the longest x1 11 us: attention_forward_own(): pl.pallas_call(forward_own_kernel, out_shape=(shape((heads * HEAD_DIM, gr...]
    pallas_call x1, Pallas kernels: 35.4 us -> 30.7 us  [attention_backward(): pl.pallas_call(functools.partial(backward_kernel, ring), out_shape=(*[sha...]
    pallas_call x1, Pallas kernels: 11.2 us -> 14.5 us  [mlp(): pl.pallas_call(functools.partial(mlp_kernel, ring), out_shape=(shape((row...]
  transfers between devices with their start and end apart: 38 -> 41, of which waited for: 16 -> 18; matrix products, arithmetic and copies ran while one was open for 12% -> 15% of each run, Pallas kernels for 29% -> 24%
where the time goes in v5:
time: 261 us; the launch traced here: 258 us
  Pallas kernels  76.3 us (29%)
  waiting for transfers between devices  71.1 us (27%)
  starting transfers between devices  48.1 us (18%)
  local copies, waits for them, and re-layouts  24 us (9%)
  other arithmetic  23.4 us (9%)
  between operations  14.7 us (6%)
    ppermute x40, waiting for transfers between devices, swap(): return lax.ppermute(value, axis, [(i, i ^ bit) for i in range(size)])  63.1 us
    ppermute x40, starting transfers between devices, swap(): return lax.ppermute(value, axis, [(i, i ^ bit) for i in range(size)])  48.1 us
    pallas_call x1, Pallas kernels, attention_backward(): pl.pallas_call(functools.partial(backward_kernel, ring), out_shape=(*[sha...  30.7 us
    pallas_call x1, Pallas kernels, attention_forward(): pl.pallas_call(functools.partial(forward_kernel, blocks), out_shape=(shap...  15.5 us
    pallas_call x1, Pallas kernels, mlp(): pl.pallas_call(functools.partial(mlp_kernel, ring), out_shape=(shape((row...  14.5 us
    pallas_call x1, Pallas kernels, attention_forward_own(): pl.pallas_call(forward_own_kernel, out_shape=(shape((heads * HEAD_DIM, gr...  11 us
    slice x1, local copies, waits for them, and re-layouts, shards(): low = seq_first[::TILE] // TILE  9.72 us
    all_gather x1, waiting for transfers between devices, shards(): whole_rest = lax.all_gather(rest, 'fsdp', axis=0, tiled=True)  7.95 us
  transfers between devices with their start and end apart: 41, of which 18 were waited for; matrix products, arithmetic and copies ran while one was open for 15% of the time, Pallas kernels for 24%

profile of v5, /device:TPU:0, one launch (start us, length us, event | category | flops | bytes accessed | tf_op | source)
XLA Modules:
  0.0 257.7 jit_solution(14435243223037139069)
XLA Ops:
  7.7 2.6 %collective-permute-start = (bf16[512,768]{1,0:T(8,128)(2,1)}, bf16[512,768]{1,0:T(8,128)(2,1)S(1)}, u32[]{:S(2)}, u32[]{:S(2)}) collective-permute-start(bf16[512,768]{1,0:T(8,128)(2,1)} %refs_0_.1), channel_id=1, source_target_pairs={{0,2},{1,3},{2,0},{3,1},{4,6},{5,7},{6,4},{7,5},{8,10},{9,11},{10,... | collective-permute-start | bytes 2359304 | tf_op jit(solution)/shard_map/ppermute | solution.py:532
  14.1 1.6 collective-permute-start.3
  15.7 2.6 %collective-permute-start.4 = (bf16[96,896]{1,0:T(8,128)(2,1)S(1)}, bf16[96,896]{1,0:T(8,128)(2,1)S(1)}, u32[]{:S(2)}, u32[]{:S(2)}) collective-permute-start(bf16[96,896]{1,0:T(8,128)(2,1)S(1)} %maximum_maximum_fusion.refs_7_), channel_id=1, source_target_pairs={{0,16},{4,20},{8,24},{12,28},{16,0},{20,4},{24,8},{28,12},{1,17},{... | collective-permute-start | bytes 516104 | tf_op jit(solution)/shard_map/ppermute | solution.py:532
  18.5 1.5 collective-permute-start.6
  20.0 8.7 %collective-permute-done.refs_2_ = bf16[512,768]{1,0:T(8,128)(2,1)S(1)} collective-permute-done((bf16[512,768]{1,0:T(8,128)(2,1)}, bf16[512,768]{1,0:T(8,128)(2,1)S(1)}, u32[]{:S(2)}, u32[]{:S(2)}) %collective-permute-start) | collective-permute-done | bytes 786464 | tf_op jit(solution)/shard_map/ppermute | solution.py:532
  28.7 1.1 slice_bitcast_fusion.4
  30.9 1.8 collective-permute-start.2
  33.3 1.6 collective-permute-start.7
  35.4 1.5 collective-permute-start.9
  38.2 2.5 collective-permute-done.7.refs_10_
  40.7 3.8 %collective-permute-done.8.refs_12_ = bf16[96,896]{1,0:T(8,128)(2,1)} collective-permute-done((bf16[96,896]{1,0:T(8,128)(2,1)S(1)}, bf16[96,896]{1,0:T(8,128)(2,1)}, u32[]{:S(2)}, u32[]{:S(2)}) %collective-permute-start.8) | collective-permute-done | bytes 172064 | tf_op jit(solution)/shard_map/ppermute | solution.py:532
  44.5 2.0 collective-permute-done.9.refs_14_
  47.1 1.8 multiply_sine_fusion
  49.9 15.5 %attention_forward.1 = (bf16[2048,768]{1,0:T(8,128)(2,1)}, bf16[3,128,2048]{2,1,0:T(8,128)(2,1)}, bf16[3,64,2048]{2,1,0:T(8,128)(2,1)}, bf16[3,2048,128]{2,1,0:T...) custom-call(s32[4]{0:T(128)} %get-tuple-element.223.low_ref, ...), custom_call_target="tpu_custom_call" | custom-call | flops 301989888 | bytes 1572864 | tf_op jit(solution)/shard_map/attention_forward/pallas_call | solution.py:395
  66.0 2.1 collective-permute-done.11
  68.1 1.4 add_convert_fusion.3
  69.5 2.0 collective-permute-start.12
  71.5 11.0 %attention_forward_own.1 = (bf16[192,1024]{1,0:T(8,128)(2,1)}, f32[8,1024]{1,0:T(8,128)}, bf16[512,768]{1,0:T(8,128)(2,1)}, bf16[512,768]{1,0:T(8,128)(2,1)}) custom-call(s32[4]{0:T(128)} %get-tuple-element.223.low_ref, s32[4]{0:T(128)} %get-tuple-element.222.high_ref, s32[2]{0:T(128)} %pad_add_fusion.me_ref, ...), custom_call_target="tpu_custom_call" | custom-call | flops 301989888 | bytes 1572864 | tf_op jit(solution)/shard_map/attention_forward_own/pallas_call | solution.py:426
  82.5 7.1 %collective-permute-done.12 = bf16[512,768]{1,0:T(8,128)(2,1)S(1)} collective-permute-done((bf16[512,768]{1,0:T(8,128)(2,1)S(1)}, bf16[512,768]{1,0:T(8,128)(2,1)S(1)}, u32[]{:S(2)}, u32[]{:S(2)}) %collective-permute-start.12) | collective-permute-done | bytes 786464 | tf_op jit(solution)/shard_map/ppermute | solution.py:532
  91.1 2.0 collective-permute-done.13
  93.1 1.9 fusion.16
  96.8 1.4 collective-permute-done.14.refs_1_
  98.1 8.0 %all-gather.2.cloned.1.call-done.refs_4_.rest_ref = bf16[768,1920]{1,0:T(8,128)(2,1)} async-done(((bf16[96,1920]{1,0:T(8,128)(2,1)}), bf16[768,1920]{1,0:T(8,128)(2,1)}) %all-gather.2.cloned.1.call-update) | async-done | bytes 2949136 | tf_op jit(solution)/shard_map/all_gather | solution.py:629
  106.1 14.5 %mlp.1 = (bf16[512,768]{1,0:T(8,128)(2,1)}, bf16[512,768]{1,0:T(8,128)(2,1)}, bf16[1024,640]{1,0:T(8,128)(2,1)}, bf16[384,1152]{1,0:T(8,128)(2,1)}, bf16[384,115...) custom-call(s32[1]{0:T(128)} %bitcast.me_ref, ...), custom_call_target="tpu_custom_call" | custom-call | flops 6039797760 | bytes 6291456 | tf_op jit(solution)/shard_map/mlp/pallas_call | solution.py:486
  120.6 2.5 collective-permute-done.16
  123.0 1.9 fusion.10
  125.0 2.1 fusion.15
  127.8 1.5 collective-permute-start.18
  129.3 9.7 %slice.116 = s32[8]{0:T(128)S(1)} slice(s32[2048]{0:T(1024)S(1)} %get-tuple-element.189), slice={[0:2048:256]} | slice | bytes 64 | tf_op jit(solution)/shard_map/slice | solution.py:633
  139.1 1.5 collective-permute-start.21
  141.7 1.9 collective-permute-start.23
  144.1 4.7 %down.1 = (bf16[512,768]{1,0:T(8,128)(2,1)}, bf16[512,768]{1,0:T(8,128)(2,1)}) custom-call(bf16[1024,640]{1,0:T(8,128)(2,1)} %get-tuple-element.112.hidden_ref, bf16[768,1920]{1,0:T(8,128)(2,1)} %all-gather.2.cloned.1.call-done.refs_4_.rest_ref), custom_call_target="tpu_custom_call" | custom-call | flops 1006632960 | bytes 4718592 | tf_op jit(solution)/shard_map/down/pallas_call | solution.py:516
  149.9 1.4 collective-permute-done.21
  151.3 9.9 %collective-permute-done.22 = bf16[192,576]{1,0:T(8,128)(2,1)S(1)} collective-permute-done((bf16[192,576]{1,0:T(8,128)(2,1)}, bf16[192,576]{1,0:T(8,128)(2,1)S(1)}, u32[]{:S(2)}, u32[]{:S(2)}) %collective-permute-start.22) | collective-permute-done | bytes 221216 | tf_op jit(solution)/shard_map/ppermute | solution.py:532
  162.6 1.2 add_convert_fusion.2
  163.8 1.5 collective-permute-start.28
  165.4 4.4 %collective-permute-start.25 = (bf16[96,1152]{1,0:T(8,128)(2,1)S(1)}, bf16[96,1152]{1,0:T(8,128)(2,1)S(1)}, u32[]{:S(2)}, u32[]{:S(2)}) collective-permute-start(bf16[96,1152]{1,0:T(8,128)(2,1)S(1)} %get-tuple-element.138), channel_id=1, source_target_pairs={{0,8},{4,12},{8,0},{12,4},{16,24},{20,28},{24,16},{28,20},{1,9},{5... | collective-permute-start | bytes 663560 | tf_op jit(solution)/shard_map/ppermute | solution.py:532
  170.2 1.9 collective-permute-start.27
  172.1 30.7 %attention_backward.1 = (bf16[512,768]{1,0:T(8,128)(2,1)}, bf16[512,768]{1,0:T(8,128)(2,1)}, bf16[512,768]{1,0:T(8,128)(2,1)}, bf16[512,768]{1,0:T(8,128)(2,1)},...) custom-call(s32[8]{0:T(128)} %get-tuple-element.225.low_ref, s32[8]{0:T(128)} %get-tuple-element.224.high_ref, ...), custom_call_target="tpu_custom_call" | custom-call | flops 38654705664 | bytes 18874368 | tf_op jit(solution)/shard_map/attention_backward/pallas_call | solution.py:452
  202.9 6.9 %collective-permute-start.32 = (bf16[384,768]{1,0:T(8,128)(2,1)}, bf16[384,768]{1,0:T(8,128)(2,1)S(1)}, u32[]{:S(2)}, u32[]{:S(2)}) collective-permute-start(bf16[384,768]{1,0:T(8,128)(2,1)} %get-tuple-element.148), channel_id=1, source_target_pairs={{0,4},{4,0},{8,12},{12,8},{16,20},{20,16},{24,28},{28,24},{1,5},{5... | collective-permute-start | bytes 1769480 | tf_op jit(solution)/shard_map/ppermute | solution.py:532
  210.0 2.3 add_convert_fusion.1
  213.6 10.3 %collective-permute-done.32 = bf16[384,768]{1,0:T(8,128)(2,1)S(1)} collective-permute-done((bf16[384,768]{1,0:T(8,128)(2,1)}, bf16[384,768]{1,0:T(8,128)(2,1)S(1)}, u32[]{:S(2)}, u32[]{:S(2)}) %collective-permute-start.32) | collective-permute-done | bytes 589856 | tf_op jit(solution)/shard_map/ppermute | solution.py:532
  224.1 2.3 collective-permute-start.33
  226.6 2.3 collective-permute-start.35
  231.5 8.2 %collective-permute-done.34 = bf16[96,768]{1,0:T(8,128)(2,1)S(1)} collective-permute-done((bf16[96,768]{1,0:T(8,128)(2,1)S(1)}, bf16[96,768]{1,0:T(8,128)(2,1)S(1)}, u32[]{:S(2)}, u32[]{:S(2)}) %collective-permute-start.34) | collective-permute-done | bytes 147488 | tf_op jit(solution)/shard_map/ppermute | solution.py:532
  241.7 1.4 maximum_add_fusion
  244.0 1.2 collective-permute-start.39
  249.0 1.7 fusion.8
  (163 shorter events, 29.9 us)
Async XLA Ops:
  7.2 25.5 %copy-start.24 = (s32[1,8]{1,0:T(1,128)S(1)}, s32[1,8]{1,0:T(1,128)}, u32[]{:S(2)}) copy-start(s32[1,8]{1,0:T(1,128)} %param.9) | copy-start | bytes 100
  7.2 98.9 %all-gather.2.cloned.1.call-start = ((), (), s32[]{:S(2)}) async-start(), calls=%async_computation | async-start | bytes 3317760 | tf_op jit(solution)/shard_map/all_gather | solution.py:629
  7.2 6.8 %collective-permute-start.1 = (bf16[512,768]{1,0:T(8,128)(2,1)}, bf16[512,768]{1,0:T(8,128)(2,1)S(1)}, u32[]{:S(2)}, u32[]{:S(2)}) collective-permute-start(bf16[512,768]{1,0:T(8,128)(2,1)} %refs_0_.1), channel_id=1, source_target_pairs={{0,1},{1,0},{2,3},{3,2},{4,5},{5,4},{6,7},{7,6},{8,9},{9,8},{10,11... | collective-permute-start | bytes 2359304 | tf_op jit(solution)/shard_map/ppermute | solution.py:532
  7.7 20.9 %collective-permute-start = (bf16[512,768]{1,0:T(8,128)(2,1)}, bf16[512,768]{1,0:T(8,128)(2,1)S(1)}, u32[]{:S(2)}, u32[]{:S(2)}) collective-permute-start(bf16[512,768]{1,0:T(8,128)(2,1)} %refs_0_.1), channel_id=1, source_target_pairs={{0,2},{1,3},{2,0},{3,1},{4,6},{5,7},{6,4},{7,5},{8,10},{9,11},{10,... | collective-permute-start | bytes 2359304 | tf_op jit(solution)/shard_map/ppermute | solution.py:532
  14.0 34.9 %copy-start.12 = (bf16[96,896]{1,0:T(8,128)(2,1)}, bf16[96,896]{1,0:T(8,128)(2,1)S(1)}, u32[]{:S(2)}) copy-start(bf16[96,896]{1,0:T(8,128)(2,1)S(1)} %maximum_maximum_fusion.refs_7_) | copy-start | bytes 516100
  14.1 34.9 %copy-start.8 = (bf16[512,768]{1,0:T(8,128)(2,1)}, bf16[512,768]{1,0:T(8,128)(2,1)S(1)}, u32[]{:S(2)}) copy-start(bf16[512,768]{1,0:T(8,128)(2,1)S(1)} %collective-permute-done.1.refs_1_) | copy-start | bytes 2359300
  14.1 19.2 %collective-permute-start.3 = (bf16[96,896]{1,0:T(8,128)(2,1)S(1)}, bf16[96,896]{1,0:T(8,128)(2,1)S(1)}, u32[]{:S(2)}, u32[]{:S(2)}) collective-permute-start(bf16[96,896]{1,0:T(8,128)(2,1)S(1)} %maximum_maximum_fusion.refs_7_), channel_id=1, source_target_pairs={{0,8},{4,12},{8,0},{12,4},{16,24},{20,28},{24,16},{28,20},{1,9},{5... | collective-permute-start | bytes 516104 | tf_op jit(solution)/shard_map/ppermute | solution.py:532
  15.7 19.1 %collective-permute-start.4 = (bf16[96,896]{1,0:T(8,128)(2,1)S(1)}, bf16[96,896]{1,0:T(8,128)(2,1)S(1)}, u32[]{:S(2)}, u32[]{:S(2)}) collective-permute-start(bf16[96,896]{1,0:T(8,128)(2,1)S(1)} %maximum_maximum_fusion.refs_7_), channel_id=1, source_target_pairs={{0,16},{4,20},{8,24},{12,28},{16,0},{20,4},{24,8},{28,12},{1,17},{... | collective-permute-start | bytes 516104 | tf_op jit(solution)/shard_map/ppermute | solution.py:532
  18.3 17.1 %collective-permute-start.5 = (bf16[96,896]{1,0:T(8,128)(2,1)S(1)}, bf16[96,896]{1,0:T(8,128)(2,1)S(1)}, u32[]{:S(2)}, u32[]{:S(2)}) collective-permute-start(bf16[96,896]{1,0:T(8,128)(2,1)S(1)} %maximum_maximum_fusion.refs_7_), channel_id=1, source_target_pairs={{0,24},{4,28},{8,16},{12,20},{16,8},{20,12},{24,0},{28,4},{1,25},{... | collective-permute-start | bytes 516104 | tf_op jit(solution)/shard_map/ppermute | solution.py:532
  18.5 19.6 %collective-permute-start.6 = (bf16[96,896]{1,0:T(8,128)(2,1)S(1)}, bf16[96,896]{1,0:T(8,128)(2,1)S(1)}, u32[]{:S(2)}, u32[]{:S(2)}) collective-permute-start(bf16[96,896]{1,0:T(8,128)(2,1)S(1)} %maximum_maximum_fusion.refs_7_), channel_id=1, source_target_pairs={{0,4},{4,0},{8,12},{12,8},{16,20},{20,16},{24,28},{28,24},{1,5},{5... | collective-permute-start | bytes 516104 | tf_op jit(solution)/shard_map/ppermute | solution.py:532
  28.7 20.2 %copy-start.9 = (bf16[512,768]{1,0:T(8,128)(2,1)}, bf16[512,768]{1,0:T(8,128)(2,1)S(1)}, u32[]{:S(2)}) copy-start(bf16[512,768]{1,0:T(8,128)(2,1)S(1)} %collective-permute-done.refs_2_) | copy-start | bytes 2359300
  30.9 6.2 %collective-permute-start.2 = (bf16[96,864]{1,0:T(8,128)(2,1)S(1)}, bf16[96,864]{1,0:T(8,128)(2,1)S(1)}, u32[]{:S(2)}, u32[]{:S(2)}) collective-permute-start(bf16[96,864]{1,0:T(8,128)(2,1)S(1)} %pad_maximum_fusion.1), channel_id=1, source_target_pairs={{0,2},{1,3},{2,0},{3,1},{4,6},{5,7},{6,4},{7,5},{8,10},{9,11},{10,... | collective-permute-start | bytes 497672 | tf_op jit(solution)/shard_map/ppermute | solution.py:532
  33.3 7.4 %collective-permute-start.7 = (bf16[96,896]{1,0:T(8,128)(2,1)S(1)}, bf16[96,896]{1,0:T(8,128)(2,1)S(1)}, u32[]{:S(2)}, u32[]{:S(2)}) collective-permute-start(bf16[96,896]{1,0:T(8,128)(2,1)S(1)} %collective-permute-done.3.refs_9_), channel_id=1, source_target_pairs={{0,4},{4,0},{8,12},{12,8},{16,20},{20,16},{24,28},{28,24},{1,5},{5... | collective-permute-start | bytes 516104 | tf_op jit(solution)/shard_map/ppermute | solution.py:532
  34.9 9.6 %collective-permute-start.8 = (bf16[96,896]{1,0:T(8,128)(2,1)S(1)}, bf16[96,896]{1,0:T(8,128)(2,1)}, u32[]{:S(2)}, u32[]{:S(2)}) collective-permute-start(bf16[96,896]{1,0:T(8,128)(2,1)S(1)} %collective-permute-done.4.refs_11_), channel_id=1, source_target_pairs={{0,4},{4,0},{8,12},{12,8},{16,20},{20,16},{24,28},{28,24},{1,5},{5... | collective-permute-start | bytes 516104 | tf_op jit(solution)/shard_map/ppermute | solution.py:532
  35.4 11.1 %collective-permute-start.9 = (bf16[96,896]{1,0:T(8,128)(2,1)S(1)}, bf16[96,896]{1,0:T(8,128)(2,1)}, u32[]{:S(2)}, u32[]{:S(2)}) collective-permute-start(bf16[96,896]{1,0:T(8,128)(2,1)S(1)} %collective-permute-done.5.refs_13_), channel_id=1, source_target_pairs={{0,4},{4,0},{8,12},{12,8},{16,20},{20,16},{24,28},{28,24},{1,5},{5... | collective-permute-start | bytes 516104 | tf_op jit(solution)/shard_map/ppermute | solution.py:532
  46.5 2.4 collective-permute-start.10
  65.4 2.7 %collective-permute-start.11 = (bf16[512,768]{1,0:T(8,128)(2,1)}, bf16[512,768]{1,0:T(8,128)(2,1)S(1)}, u32[]{:S(2)}, u32[]{:S(2)}) collective-permute-start(bf16[512,768]{1,0:T(8,128)(2,1)} %get-tuple-element.92), channel_id=1, source_target_pairs={{0,1},{1,0},{2,3},{3,2},{4,5},{5,4},{6,7},{7,6},{8,9},{9,8},{10,11... | collective-permute-start | bytes 2359304 | tf_op jit(solution)/shard_map/ppermute | solution.py:532
  69.5 20.1 %collective-permute-start.12 = (bf16[512,768]{1,0:T(8,128)(2,1)S(1)}, bf16[512,768]{1,0:T(8,128)(2,1)S(1)}, u32[]{:S(2)}, u32[]{:S(2)}) collective-permute-start(bf16[512,768]{1,0:T(8,128)(2,1)S(1)} %add_convert_fusion.3), channel_id=1, source_target_pairs={{0,2},{1,3},{2,0},{3,1},{4,6},{5,7},{6,4},{7,5},{8,10},{9,11},{10,... | collective-permute-start | bytes 2359304 | tf_op jit(solution)/shard_map/ppermute | solution.py:532
  71.5 18.1 %copy-start.6 = (bf16[512,768]{1,0:T(8,128)(2,1)S(1)}, bf16[512,768]{1,0:T(8,128)(2,1)}, u32[]{:S(2)}) copy-start(bf16[512,768]{1,0:T(8,128)(2,1)} %refs_2_.1) | copy-start | bytes 2359300
  71.5 18.6 %copy-start = (bf16[512,768]{1,0:T(8,128)(2,1)S(1)}, bf16[512,768]{1,0:T(8,128)(2,1)}, u32[]{:S(2)}) copy-start(bf16[512,768]{1,0:T(8,128)(2,1)} %refs_0_.1) | copy-start | bytes 2359300
  89.5 3.6 %collective-permute-start.13 = (bf16[512,768]{1,0:T(8,128)(2,1)}, bf16[512,768]{1,0:T(8,128)(2,1)S(1)}, u32[]{:S(2)}, u32[]{:S(2)}) collective-permute-start(bf16[512,768]{1,0:T(8,128)(2,1)} %get-tuple-element.99), channel_id=1, source_target_pairs={{0,1},{1,0},{2,3},{3,2},{4,5},{5,4},{6,7},{7,6},{8,9},{9,8},{10,11... | collective-permute-start | bytes 2359304 | tf_op jit(solution)/shard_map/ppermute | solution.py:532
  89.5 6.3 %collective-permute-start.15 = (bf16[512,768]{1,0:T(8,128)(2,1)S(1)}, bf16[512,768]{1,0:T(8,128)(2,1)S(1)}, u32[]{:S(2)}, u32[]{:S(2)}) collective-permute-start(bf16[512,768]{1,0:T(8,128)(2,1)S(1)} %copy-done.6), channel_id=1, source_target_pairs={{0,1},{1,0},{2,3},{3,2},{4,5},{5,4},{6,7},{7,6},{8,9},{9,8},{10,11... | collective-permute-start | bytes 2359304 | tf_op jit(solution)/shard_map/ppermute | solution.py:532
  95.6 2.5 collective-permute-start.14
  120.5 2.5 collective-permute-start.16
  127.1 12.0 %collective-permute-start.17 = (bf16[512,768]{1,0:T(8,128)(2,1)}, bf16[512,768]{1,0:T(8,128)(2,1)}, u32[]{:S(2)}, u32[]{:S(2)}) collective-permute-start(bf16[512,768]{1,0:T(8,128)(2,1)} %get-tuple-element.121.refs_0_), channel_id=1, source_target_pairs={{0,1},{1,0},{2,3},{3,2},{4,5},{5,4},{6,7},{7,6},{8,9},{9,8},{10,11... | collective-permute-start | bytes 2359304 | tf_op jit(solution)/shard_map/ppermute | solution.py:532
  127.2 22.1 %collective-permute-start.20 = (bf16[384,1152]{1,0:T(8,128)(2,1)}, bf16[384,1152]{1,0:T(8,128)(2,1)S(1)}, u32[]{:S(2)}, u32[]{:S(2)}) collective-permute-start(bf16[384,1152]{1,0:T(8,128)(2,1)} %get-tuple-element.104), channel_id=1, source_target_pairs={{0,4},{4,0},{8,12},{12,8},{16,20},{20,16},{24,28},{28,24},{1,5},{5... | collective-permute-start | bytes 2654216 | tf_op jit(solution)/shard_map/ppermute | solution.py:532
  127.8 21.6 %collective-permute-start.18 = (bf16[512,768]{1,0:T(8,128)(2,1)}, bf16[512,768]{1,0:T(8,128)(2,1)}, u32[]{:S(2)}, u32[]{:S(2)}) collective-permute-start(bf16[512,768]{1,0:T(8,128)(2,1)} %get-tuple-element.121.refs_0_), channel_id=1, source_target_pairs={{0,2},{1,3},{2,0},{3,1},{4,6},{5,7},{6,4},{7,5},{8,10},{9,11},{10,... | collective-permute-start | bytes 2359304 | tf_op jit(solution)/shard_map/ppermute | solution.py:532
  139.1 12.1 %collective-permute-start.21 = (bf16[192,576]{1,0:T(8,128)(2,1)}, bf16[192,576]{1,0:T(8,128)(2,1)S(1)}, u32[]{:S(2)}, u32[]{:S(2)}) collective-permute-start(bf16[192,576]{1,0:T(8,128)(2,1)} %get-tuple-element.108), channel_id=1, source_target_pairs={{0,8},{4,12},{8,0},{12,4},{16,24},{20,28},{24,16},{28,20},{1,9},{5... | collective-permute-start | bytes 663560 | tf_op jit(solution)/shard_map/ppermute | solution.py:532
  140.7 20.5 %collective-permute-start.22 = (bf16[192,576]{1,0:T(8,128)(2,1)}, bf16[192,576]{1,0:T(8,128)(2,1)S(1)}, u32[]{:S(2)}, u32[]{:S(2)}) collective-permute-start(bf16[192,576]{1,0:T(8,128)(2,1)} %get-tuple-element.109), channel_id=1, source_target_pairs={{0,16},{4,20},{8,24},{12,28},{16,0},{20,4},{24,8},{28,12},{1,17},{... | collective-permute-start | bytes 663560 | tf_op jit(solution)/shard_map/ppermute | solution.py:532
  141.7 19.5 %collective-permute-start.23 = (bf16[192,576]{1,0:T(8,128)(2,1)}, bf16[192,576]{1,0:T(8,128)(2,1)S(1)}, u32[]{:S(2)}, u32[]{:S(2)}) collective-permute-start(bf16[192,576]{1,0:T(8,128)(2,1)} %get-tuple-element.110), channel_id=1, source_target_pairs={{0,24},{4,28},{8,16},{12,20},{16,8},{20,12},{24,0},{28,4},{1,25},{... | collective-permute-start | bytes 663560 | tf_op jit(solution)/shard_map/ppermute | solution.py:532
  144.1 17.1 %copy-start.4 = (bf16[384,1152]{1,0:T(8,128)(2,1)S(1)}, bf16[384,1152]{1,0:T(8,128)(2,1)}, u32[]{:S(2)}) copy-start(bf16[384,1152]{1,0:T(8,128)(2,1)} %get-tuple-element.103) | copy-start | bytes 2654212
  149.4 12.3 %collective-permute-start.24 = (bf16[512,768]{1,0:T(8,128)(2,1)}, bf16[512,768]{1,0:T(8,128)(2,1)S(1)}, u32[]{:S(2)}, u32[]{:S(2)}) collective-permute-start(bf16[512,768]{1,0:T(8,128)(2,1)} %get-tuple-element.119), channel_id=1, source_target_pairs={{0,1},{1,0},{2,3},{3,2},{4,5},{5,4},{6,7},{7,6},{8,9},{9,8},{10,11... | collective-permute-start | bytes 2359304 | tf_op jit(solution)/shard_map/ppermute | solution.py:532
  149.4 14.4 %collective-permute-start.19 = (bf16[512,768]{1,0:T(8,128)(2,1)}, bf16[512,768]{1,0:T(8,128)(2,1)S(1)}, u32[]{:S(2)}, u32[]{:S(2)}) collective-permute-start(bf16[512,768]{1,0:T(8,128)(2,1)} %collective-permute-done.18.refs_2_), channel_id=1, source_target_pairs={{0,1},{1,0},{2,3},{3,2},{4,5},{5,4},{6,7},{7,6},{8,9},{9,8},{10,11... | collective-permute-start | bytes 2359304 | tf_op jit(solution)/shard_map/ppermute | solution.py:532
  163.8 38.9 %collective-permute-start.28 = (bf16[96,576]{1,0:T(8,128)(2,1)S(1)}, bf16[96,576]{1,0:T(8,128)(2,1)S(1)}, u32[]{:S(2)}, u32[]{:S(2)}) collective-permute-start(bf16[96,576]{1,0:T(8,128)(2,1)S(1)} %get-tuple-element.211), channel_id=1, source_target_pairs={{0,4},{4,0},{8,12},{12,8},{16,20},{20,16},{24,28},{28,24},{1,5},{5... | collective-permute-start | bytes 331784 | tf_op jit(solution)/shard_map/ppermute | solution.py:532
  165.4 37.4 %collective-permute-start.25 = (bf16[96,1152]{1,0:T(8,128)(2,1)S(1)}, bf16[96,1152]{1,0:T(8,128)(2,1)S(1)}, u32[]{:S(2)}, u32[]{:S(2)}) collective-permute-start(bf16[96,1152]{1,0:T(8,128)(2,1)S(1)} %get-tuple-element.138), channel_id=1, source_target_pairs={{0,8},{4,12},{8,0},{12,4},{16,24},{20,28},{24,16},{28,20},{1,9},{5... | collective-permute-start | bytes 663560 | tf_op jit(solution)/shard_map/ppermute | solution.py:532
  169.7 33.1 %collective-permute-start.26 = (bf16[96,1152]{1,0:T(8,128)(2,1)S(1)}, bf16[96,1152]{1,0:T(8,128)(2,1)S(1)}, u32[]{:S(2)}, u32[]{:S(2)}) collective-permute-start(bf16[96,1152]{1,0:T(8,128)(2,1)S(1)} %get-tuple-element.139), channel_id=1, source_target_pairs={{0,16},{4,20},{8,24},{12,28},{16,0},{20,4},{24,8},{28,12},{1,17},{... | collective-permute-start | bytes 663560 | tf_op jit(solution)/shard_map/ppermute | solution.py:532
  170.2 32.6 %collective-permute-start.27 = (bf16[96,1152]{1,0:T(8,128)(2,1)S(1)}, bf16[96,1152]{1,0:T(8,128)(2,1)S(1)}, u32[]{:S(2)}, u32[]{:S(2)}) collective-permute-start(bf16[96,1152]{1,0:T(8,128)(2,1)S(1)} %get-tuple-element.140), channel_id=1, source_target_pairs={{0,24},{4,28},{8,16},{12,20},{16,8},{20,12},{24,0},{28,4},{1,25},{... | collective-permute-start | bytes 663560 | tf_op jit(solution)/shard_map/ppermute | solution.py:532
  202.8 7.2 %collective-permute-start.30 = (bf16[512,768]{1,0:T(8,128)(2,1)}, bf16[512,768]{1,0:T(8,128)(2,1)S(1)}, u32[]{:S(2)}, u32[]{:S(2)}) collective-permute-start(bf16[512,768]{1,0:T(8,128)(2,1)} %get-tuple-element.145), channel_id=1, source_target_pairs={{0,1},{1,0},{2,3},{3,2},{4,5},{5,4},{6,7},{7,6},{8,9},{9,8},{10,11... | collective-permute-start | bytes 2359304 | tf_op jit(solution)/shard_map/ppermute | solution.py:532
  202.9 21.0 %collective-permute-start.32 = (bf16[384,768]{1,0:T(8,128)(2,1)}, bf16[384,768]{1,0:T(8,128)(2,1)S(1)}, u32[]{:S(2)}, u32[]{:S(2)}) collective-permute-start(bf16[384,768]{1,0:T(8,128)(2,1)} %get-tuple-element.148), channel_id=1, source_target_pairs={{0,4},{4,0},{8,12},{12,8},{16,20},{20,16},{24,28},{28,24},{1,5},{5... | collective-permute-start | bytes 1769480 | tf_op jit(solution)/shard_map/ppermute | solution.py:532
  209.8 37.8 %collective-permute-start.29 = (bf16[512,768]{1,0:T(8,128)(2,1)}, bf16[512,768]{1,0:T(8,128)(2,1)S(1)}, u32[]{:S(2)}, u32[]{:S(2)}) collective-permute-start(bf16[512,768]{1,0:T(8,128)(2,1)} %get-tuple-element.143), channel_id=1, source_target_pairs={{0,1},{1,0},{2,3},{3,2},{4,5},{5,4},{6,7},{7,6},{8,9},{9,8},{10,11... | collective-permute-start | bytes 2359304 | tf_op jit(solution)/shard_map/ppermute | solution.py:532
  212.2 35.4 %collective-permute-start.31 = (bf16[512,768]{1,0:T(8,128)(2,1)}, bf16[512,768]{1,0:T(8,128)(2,1)S(1)}, u32[]{:S(2)}, u32[]{:S(2)}) collective-permute-start(bf16[512,768]{1,0:T(8,128)(2,1)} %add_convert_fusion.1), channel_id=1, source_target_pairs={{0,2},{1,3},{2,0},{3,1},{4,6},{5,7},{6,4},{7,5},{8,10},{9,11},{10,... | collective-permute-start | bytes 2359304 | tf_op jit(solution)/shard_map/ppermute | solution.py:532
  224.1 6.8 %collective-permute-start.33 = (bf16[96,768]{1,0:T(8,128)(2,1)S(1)}, bf16[96,768]{1,0:T(8,128)(2,1)S(1)}, u32[]{:S(2)}, u32[]{:S(2)}) collective-permute-start(bf16[96,768]{1,0:T(8,128)(2,1)S(1)} %get-tuple-element.201), channel_id=1, source_target_pairs={{0,8},{4,12},{8,0},{12,4},{16,24},{20,28},{24,16},{28,20},{1,9},{5... | collective-permute-start | bytes 442376 | tf_op jit(solution)/shard_map/ppermute | solution.py:532
  226.5 13.2 %collective-permute-start.34 = (bf16[96,768]{1,0:T(8,128)(2,1)S(1)}, bf16[96,768]{1,0:T(8,128)(2,1)S(1)}, u32[]{:S(2)}, u32[]{:S(2)}) collective-permute-start(bf16[96,768]{1,0:T(8,128)(2,1)S(1)} %get-tuple-element.203), channel_id=1, source_target_pairs={{0,16},{4,20},{8,24},{12,28},{16,0},{20,4},{24,8},{28,12},{1,17},{... | collective-permute-start | bytes 442376 | tf_op jit(solution)/shard_map/ppermute | solution.py:532
  226.6 13.0 %collective-permute-start.35 = (bf16[96,768]{1,0:T(8,128)(2,1)S(1)}, bf16[96,768]{1,0:T(8,128)(2,1)S(1)}, u32[]{:S(2)}, u32[]{:S(2)}) collective-permute-start(bf16[96,768]{1,0:T(8,128)(2,1)S(1)} %get-tuple-element.202), channel_id=1, source_target_pairs={{0,24},{4,28},{8,16},{12,20},{16,8},{20,12},{24,0},{28,4},{1,25},{... | collective-permute-start | bytes 442376 | tf_op jit(solution)/shard_map/ppermute | solution.py:532
  230.9 10.8 %collective-permute-start.36 = (bf16[96,864]{1,0:T(8,128)(2,1)}, bf16[96,864]{1,0:T(8,128)(2,1)}, u32[]{:S(2)}, u32[]{:S(2)}) collective-permute-start(bf16[96,864]{1,0:T(8,128)(2,1)} %pad_maximum_fusion.2), channel_id=1, source_target_pairs={{0,2},{1,3},{2,0},{3,1},{4,6},{5,7},{6,4},{7,5},{8,10},{9,11},{10,... | collective-permute-start | bytes 497672 | tf_op jit(solution)/shard_map/ppermute | solution.py:532
  243.3 3.6 %collective-permute-start.37 = (f32[2,96]{1,0:T(2,128)S(1)}, f32[2,96]{1,0:T(2,128)S(1)}, u32[]{:S(2)}, u32[]{:S(2)}) collective-permute-start(f32[2,96]{1,0:T(2,128)S(1)} %maximum_divide_fusion), channel_id=1, source_target_pairs={{0,1},{1,0},{2,3},{3,2},{4,5},{5,4},{6,7},{7,6},{8,9},{9,8},{10,11... | collective-permute-start | bytes 2312 | tf_op jit(solution)/shard_map/ppermute | solution.py:532
  243.4 3.6 %collective-permute-start.38 = (f32[2,96]{1,0:T(2,128)S(1)}, f32[2,96]{1,0:T(2,128)S(1)}, u32[]{:S(2)}, u32[]{:S(2)}) collective-permute-start(f32[2,96]{1,0:T(2,128)S(1)} %maximum_divide_fusion), channel_id=1, source_target_pairs={{0,2},{1,3},{2,0},{3,1},{4,6},{5,7},{6,4},{7,5},{8,10},{9,11},{10,... | collective-permute-start | bytes 2312 | tf_op jit(solution)/shard_map/ppermute | solution.py:532
  244.0 3.0 %collective-permute-start.39 = (f32[2,96]{1,0:T(2,128)S(1)}, f32[2,96]{1,0:T(2,128)S(1)}, u32[]{:S(2)}, u32[]{:S(2)}) collective-permute-start(f32[2,96]{1,0:T(2,128)S(1)} %maximum_divide_fusion), channel_id=1, source_target_pairs={{0,3},{1,2},{2,1},{3,0},{4,7},{5,6},{6,5},{7,4},{8,11},{9,10},{10,... | collective-permute-start | bytes 2312 | tf_op jit(solution)/shard_map/ppermute | solution.py:532
  (18 other events, 134.6 us)
Sparse Core Ops, SparseCore 0:
  47.2 58.7 all-gather.1

commit v6 on v4

--- a/solution.py
+++ b/solution.py
@@ -343,20 +343,24 @@
 
 
 def mlp_late_kernel(ring, me_ref, *refs):
-    own_ref, near_ref, hidden_ref, d_both_ref, rest_ref, out_own_ref, out_near_ref = refs[:7]
-    grads = refs[7:-3]
-    rows_ref, last_ref, flat_ref = refs[-3:]
+    own_ref, near_ref, d_both_ref = refs[:3]
+    grads = refs[3:-2]
+    rows_ref, flat_ref = refs[-2:]
     rows = own_ref.shape[0]
-    wide = hidden_ref.shape[1]
+    wide = d_both_ref.shape[1] // 2
     units = flat_ref.shape[1] // 2
     rows_ref[:, :rows] = own_ref[...].T
     rows_ref[:, rows:] = near_ref[...].T
     grad = mm(rows_ref[...], d_both_ref[...]).astype(BF16)
     flat_ref[...] = jnp.concatenate([grad[:, :units], grad[:, wide : wide + units]], axis=1)
     store_slabs(me_ref[0], ring, flat_ref, grads)
-    last_ref[...] = rest_ref[:, 2 * wide :].T
-    out_own_ref[...] = mm(hidden_ref[:rows, :], last_ref[...]).astype(BF16)
-    out_near_ref[...] = mm(hidden_ref[rows:, :], last_ref[...]).astype(BF16)
+
+
+def down_kernel(hidden_ref, rest_ref, own_ref, near_ref, last_ref):
+    rows = own_ref.shape[0]
+    last_ref[...] = rest_ref[:, 2 * hidden_ref.shape[1] :].T
+    own_ref[...] = mm(hidden_ref[:rows, :], last_ref[...]).astype(BF16)
+    near_ref[...] = mm(hidden_ref[rows:, :], last_ref[...]).astype(BF16)
 
 
 def vmem_spec():
@@ -468,31 +472,44 @@
     )(spot, *rows_in, *cots, rest)
 
 
-def mlp_late(ring, direct, spot, rows_in, hidden, d_both, rest, units):
+def mlp_late(ring, direct, spot, rows_in, d_both, units):
     rows, model = rows_in[0].shape
-    wide = hidden.shape[1]
+    wide = d_both.shape[1] // 2
     outs = 2 if direct else 1
     shape = jax.ShapeDtypeStruct
     return pl.pallas_call(
         functools.partial(mlp_late_kernel, ring),
-        out_shape=(
-            shape((rows, model), BF16),
-            shape((rows, model), BF16),
-            *[shape((model // outs, 2 * units), BF16) for _ in range(outs)],
-        ),
-        in_specs=[smem_spec()] + [vmem_spec()] * 5,
-        out_specs=[vmem_spec()] * (2 + outs),
+        out_shape=tuple(shape((model // outs, 2 * units), BF16) for _ in range(outs)),
+        in_specs=[smem_spec()] + [vmem_spec()] * 3,
+        out_specs=(vmem_spec(),) * outs,
         scratch_shapes=[
             pltpu.VMEM((model, 2 * rows), BF16),
-            pltpu.VMEM((wide, model), BF16),
             pltpu.VMEM((model, 2 * units), BF16),
         ],
         compiler_params=pltpu.CompilerParams(vmem_limit_bytes=VMEM_BYTES),
         cost_estimate=pl.CostEstimate(
-            flops=12 * rows * model * wide, bytes_accessed=rows * model * 16, transcendentals=0
+            flops=8 * rows * model * wide, bytes_accessed=rows * model * 12, transcendentals=0
         ),
         name="mlp_late",
-    )(spot, *rows_in, hidden, d_both, rest)
+    )(spot, *rows_in, d_both)
+
+
+def down(hidden, rest):
+    rows, wide = hidden.shape
+    model = rest.shape[0]
+    out = jax.ShapeDtypeStruct((rows // 2, model), BF16)
+    return pl.pallas_call(
+        down_kernel,
+        out_shape=(out, out),
+        in_specs=[vmem_spec()] * 2,
+        out_specs=[vmem_spec()] * 2,
+        scratch_shapes=[pltpu.VMEM((wide, model), BF16)],
+        compiler_params=pltpu.CompilerParams(vmem_limit_bytes=VMEM_BYTES),
+        cost_estimate=pl.CostEstimate(
+            flops=2 * rows * model * wide, bytes_accessed=rows * model * 6, transcendentals=0
+        ),
+        name="down",
+    )(hidden, rest)
 
 
 def swap(value, axis, bit):
@@ -623,12 +640,13 @@
     d_low = d_mid.astype(BF16)
     d_attn = gather_rows(d_low)
 
-    out_own, out_near, *pair_halves = mlp_late(
-        ring, direct, spot, full2, after(hidden, d_attn[1]), d_both, whole_rest, 2 * units
+    pair_halves = mlp_late(
+        ring, direct, spot, full2, after(d_both, d_attn[1]), 2 * units
     )
+    out_own, out_near = down(after(hidden, pair_halves[0]), whole_rest)
     output = (h_mid + pair_sum(out_own, out_near)).astype(BF16)
     if direct:
-        pair_sums = pair_slabs(*pair_halves).reshape(ring // 2, slab, 4 * units)
+        pair_sums = pair_slabs(after(pair_halves[0], out_near), pair_halves[1]).reshape(ring // 2, slab, 4 * units)
         last_sums = pair_slabs(*last_halves).reshape(ring // 2, slab, 2 * units)
         sums = [
             jnp.concatenate([pair_sums[at], last_sums[at]], axis=1) for at in range(ring // 2)

time: 250 us -> 252 us (level)
    pallas_call x1 -> x2, Pallas kernels: 8.45 us -> 10.6 us  [the longest x1 6.03 us: mlp_late(): pl.pallas_call(functools.partial(mlp_late_kernel, ring), out_shape=tuple(...]
  transfers between devices with their start and end apart: 38 -> 38, of which waited for: 16 -> 19; matrix products, arithmetic and copies ran while one was open for 12% -> 12% of each run, Pallas kernels for 29% -> 29%
where the time goes in v6:
time: 252 us; the launch traced here: 251 us
  Pallas kernels  84.4 us (33%)
  waiting for transfers between devices  78.7 us (31%)
  starting transfers between devices  34.1 us (14%)
  other arithmetic  25.9 us (10%)
  between operations  14.6 us (6%)
  local copies, waits for them, and re-layouts  13.6 us (5%)
    ppermute x37, waiting for transfers between devices, swap(): return lax.ppermute(value, axis, [(i, i ^ bit) for i in range(size)])  78.3 us
    pallas_call x1, Pallas kernels, attention_backward(): pl.pallas_call(functools.partial(backward_kernel, ring), out_shape=(*[sha...  35.4 us
    ppermute x37, starting transfers between devices, swap(): return lax.ppermute(value, axis, [(i, i ^ bit) for i in range(size)])  34 us
    pallas_call x1, Pallas kernels, attention_forward(): pl.pallas_call(functools.partial(forward_kernel, blocks), out_shape=(shap...  27.2 us
    pallas_call x1, Pallas kernels, mlp(): pl.pallas_call(functools.partial(mlp_kernel, ring), out_shape=(shape((row...  11.3 us
    unnamed x56, local copies, waits for them, and re-layouts  8.46 us
    pallas_call x1, Pallas kernels, mlp_late(): pl.pallas_call(functools.partial(mlp_late_kernel, ring), out_shape=tuple(...  6.03 us
  transfers between devices with their start and end apart: 38, of which 19 were waited for; matrix products, arithmetic and copies ran while one was open for 12% of the time, Pallas kernels for 29%

profile of v6, /device:TPU:0, one launch (start us, length us, event | category | flops | bytes accessed | tf_op | source)
XLA Modules:
  0.0 251.2 jit_solution(216484494289844959)
XLA Ops:
  7.7 2.6 %collective-permute-start.1 = (bf16[512,768]{1,0:T(8,128)(2,1)}, bf16[512,768]{1,0:T(8,128)(2,1)S(1)}, u32[]{:S(2)}, u32[]{:S(2)}) collective-permute-start(bf16[512,768]{1,0:T(8,128)(2,1)} %refs_0_.1), channel_id=1, source_target_pairs={{0,2},{1,3},{2,0},{3,1},{4,6},{5,7},{6,4},{7,5},{8,10},{9,11},{10,... | collective-permute-start | bytes 2359304 | tf_op jit(solution)/shard_map/ppermute | solution.py:517
  10.3 1.1 copy.32
  15.1 1.0 copy.36
  17.4 1.6 collective-permute-start.3
  19.0 2.6 %collective-permute-start.5 = (bf16[96,896]{1,0:T(8,128)(2,1)S(1)}, bf16[96,896]{1,0:T(8,128)(2,1)S(1)}, u32[]{:S(2)}, u32[]{:S(2)}) collective-permute-start(bf16[96,896]{1,0:T(8,128)(2,1)S(1)} %maximum_maximum_fusion.refs_7_), channel_id=1, source_target_pairs={{0,16},{4,20},{8,24},{12,28},{16,0},{20,4},{24,8},{28,12},{1,17},{... | collective-permute-start | bytes 516104 | tf_op jit(solution)/shard_map/ppermute | solution.py:517
  21.8 6.8 %collective-permute-done.1.refs_2_ = bf16[512,768]{1,0:T(8,128)(2,1)S(1)} collective-permute-done((bf16[512,768]{1,0:T(8,128)(2,1)}, bf16[512,768]{1,0:T(8,128)(2,1)S(1)}, u32[]{:S(2)}, u32[]{:S(2)}) %collective-permute-start.1) | collective-permute-done | bytes 786464 | tf_op jit(solution)/shard_map/ppermute | solution.py:517
  28.7 1.8 collective-permute-start.15
  31.0 1.5 collective-permute-start.2
  33.0 1.5 collective-permute-done.5.refs_11_
  34.6 1.5 collective-permute-start.6
  36.7 1.0 concatenate.33
  38.3 3.8 %collective-permute-done.4.refs_10_ = bf16[96,896]{1,0:T(8,128)(2,1)} collective-permute-done((bf16[96,896]{1,0:T(8,128)(2,1)S(1)}, bf16[96,896]{1,0:T(8,128)(2,1)}, u32[]{:S(2)}, u32[]{:S(2)}) %collective-permute-start.4) | collective-permute-done | bytes 172064 | tf_op jit(solution)/shard_map/ppermute | solution.py:517
  42.1 3.7 %collective-permute-done.6.refs_12_ = bf16[96,896]{1,0:T(8,128)(2,1)} collective-permute-done((bf16[96,896]{1,0:T(8,128)(2,1)S(1)}, bf16[96,896]{1,0:T(8,128)(2,1)}, u32[]{:S(2)}, u32[]{:S(2)}) %collective-permute-start.6) | collective-permute-done | bytes 172064 | tf_op jit(solution)/shard_map/ppermute | solution.py:517
  45.8 2.0 collective-permute-done.8.refs_14_
  48.6 1.8 multiply_sine_fusion
  51.3 27.2 %attention_forward.1 = (bf16[2048,768]{1,0:T(8,128)(2,1)}, bf16[3,128,2048]{2,1,0:T(8,128)(2,1)}, bf16[3,64,2048]{2,1,0:T(8,128)(2,1)}, bf16[3,80,2048]{2,1,0:T(...) custom-call(s32[4]{0:T(128)} %get-tuple-element.183.low_ref, ...), custom_call_target="tpu_custom_call" | custom-call | flops 4026531840 | bytes 12582912 | tf_op jit(solution)/shard_map/attention_forward/pallas_call | solution.py:381
  79.1 2.0 collective-permute-done.11
  81.2 1.4 add_convert_fusion.3
  84.3 18.2 %collective-permute-done.12 = bf16[512,768]{1,0:T(8,128)(2,1)S(1)} collective-permute-done((bf16[512,768]{1,0:T(8,128)(2,1)S(1)}, bf16[512,768]{1,0:T(8,128)(2,1)S(1)}, u32[]{:S(2)}, u32[]{:S(2)}) %collective-permute-start.12) | collective-permute-done | bytes 786464 | tf_op jit(solution)/shard_map/ppermute | solution.py:517
  105.0 1.4 collective-permute-done.13.refs_1_
  106.8 11.3 %mlp.1 = (bf16[512,768]{1,0:T(8,128)(2,1)}, bf16[512,768]{1,0:T(8,128)(2,1)}, bf16[1024,640]{1,0:T(8,128)(2,1)}, bf16[1024,1280]{1,0:T(8,128)(2,1)}, bf16[384,576]{1,0:T(8,128)(2,1)}, /*index=5*/bf16[384,576]{1,0:T(8,128)(2,1)}) custom-call(s32[1]{0:T(128)} %bitcast.me_ref, bf16[512,768]{1,0:T(8,128)(2,1)} %copy-done.6, ...), custom_call_target="tpu_custom_call" | custom-call | flops 6039797760 | bytes 6291456 | tf_op jit(solution)/shard_map/mlp/pallas_call | solution.py:451
  118.0 2.5 collective-permute-done.16
  120.5 1.9 fusion.10
  122.5 1.9 fusion.15
  124.5 1.1 collective-permute-start.21
  127.5 6.0 %mlp_late.1 = (bf16[384,1152]{1,0:T(8,128)(2,1)}, bf16[384,1152]{1,0:T(8,128)(2,1)}) custom-call(s32[1]{0:T(128)} %bitcast.me_ref, bf16[512,768]{1,0:T(8,128)(2,1)} %copy-done.6, bf16[512,768]{1,0:T(8,128)(2,1)} %collective-permute-done.13.refs_1_, bf16[1024,1280]{1,0:T(8,128)(2,1)} %get-tuple-element.74.refs_2_), custom_call_target="tpu_custom_call" | custom-call | flops 2013265920 | bytes 4718592 | tf_op jit(solution)/shard_map/mlp_late/pallas_call | solution.py:480
  133.5 4.6 %down.1 = (bf16[512,768]{1,0:T(8,128)(2,1)}, bf16[512,768]{1,0:T(8,128)(2,1)}) custom-call(bf16[1024,640]{1,0:T(8,128)(2,1)} %get-tuple-element.77.hidden_ref, bf16[768,1920]{1,0:T(8,128)(2,1)} %all-gather.2.cloned.1.call-done.refs_4_.rest_ref), custom_call_target="tpu_custom_call" | custom-call | flops 1006632960 | bytes 4718592 | tf_op jit(solution)/shard_map/down/pallas_call | solution.py:501
  138.5 1.3 collective-permute-start.20
  140.3 1.3 add_convert_fusion.5
  141.6 3.6 %collective-permute-done.18.refs_2_ = bf16[512,768]{1,0:T(8,128)(2,1)} collective-permute-done((bf16[512,768]{1,0:T(8,128)(2,1)S(1)}, bf16[512,768]{1,0:T(8,128)(2,1)}, u32[]{:S(2)}, u32[]{:S(2)}) %collective-permute-start.18) | collective-permute-done | bytes 786464 | tf_op jit(solution)/shard_map/ppermute | solution.py:517
  145.3 2.4 add_convert_fusion.2
  147.7 13.0 %collective-permute-done.20 = bf16[384,1152]{1,0:T(8,128)(2,1)S(1)} collective-permute-done((bf16[384,1152]{1,0:T(8,128)(2,1)}, bf16[384,1152]{1,0:T(8,128)(2,1)S(1)}, u32[]{:S(2)}, u32[]{:S(2)}) %collective-permute-start.20) | collective-permute-done | bytes 884768 | tf_op jit(solution)/shard_map/ppermute | solution.py:517
  161.1 1.9 collective-permute-start.23
  163.0 1.9 collective-permute-start.24
  165.6 35.4 %attention_backward.1 = (bf16[512,768]{1,0:T(8,128)(2,1)}, bf16[512,768]{1,0:T(8,128)(2,1)}, bf16[512,768]{1,0:T(8,128)(2,1)}, bf16[512,768]{1,0:T(8,128)(2,1)},...) custom-call(s32[8]{0:T(128)} %get-tuple-element.185.low_ref, s32[8]{0:T(128)} %get-tuple-element.184.high_ref, ...), custom_call_target="tpu_custom_call" | custom-call | flops 38654705664 | bytes 18874368 | tf_op jit(solution)/shard_map/attention_backward/pallas_call | solution.py:417
  201.1 1.5 collective-permute-start.29
  203.6 2.3 add_convert_fusion.1
  205.8 1.4 collective-permute-start.28
  208.2 8.8 %collective-permute-done.29 = bf16[384,768]{1,0:T(8,128)(2,1)S(1)} collective-permute-done((bf16[384,768]{1,0:T(8,128)(2,1)}, bf16[384,768]{1,0:T(8,128)(2,1)S(1)}, u32[]{:S(2)}, u32[]{:S(2)}) %collective-permute-start.29) | collective-permute-done | bytes 589856 | tf_op jit(solution)/shard_map/ppermute | solution.py:517
  217.2 2.1 collective-permute-start.30
  219.4 1.7 collective-permute-start.31
  221.1 1.0 collective-permute-start.32
  223.0 2.2 collective-permute-done.30
  225.2 1.1 collective-permute-start.33
  226.3 7.1 %collective-permute-done.31 = bf16[96,768]{1,0:T(8,128)(2,1)S(1)} collective-permute-done((bf16[96,768]{1,0:T(8,128)(2,1)S(1)}, bf16[96,768]{1,0:T(8,128)(2,1)S(1)}, u32[]{:S(2)}, u32[]{:S(2)}) %collective-permute-start.31) | collective-permute-done | bytes 147488 | tf_op jit(solution)/shard_map/ppermute | solution.py:517
  235.4 1.4 maximum_add_fusion
  237.7 1.3 collective-permute-start.36
  242.7 1.7 fusion.8
  (158 shorter events, 28.5 us)
Async XLA Ops:
  7.2 99.6 %all-gather.2.cloned.1.call-start = ((), (), s32[]{:S(2)}) async-start(), calls=%async_computation | async-start | bytes 3317760 | tf_op jit(solution)/shard_map/all_gather | solution.py:612
  7.2 10.2 %collective-permute-start = (bf16[512,768]{1,0:T(8,128)(2,1)}, bf16[512,768]{1,0:T(8,128)(2,1)S(1)}, u32[]{:S(2)}, u32[]{:S(2)}) collective-permute-start(bf16[512,768]{1,0:T(8,128)(2,1)} %refs_0_.1), channel_id=1, source_target_pairs={{0,1},{1,0},{2,3},{3,2},{4,5},{5,4},{6,7},{7,6},{8,9},{9,8},{10,11... | collective-permute-start | bytes 2359304 | tf_op jit(solution)/shard_map/ppermute | solution.py:517
  7.7 20.9 %collective-permute-start.1 = (bf16[512,768]{1,0:T(8,128)(2,1)}, bf16[512,768]{1,0:T(8,128)(2,1)S(1)}, u32[]{:S(2)}, u32[]{:S(2)}) collective-permute-start(bf16[512,768]{1,0:T(8,128)(2,1)} %refs_0_.1), channel_id=1, source_target_pairs={{0,2},{1,3},{2,0},{3,1},{4,6},{5,7},{6,4},{7,5},{8,10},{9,11},{10,... | collective-permute-start | bytes 2359304 | tf_op jit(solution)/shard_map/ppermute | solution.py:517
  14.8 35.6 %copy-start.13 = (s32[2048]{0:T(1024)}, s32[2048]{0:T(1024)S(1)}, u32[]{:S(2)}) copy-start(s32[2048]{0:T(1024)S(1)} %convert_reduce_fusion.1) | copy-start | bytes 24580
  17.4 33.1 %copy-start.12 = (bf16[96,896]{1,0:T(8,128)(2,1)}, bf16[96,896]{1,0:T(8,128)(2,1)S(1)}, u32[]{:S(2)}) copy-start(bf16[96,896]{1,0:T(8,128)(2,1)S(1)} %maximum_maximum_fusion.refs_7_) | copy-start | bytes 516100
  17.4 33.0 %copy-start.15 = (bf16[512,768]{1,0:T(8,128)(2,1)}, bf16[512,768]{1,0:T(8,128)(2,1)S(1)}, u32[]{:S(2)}) copy-start(bf16[512,768]{1,0:T(8,128)(2,1)S(1)} %collective-permute-done.refs_1_) | copy-start | bytes 2359300
  17.4 15.1 %collective-permute-start.3 = (bf16[96,896]{1,0:T(8,128)(2,1)S(1)}, bf16[96,896]{1,0:T(8,128)(2,1)S(1)}, u32[]{:S(2)}, u32[]{:S(2)}) collective-permute-start(bf16[96,896]{1,0:T(8,128)(2,1)S(1)} %maximum_maximum_fusion.refs_7_), channel_id=1, source_target_pairs={{0,8},{4,12},{8,0},{12,4},{16,24},{20,28},{24,16},{28,20},{1,9},{5... | collective-permute-start | bytes 516104 | tf_op jit(solution)/shard_map/ppermute | solution.py:517
  19.0 15.5 %collective-permute-start.5 = (bf16[96,896]{1,0:T(8,128)(2,1)S(1)}, bf16[96,896]{1,0:T(8,128)(2,1)S(1)}, u32[]{:S(2)}, u32[]{:S(2)}) collective-permute-start(bf16[96,896]{1,0:T(8,128)(2,1)S(1)} %maximum_maximum_fusion.refs_7_), channel_id=1, source_target_pairs={{0,16},{4,20},{8,24},{12,28},{16,0},{20,4},{24,8},{28,12},{1,17},{... | collective-permute-start | bytes 516104 | tf_op jit(solution)/shard_map/ppermute | solution.py:517
  21.6 14.4 %collective-permute-start.7 = (bf16[96,896]{1,0:T(8,128)(2,1)S(1)}, bf16[96,896]{1,0:T(8,128)(2,1)S(1)}, u32[]{:S(2)}, u32[]{:S(2)}) collective-permute-start(bf16[96,896]{1,0:T(8,128)(2,1)S(1)} %maximum_maximum_fusion.refs_7_), channel_id=1, source_target_pairs={{0,24},{4,28},{8,16},{12,20},{16,8},{20,12},{24,0},{28,4},{1,25},{... | collective-permute-start | bytes 516104 | tf_op jit(solution)/shard_map/ppermute | solution.py:517
  28.7 21.8 %copy-start.16 = (bf16[512,768]{1,0:T(8,128)(2,1)}, bf16[512,768]{1,0:T(8,128)(2,1)S(1)}, u32[]{:S(2)}) copy-start(bf16[512,768]{1,0:T(8,128)(2,1)S(1)} %collective-permute-done.1.refs_2_) | copy-start | bytes 2359300
  28.7 7.9 %collective-permute-start.15 = (bf16[96,864]{1,0:T(8,128)(2,1)S(1)}, bf16[96,864]{1,0:T(8,128)(2,1)S(1)}, u32[]{:S(2)}, u32[]{:S(2)}) collective-permute-start(bf16[96,864]{1,0:T(8,128)(2,1)S(1)} %pad_maximum_fusion.5), channel_id=1, source_target_pairs={{0,2},{1,3},{2,0},{3,1},{4,6},{5,7},{6,4},{7,5},{8,10},{9,11},{10,... | collective-permute-start | bytes 497672 | tf_op jit(solution)/shard_map/ppermute | solution.py:517
  31.0 7.3 %collective-permute-start.2 = (bf16[96,896]{1,0:T(8,128)(2,1)S(1)}, bf16[96,896]{1,0:T(8,128)(2,1)S(1)}, u32[]{:S(2)}, u32[]{:S(2)}) collective-permute-start(bf16[96,896]{1,0:T(8,128)(2,1)S(1)} %maximum_maximum_fusion.refs_7_), channel_id=1, source_target_pairs={{0,4},{4,0},{8,12},{12,8},{16,20},{20,16},{24,28},{28,24},{1,5},{5... | collective-permute-start | bytes 516104 | tf_op jit(solution)/shard_map/ppermute | solution.py:517
  32.5 15.4 %copy-start.21 = (bf16[96,896]{1,0:T(8,128)(2,1)}, bf16[96,896]{1,0:T(8,128)(2,1)S(1)}, u32[]{:S(2)}) copy-start(bf16[96,896]{1,0:T(8,128)(2,1)S(1)} %collective-permute-done.3.refs_9_) | copy-start | bytes 516100
  32.5 9.6 %collective-permute-start.4 = (bf16[96,896]{1,0:T(8,128)(2,1)S(1)}, bf16[96,896]{1,0:T(8,128)(2,1)}, u32[]{:S(2)}, u32[]{:S(2)}) collective-permute-start(bf16[96,896]{1,0:T(8,128)(2,1)S(1)} %collective-permute-done.3.refs_9_), channel_id=1, source_target_pairs={{0,4},{4,0},{8,12},{12,8},{16,20},{20,16},{24,28},{28,24},{1,5},{5... | collective-permute-start | bytes 516104 | tf_op jit(solution)/shard_map/ppermute | solution.py:517
  34.6 13.3 %copy-start.22 = (bf16[96,896]{1,0:T(8,128)(2,1)}, bf16[96,896]{1,0:T(8,128)(2,1)S(1)}, u32[]{:S(2)}) copy-start(bf16[96,896]{1,0:T(8,128)(2,1)S(1)} %collective-permute-done.5.refs_11_) | copy-start | bytes 516100
  34.6 11.2 %collective-permute-start.6 = (bf16[96,896]{1,0:T(8,128)(2,1)S(1)}, bf16[96,896]{1,0:T(8,128)(2,1)}, u32[]{:S(2)}, u32[]{:S(2)}) collective-permute-start(bf16[96,896]{1,0:T(8,128)(2,1)S(1)} %collective-permute-done.5.refs_11_), channel_id=1, source_target_pairs={{0,4},{4,0},{8,12},{12,8},{16,20},{20,16},{24,28},{28,24},{1,5},{5... | collective-permute-start | bytes 516104 | tf_op jit(solution)/shard_map/ppermute | solution.py:517
  36.1 11.8 %copy-start.23 = (bf16[96,896]{1,0:T(8,128)(2,1)}, bf16[96,896]{1,0:T(8,128)(2,1)S(1)}, u32[]{:S(2)}) copy-start(bf16[96,896]{1,0:T(8,128)(2,1)S(1)} %collective-permute-done.7.refs_13_) | copy-start | bytes 516100
  36.1 11.8 %collective-permute-start.8 = (bf16[96,896]{1,0:T(8,128)(2,1)S(1)}, bf16[96,896]{1,0:T(8,128)(2,1)}, u32[]{:S(2)}, u32[]{:S(2)}) collective-permute-start(bf16[96,896]{1,0:T(8,128)(2,1)S(1)} %collective-permute-done.7.refs_13_), channel_id=1, source_target_pairs={{0,4},{4,0},{8,12},{12,8},{16,20},{20,16},{24,28},{28,24},{1,5},{5... | collective-permute-start | bytes 516104 | tf_op jit(solution)/shard_map/ppermute | solution.py:517
  47.9 2.5 collective-permute-start.9
  78.5 2.7 %collective-permute-start.11 = (bf16[512,768]{1,0:T(8,128)(2,1)}, bf16[512,768]{1,0:T(8,128)(2,1)S(1)}, u32[]{:S(2)}, u32[]{:S(2)}) collective-permute-start(bf16[512,768]{1,0:T(8,128)(2,1)} %get-tuple-element.67), channel_id=1, source_target_pairs={{0,1},{1,0},{2,3},{3,2},{4,5},{5,4},{6,7},{7,6},{8,9},{9,8},{10,11... | collective-permute-start | bytes 2359304 | tf_op jit(solution)/shard_map/ppermute | solution.py:517
  79.1 5.3 %collective-permute-start.10 = (bf16[512,768]{1,0:T(8,128)(2,1)}, bf16[512,768]{1,0:T(8,128)(2,1)S(1)}, u32[]{:S(2)}, u32[]{:S(2)}) collective-permute-start(bf16[512,768]{1,0:T(8,128)(2,1)} %get-tuple-element.65), channel_id=1, source_target_pairs={{0,1},{1,0},{2,3},{3,2},{4,5},{5,4},{6,7},{7,6},{8,9},{9,8},{10,11... | collective-permute-start | bytes 2359304 | tf_op jit(solution)/shard_map/ppermute | solution.py:517
  81.2 21.3 %copy-start.5 = (bf16[512,768]{1,0:T(8,128)(2,1)S(1)}, bf16[512,768]{1,0:T(8,128)(2,1)}, u32[]{:S(2)}) copy-start(bf16[512,768]{1,0:T(8,128)(2,1)} %get-tuple-element.64) | copy-start | bytes 2359300
  82.6 19.9 %collective-permute-start.12 = (bf16[512,768]{1,0:T(8,128)(2,1)S(1)}, bf16[512,768]{1,0:T(8,128)(2,1)S(1)}, u32[]{:S(2)}, u32[]{:S(2)}) collective-permute-start(bf16[512,768]{1,0:T(8,128)(2,1)S(1)} %add_convert_fusion.3), channel_id=1, source_target_pairs={{0,2},{1,3},{2,0},{3,1},{4,6},{5,7},{6,4},{7,5},{8,10},{9,11},{10,... | collective-permute-start | bytes 2359304 | tf_op jit(solution)/shard_map/ppermute | solution.py:517
  83.2 20.8 %collective-permute-start.14 = (bf16[512,768]{1,0:T(8,128)(2,1)S(1)}, bf16[512,768]{1,0:T(8,128)(2,1)S(1)}, u32[]{:S(2)}, u32[]{:S(2)}) collective-permute-start(bf16[512,768]{1,0:T(8,128)(2,1)S(1)} %copy-done.7), channel_id=1, source_target_pairs={{0,1},{1,0},{2,3},{3,2},{4,5},{5,4},{6,7},{7,6},{8,9},{9,8},{10,11... | collective-permute-start | bytes 2359304 | tf_op jit(solution)/shard_map/ppermute | solution.py:517
  103.9 2.5 collective-permute-start.13
  118.0 2.5 collective-permute-start.16
  124.3 2.3 collective-permute-start.17
  124.5 15.8 %collective-permute-start.21 = (bf16[384,576]{1,0:T(8,128)(2,1)}, bf16[384,576]{1,0:T(8,128)(2,1)}, u32[]{:S(2)}, u32[]{:S(2)}) collective-permute-start(bf16[384,576]{1,0:T(8,128)(2,1)} %get-tuple-element.82), channel_id=1, source_target_pairs={{0,4},{4,0},{8,12},{12,8},{16,20},{20,16},{24,28},{28,24},{1,5},{5... | collective-permute-start | bytes 1327112 | tf_op jit(solution)/shard_map/ppermute | solution.py:517
  125.6 19.6 %collective-permute-start.18 = (bf16[512,768]{1,0:T(8,128)(2,1)S(1)}, bf16[512,768]{1,0:T(8,128)(2,1)}, u32[]{:S(2)}, u32[]{:S(2)}) collective-permute-start(bf16[512,768]{1,0:T(8,128)(2,1)S(1)} %get-tuple-element.85.refs_0_), channel_id=1, source_target_pairs={{0,2},{1,3},{2,0},{3,1},{4,6},{5,7},{6,4},{7,5},{8,10},{9,11},{10,... | collective-permute-start | bytes 2359304 | tf_op jit(solution)/shard_map/ppermute | solution.py:517
  138.1 7.1 %collective-permute-start.22 = (bf16[512,768]{1,0:T(8,128)(2,1)}, bf16[512,768]{1,0:T(8,128)(2,1)}, u32[]{:S(2)}, u32[]{:S(2)}) collective-permute-start(bf16[512,768]{1,0:T(8,128)(2,1)} %get-tuple-element.78), channel_id=1, source_target_pairs={{0,1},{1,0},{2,3},{3,2},{4,5},{5,4},{6,7},{7,6},{8,9},{9,8},{10,11... | collective-permute-start | bytes 2359304 | tf_op jit(solution)/shard_map/ppermute | solution.py:517
  138.5 22.2 %collective-permute-start.20 = (bf16[384,1152]{1,0:T(8,128)(2,1)}, bf16[384,1152]{1,0:T(8,128)(2,1)S(1)}, u32[]{:S(2)}, u32[]{:S(2)}) collective-permute-start(bf16[384,1152]{1,0:T(8,128)(2,1)} %get-tuple-element.80), channel_id=1, source_target_pairs={{0,4},{4,0},{8,12},{12,8},{16,20},{20,16},{24,28},{28,24},{1,5},{5... | collective-permute-start | bytes 2654216 | tf_op jit(solution)/shard_map/ppermute | solution.py:517
  145.2 15.9 %collective-permute-start.19 = (bf16[512,768]{1,0:T(8,128)(2,1)}, bf16[512,768]{1,0:T(8,128)(2,1)S(1)}, u32[]{:S(2)}, u32[]{:S(2)}) collective-permute-start(bf16[512,768]{1,0:T(8,128)(2,1)} %collective-permute-done.18.refs_2_), channel_id=1, source_target_pairs={{0,1},{1,0},{2,3},{3,2},{4,5},{5,4},{6,7},{7,6},{8,9},{9,8},{10,11... | collective-permute-start | bytes 2359304 | tf_op jit(solution)/shard_map/ppermute | solution.py:517
  145.2 15.4 %copy-start.4 = (bf16[384,1152]{1,0:T(8,128)(2,1)S(1)}, bf16[384,1152]{1,0:T(8,128)(2,1)}, u32[]{:S(2)}) copy-start(bf16[384,1152]{1,0:T(8,128)(2,1)} %get-tuple-element.79) | copy-start | bytes 2654212
  161.1 39.9 %collective-permute-start.23 = (bf16[96,1728]{1,0:T(8,128)(2,1)S(1)}, bf16[96,1728]{1,0:T(8,128)(2,1)S(1)}, u32[]{:S(2)}, u32[]{:S(2)}) collective-permute-start(bf16[96,1728]{1,0:T(8,128)(2,1)S(1)} %pad_maximum_fusion.1), channel_id=1, source_target_pairs={{0,8},{4,12},{8,0},{12,4},{16,24},{20,28},{24,16},{28,20},{1,9},{5... | collective-permute-start | bytes 995336 | tf_op jit(solution)/shard_map/ppermute | solution.py:517
  163.0 38.0 %collective-permute-start.24 = (bf16[96,1728]{1,0:T(8,128)(2,1)S(1)}, bf16[96,1728]{1,0:T(8,128)(2,1)S(1)}, u32[]{:S(2)}, u32[]{:S(2)}) collective-permute-start(bf16[96,1728]{1,0:T(8,128)(2,1)S(1)} %pad_maximum_fusion.2), channel_id=1, source_target_pairs={{0,16},{4,20},{8,24},{12,28},{16,0},{20,4},{24,8},{28,12},{1,17},{... | collective-permute-start | bytes 995336 | tf_op jit(solution)/shard_map/ppermute | solution.py:517
  165.0 36.0 %collective-permute-start.25 = (bf16[96,1728]{1,0:T(8,128)(2,1)S(1)}, bf16[96,1728]{1,0:T(8,128)(2,1)S(1)}, u32[]{:S(2)}, u32[]{:S(2)}) collective-permute-start(bf16[96,1728]{1,0:T(8,128)(2,1)S(1)} %pad_maximum_fusion.3), channel_id=1, source_target_pairs={{0,24},{4,28},{8,16},{12,20},{16,8},{20,12},{24,0},{28,4},{1,25},{... | collective-permute-start | bytes 995336 | tf_op jit(solution)/shard_map/ppermute | solution.py:517
  201.0 2.6 %collective-permute-start.27 = (bf16[512,768]{1,0:T(8,128)(2,1)}, bf16[512,768]{1,0:T(8,128)(2,1)S(1)}, u32[]{:S(2)}, u32[]{:S(2)}) collective-permute-start(bf16[512,768]{1,0:T(8,128)(2,1)} %get-tuple-element.108), channel_id=1, source_target_pairs={{0,1},{1,0},{2,3},{3,2},{4,5},{5,4},{6,7},{7,6},{8,9},{9,8},{10,11... | collective-permute-start | bytes 2359304 | tf_op jit(solution)/shard_map/ppermute | solution.py:517
  201.1 16.0 %collective-permute-start.29 = (bf16[384,768]{1,0:T(8,128)(2,1)}, bf16[384,768]{1,0:T(8,128)(2,1)S(1)}, u32[]{:S(2)}, u32[]{:S(2)}) collective-permute-start(bf16[384,768]{1,0:T(8,128)(2,1)} %get-tuple-element.111), channel_id=1, source_target_pairs={{0,4},{4,0},{8,12},{12,8},{16,20},{20,16},{24,28},{28,24},{1,5},{5... | collective-permute-start | bytes 1769480 | tf_op jit(solution)/shard_map/ppermute | solution.py:517
  202.6 38.7 %collective-permute-start.26 = (bf16[512,768]{1,0:T(8,128)(2,1)}, bf16[512,768]{1,0:T(8,128)(2,1)S(1)}, u32[]{:S(2)}, u32[]{:S(2)}) collective-permute-start(bf16[512,768]{1,0:T(8,128)(2,1)} %get-tuple-element.106), channel_id=1, source_target_pairs={{0,1},{1,0},{2,3},{3,2},{4,5},{5,4},{6,7},{7,6},{8,9},{9,8},{10,11... | collective-permute-start | bytes 2359304 | tf_op jit(solution)/shard_map/ppermute | solution.py:517
  205.8 11.2 %copy-start.11 = (bf16[384,768]{1,0:T(8,128)(2,1)S(1)}, bf16[384,768]{1,0:T(8,128)(2,1)}, u32[]{:S(2)}) copy-start(bf16[384,768]{1,0:T(8,128)(2,1)} %get-tuple-element.110) | copy-start | bytes 1769476
  205.8 35.5 %collective-permute-start.28 = (bf16[512,768]{1,0:T(8,128)(2,1)}, bf16[512,768]{1,0:T(8,128)(2,1)S(1)}, u32[]{:S(2)}, u32[]{:S(2)}) collective-permute-start(bf16[512,768]{1,0:T(8,128)(2,1)} %add_convert_fusion.1), channel_id=1, source_target_pairs={{0,2},{1,3},{2,0},{3,1},{4,6},{5,7},{6,4},{7,5},{8,10},{9,11},{10,... | collective-permute-start | bytes 2359304 | tf_op jit(solution)/shard_map/ppermute | solution.py:517
  217.2 7.9 %collective-permute-start.30 = (bf16[96,768]{1,0:T(8,128)(2,1)S(1)}, bf16[96,768]{1,0:T(8,128)(2,1)S(1)}, u32[]{:S(2)}, u32[]{:S(2)}) collective-permute-start(bf16[96,768]{1,0:T(8,128)(2,1)S(1)} %get-tuple-element.160), channel_id=1, source_target_pairs={{0,8},{4,12},{8,0},{12,4},{16,24},{20,28},{24,16},{28,20},{1,9},{5... | collective-permute-start | bytes 442376 | tf_op jit(solution)/shard_map/ppermute | solution.py:517
  219.4 14.0 %collective-permute-start.31 = (bf16[96,768]{1,0:T(8,128)(2,1)S(1)}, bf16[96,768]{1,0:T(8,128)(2,1)S(1)}, u32[]{:S(2)}, u32[]{:S(2)}) collective-permute-start(bf16[96,768]{1,0:T(8,128)(2,1)S(1)} %get-tuple-element.162), channel_id=1, source_target_pairs={{0,16},{4,20},{8,24},{12,28},{16,0},{20,4},{24,8},{28,12},{1,17},{... | collective-permute-start | bytes 442376 | tf_op jit(solution)/shard_map/ppermute | solution.py:517
  221.1 12.3 %collective-permute-start.32 = (bf16[96,768]{1,0:T(8,128)(2,1)S(1)}, bf16[96,768]{1,0:T(8,128)(2,1)S(1)}, u32[]{:S(2)}, u32[]{:S(2)}) collective-permute-start(bf16[96,768]{1,0:T(8,128)(2,1)S(1)} %get-tuple-element.161), channel_id=1, source_target_pairs={{0,24},{4,28},{8,16},{12,20},{16,8},{20,12},{24,0},{28,4},{1,25},{... | collective-permute-start | bytes 442376 | tf_op jit(solution)/shard_map/ppermute | solution.py:517
  225.2 10.2 %collective-permute-start.33 = (bf16[96,864]{1,0:T(8,128)(2,1)}, bf16[96,864]{1,0:T(8,128)(2,1)}, u32[]{:S(2)}, u32[]{:S(2)}) collective-permute-start(bf16[96,864]{1,0:T(8,128)(2,1)} %pad_maximum_fusion.6), channel_id=1, source_target_pairs={{0,2},{1,3},{2,0},{3,1},{4,6},{5,7},{6,4},{7,5},{8,10},{9,11},{10,... | collective-permute-start | bytes 497672 | tf_op jit(solution)/shard_map/ppermute | solution.py:517
  237.0 3.6 %collective-permute-start.34 = (f32[2,96]{1,0:T(2,128)S(1)}, f32[2,96]{1,0:T(2,128)S(1)}, u32[]{:S(2)}, u32[]{:S(2)}) collective-permute-start(f32[2,96]{1,0:T(2,128)S(1)} %maximum_divide_fusion), channel_id=1, source_target_pairs={{0,1},{1,0},{2,3},{3,2},{4,5},{5,4},{6,7},{7,6},{8,9},{9,8},{10,11... | collective-permute-start | bytes 2312 | tf_op jit(solution)/shard_map/ppermute | solution.py:517
  237.1 3.6 %collective-permute-start.35 = (f32[2,96]{1,0:T(2,128)S(1)}, f32[2,96]{1,0:T(2,128)S(1)}, u32[]{:S(2)}, u32[]{:S(2)}) collective-permute-start(f32[2,96]{1,0:T(2,128)S(1)} %maximum_divide_fusion), channel_id=1, source_target_pairs={{0,2},{1,3},{2,0},{3,1},{4,6},{5,7},{6,4},{7,5},{8,10},{9,11},{10,... | collective-permute-start | bytes 2312 | tf_op jit(solution)/shard_map/ppermute | solution.py:517
  237.7 3.0 %collective-permute-start.36 = (f32[2,96]{1,0:T(2,128)S(1)}, f32[2,96]{1,0:T(2,128)S(1)}, u32[]{:S(2)}, u32[]{:S(2)}) collective-permute-start(f32[2,96]{1,0:T(2,128)S(1)} %maximum_divide_fusion), channel_id=1, source_target_pairs={{0,3},{1,2},{2,1},{3,0},{4,7},{5,6},{6,5},{7,4},{8,11},{9,10},{10,... | collective-permute-start | bytes 2312 | tf_op jit(solution)/shard_map/ppermute | solution.py:517
  (15 other events, 59.9 us)
Sparse Core Ops, SparseCore 0:
  48.0 58.7 all-gather.1
